TPU v7x, 32 devices: a whole 2x2x4 slice. The times are simulated.
32 devices in a mesh: gy: 4 (over z), gx: 8 (over y, x, core).
Axes of the slice: x: 2, y: 2, z: 4, core: 2. Of those that a mesh axis runs over, the one named last changes fastest.
Arguments:
- observed: float32 [16, 128, 1024], P(None, 'gy', 'gx'), may hold values from 0 to 20, as said below
- profiles: float32 [64, 3, 9], replicated, may hold values from 0.03 to 0.25
- tile_index: int32 [4, 8], replicated, may hold values from 0 to 63
Outputs:
- estimate: float32 [16, 128, 1024], P(None, 'gy', 'gx')
Inputs may be any that keep to these rules, and one draw needn't show every extreme that they name: `observed`: nonnegative intensities.
All inputs are finite; a program needn't handle non-finite values.
Results may differ from a plain program's by a relative error of at most 0.0003.
Values sent between devices are 32-bit elements; how exact they have to be, the bound alone decides.
No kernel may reach another device: no remote copies, remote signals or barrier semaphores. Data moves between devices by JAX's collectives and lax.ppermute only.
A program may use at most 64 MiB of HBM per device.

v0:
```python
import functools
import jax
import jax.numpy as jnp
from jax import lax
from jax.experimental import pallas as pl
from jax.experimental.pallas import tpu as pltpu
from jax.sharding import PartitionSpec as P

ITERS = 2
WEIGHT_TV = 0.02
SMOOTHING = 0.1
DAMPING = 0.05
START_STEP = 0.5
SUB = 8
F32 = jnp.float32
BF16 = jnp.bfloat16
VMEM_BYTES = 44 * 1024 * 1024


def plan(layers, height, breadth, taps):
    radius = (taps - 1) // 2
    halo = 6 * radius
    off = -(-halo // SUB) * SUB + SUB
    slot = 1
    while slot < halo:
        slot *= 2
    return dict(
        layers=layers, height=height, breadth=breadth, taps=taps, radius=radius, halo=halo, off=off,
        rows=height + 2 * off, slot=slot, per_pack=breadth // slot, first=off // SUB, last=(off + height) // SUB,
        tiles=(height + 2 * off) // SUB,
    )


def reach(s, extent):
    low = (s["off"] - extent) // SUB
    high = -(-(s["off"] + s["height"] + extent) // SUB)
    return low, high


def bands(s):
    return ((0, s["first"]), (s["first"], s["last"]), (s["last"], s["tiles"]))


def place():
    return lax.axis_index("gy"), lax.axis_index("gx"), lax.axis_size("gy"), lax.axis_size("gx")


def weights_kernel(s, index_ref, profiles_ref, taps_ref, high_ref, low_ref):
    gy, gx, ny, nx = place()
    breadth, taps, radius = s["breadth"], s["taps"], s["radius"]
    ring = 2 * breadth
    lane = lax.broadcasted_iota(jnp.int32, (SUB, breadth), 1)
    chunk = 32
    for band in range(3):
        row = gy + (band - 1)
        picked = []
        for side in range(3):
            col = gx + (side - 1)
            inside = (row >= 0) & (row < ny) & (col >= 0) & (col < nx)
            number = index_ref[jnp.clip(row, 0, ny - 1), jnp.clip(col, 0, nx - 1)]
            picked.append((inside, number))
        columns = []
        for dim in range(3):
            for tap in range(taps):
                left, centre, right = [
                    jnp.where(inside, profiles_ref[tap, dim, number], 0.0) for inside, number in picked
                ]
                main = jnp.full((SUB, breadth), centre, F32)
                side = jnp.where(lane < breadth // 2, right, left)
                if dim < 2:
                    taps_ref[band, dim, 0, tap] = main
                    taps_ref[band, dim, 1, tap] = side
                else:
                    columns.append(jnp.concatenate([main, side], axis=1)[:1])

        def build(piece, carry, band=band, columns=columns):
            start = pl.multiple_of(piece * chunk, chunk)
            source = lax.broadcasted_iota(jnp.int32, (chunk, ring), 0) + start
            target = lax.broadcasted_iota(jnp.int32, (chunk, ring), 1)
            distance = target - source + radius
            distance = jnp.where(distance < 0, distance + ring, distance)
            distance = jnp.where(distance >= ring, distance - ring, distance)
            total = jnp.zeros((chunk, ring), F32)
            for tap in range(taps):
                total = jnp.where(distance == tap, columns[tap], total)
            upper = total.astype(BF16)
            high_ref[band, pl.ds(start, chunk), :] = upper
            low_ref[band, pl.ds(start, chunk), :] = (total - upper.astype(F32)).astype(BF16)
            return carry

        lax.fori_loop(0, ring // chunk, build, 0)


def pack_kernel(s, tile_ref, even_ref, odd_ref, first_ref, second_ref):
    gy, gx, _, _ = place()
    halo, height, slot, per = s["halo"], s["height"], s["slot"], s["per_pack"]
    breadth = s["breadth"]
    row_even, col_even = lax.rem(gy, 2) == 0, lax.rem(gx, 2) == 0
    lane = lax.broadcasted_iota(jnp.int32, (1, breadth), 1)
    pieces = ((0, None, halo), (halo, tile_ref, height), (halo + height, None, halo))
    for start, ref, count in pieces:
        for group in range(s["layers"] // per):
            first = jnp.zeros((count, breadth), F32)
            second = jnp.zeros((count, breadth), F32)
            for member in range(per):
                layer = group * per + member
                if ref is not None:
                    value = ref[layer]
                elif start == 0:
                    value = jnp.where(row_even, odd_ref[layer], even_ref[layer])
                else:
                    value = jnp.where(row_even, even_ref[layer], odd_ref[layer])
                mine = (lane >= member * slot) & (lane < (member + 1) * slot)
                to_left = member * slot
                to_right = (member * slot + slot) % breadth
                first = jnp.where(mine, pltpu.roll(value, jnp.where(col_even, to_right, to_left), 1), first)
                second = jnp.where(mine, pltpu.roll(value, jnp.where(col_even, to_left, to_right), 1), second)
            first_ref[group, start:start + count, :] = first
            second_ref[group, start:start + count, :] = second


def dot_split(value, high, low, contract):
    dims = (((1,), (contract,)), ((), ()))
    upper = value.astype(BF16)
    lower = (value - upper.astype(F32)).astype(BF16)
    mul = functools.partial(lax.dot_general, dimension_numbers=dims, preferred_element_type=F32)
    return mul(upper, high) + (mul(upper, low) + mul(lower, high))


def rows_of(ref, low, high):
    count = (high - low) * SUB
    pair = [ref[half, :, low * SUB:high * SUB, :] for half in range(2)]
    layers, breadth = pair[0].shape[0], pair[0].shape[2]
    return jnp.concatenate([p.reshape(layers * count, breadth) for p in pair], axis=1)


def column_pass(s, source, target, low, high, m_high, m_low, contract, add):
    if low >= high:
        return
    layers, breadth, count = s["layers"], s["breadth"], (high - low) * SUB
    result = dot_split(rows_of(source, low, high), m_high, m_low, contract)
    for half in range(2):
        piece = result[:, half * breadth:(half + 1) * breadth].reshape(layers, count, breadth)
        if add:
            piece = piece + target[half, :, low * SUB:high * SUB, :]
        target[half, :, low * SUB:high * SUB, :] = piece


def row_depth(s, source, half, tile, row_taps, depth_taps, transposed):
    layers, taps, radius = s["layers"], s["taps"], s["radius"]
    start = tile * SUB
    mixed = []
    for layer in range(layers):
        total = None
        for tap in range(taps):
            shift = tap - radius if transposed else radius - tap
            term = row_taps[tap] * source[half, layer, pl.ds(start + shift, SUB), :]
            total = term if total is None else total + term
        mixed.append(total)
    outs = []
    for layer in range(layers):
        total = None
        for tap in range(taps):
            shift = tap - radius if transposed else radius - tap
            if 0 <= layer + shift < layers:
                term = depth_taps[tap] * mixed[layer + shift]
                total = term if total is None else total + term
        outs.append(total)
    return outs


def row_depth_pass(s, taps_ref, band, source, low, high, transposed, emit):
    def body(tile, carry):
        for half in range(2):
            row_taps = [taps_ref[band, 1, half, t] for t in range(s["taps"])]
            depth_taps = [taps_ref[band, 0, half, t] for t in range(s["taps"])]
            emit(half, tile, row_depth(s, source, half, tile, row_taps, depth_taps, transposed))
        return carry

    if low < high:
        lax.fori_loop(low, high, body, 0)


def slope_pass(s, source, shift, low, high, divergence, flux_rows, where):
    gy, gx, ny, nx = where
    layers, height, breadth = s["layers"], s["height"], s["breadth"]
    ring = 2 * breadth
    lane = lax.broadcasted_iota(jnp.int32, (SUB, ring), 1)
    col = gx * breadth + jnp.where(lane < breadth + breadth // 2, lane, lane - ring)
    col_mask = jnp.where((col >= 0) & (col < nx * breadth - 1), 1.0, 0.0).astype(F32)

    def body(tile, carry):
        start = tile * SUB
        row = gy * height + start - s["off"] + shift + lax.broadcasted_iota(jnp.int32, (SUB, ring), 0)
        row_mask = jnp.where((row >= 0) & (row < ny * height - 1), 1.0, 0.0).astype(F32)

        def load(layer, begin):
            return jnp.concatenate([source[half, layer, pl.ds(begin, SUB), :] for half in range(2)], axis=1)

        here = load(0, start)
        flux_before = None
        for layer in range(layers):
            below = load(layer, start + 1)
            step_rows = (below - here) * row_mask
            step_cols = (pltpu.roll(here, ring - 1, 1) - here) * col_mask
            square = step_rows * step_rows + step_cols * step_cols + SMOOTHING * SMOOTHING
            if layer + 1 < layers:
                after = load(layer + 1, start)
                step_depth = after - here
                square = square + step_depth * step_depth
            inverse = lax.rsqrt(square)
            f_rows, f_cols = step_rows * inverse, step_cols * inverse
            total = pltpu.roll(f_cols, 1, 1) - f_cols - f_rows
            if flux_before is not None:
                total = total + flux_before
            if layer + 1 < layers:
                flux_before = step_depth * inverse
                total = total - flux_before
                here = after
            for half in range(2):
                part = slice(half * breadth, (half + 1) * breadth)
                divergence[half, layer, pl.ds(start, SUB), :] = total[:, part]
                flux_rows[half, layer, pl.ds(start, SUB), :] = f_rows[:, part]
        return carry

    lax.fori_loop(low - 1, high, body, 0)


def main_kernel(s, tile_ref, even_ref, odd_ref, first_ref, second_ref, taps_ref, high_ref, low_ref,
                x1_ref, g1_ref, pull_ref, again_ref, part_ref,
                x0, x1, g0, y0, y1, y2, r0, r1, r2, q0, q1, q2, acc, div, flux):
    where = place()
    gy, gx, ny, nx = where
    layers, height, breadth, off = s["layers"], s["height"], s["breadth"], s["off"]
    halo, slot, per, radius = s["halo"], s["slot"], s["per_pack"], s["radius"]
    first_tile, last_tile = s["first"], s["last"]
    row_even, col_even = lax.rem(gy, 2) == 0, lax.rem(gx, 2) == 0
    lane = lax.broadcasted_iota(jnp.int32, (1, breadth), 1)
    ys, rs, qs = (y0, y1, y2), (r0, r1, r2), (q0, q1, q2)
    span = bands(s)

    top = off - halo
    x0[:, :, :top, :] = jnp.zeros((2, layers, top, breadth), F32)
    x0[:, :, off + height + halo:, :] = jnp.zeros((2, layers, top, breadth), F32)
    x0[0, :, top:off, :] = jnp.where(row_even, odd_ref[...], even_ref[...])
    x0[0, :, off:off + height, :] = tile_ref[...]
    x0[0, :, off + height:off + height + halo, :] = jnp.where(row_even, even_ref[...], odd_ref[...])

    def unpack(group, carry):
        first, second = first_ref[group], second_ref[group]
        right = jnp.where(col_even, first, second)
        left = jnp.where(col_even, second, first)
        for member in range(per):
            value = jnp.where(lane < slot, pltpu.roll(right, (breadth - member * slot) % breadth, 1), 0.0)
            value = jnp.where(lane >= breadth - slot, pltpu.roll(left, (breadth - slot - member * slot) % breadth, 1), value)
            x0[1, group * per + member, top:top + 2 * halo + height, :] = value
        return carry

    lax.fori_loop(0, layers // per, unpack, 0)

    zero = jnp.zeros((2, layers, SUB, breadth), F32)
    y0[:, :, :SUB, :] = zero
    y2[:, :, (s["tiles"] - 1) * SUB:, :] = zero
    for tile in (first_tile, first_tile + 1):
        r0[:, :, tile * SUB:(tile + 1) * SUB, :] = zero
    for tile in (first_tile - 2, first_tile - 1, last_tile, last_tile + 1):
        r1[:, :, tile * SUB:(tile + 1) * SUB, :] = zero
    for tile in (last_tile - 2, last_tile - 1):
        r2[:, :, tile * SUB:(tile + 1) * SUB, :] = zero

    def forward(source, extent, emit):
        low, high = reach(s, extent)
        in_low, in_high = reach(s, extent + radius)
        for band in range(3):
            out_low, out_high = max(low, span[band][0]), min(high, span[band][1])
            column_pass(s, source, ys[band], max(out_low - 1, in_low), min(out_high + 1, in_high),
                        high_ref[band], low_ref[band], 0, False)
            row_depth_pass(s, taps_ref, band, ys[band], out_low, out_high, False,
                           functools.partial(emit, band))

    def backward(extent):
        low, high = reach(s, extent)
        for band in range(3):
            out_low, out_high = max(low, span[band][0] - 1), min(high, span[band][1] + 1)

            def emit(half, tile, outs, band=band):
                for layer in range(layers):
                    qs[band][half, layer, pl.ds(pl.multiple_of(tile * SUB, SUB), SUB), :] = outs[layer]

            row_depth_pass(s, taps_ref, band, rs[band], out_low, out_high, True, emit)
        middle = span[1]
        column_pass(s, q1, acc, max(low, middle[0] - 1), min(high, middle[1] + 1), high_ref[1], low_ref[1], 1, False)
        if low < middle[0] - 1:
            acc[:, :, low * SUB:(middle[0] - 1) * SUB, :] = jnp.zeros((2, layers, (middle[0] - 1 - low) * SUB, breadth), F32)
            acc[:, :, (middle[1] + 1) * SUB:high * SUB, :] = jnp.zeros((2, layers, (high - middle[1] - 1) * SUB, breadth), F32)
        for band in (0, 2):
            out_low, out_high = max(low, span[band][0] - 1), min(high, span[band][1] + 1)
            column_pass(s, qs[band], acc, out_low, out_high, high_ref[band], low_ref[band], 1, True)

    def residual(band, half, tile, outs):
        at = pl.ds(pl.multiple_of(tile * SUB, SUB), SUB)
        for layer in range(layers):
            rs[band][half, layer, at, :] = outs[layer] - x0[half, layer, at, :]

    def plain(band, half, tile, outs):
        at = pl.ds(pl.multiple_of(tile * SUB, SUB), SUB)
        for layer in range(layers):
            rs[band][half, layer, at, :] = outs[layer]

    def inside(tile, half):
        row = gy * height + tile * SUB - off + lax.broadcasted_iota(jnp.int32, (SUB, breadth), 0)
        here = lax.broadcasted_iota(jnp.int32, (SUB, breadth), 1)
        if half == 1:
            here = jnp.where(here < breadth // 2, here + breadth, here - breadth)
        col = gx * breadth + here
        return (row >= 0) & (row < ny * height) & (col >= 0) & (col < nx * breadth)

    def slope(source, half, tile):
        at = pl.ds(pl.multiple_of(tile * SUB, SUB), SUB)
        before = pl.ds(tile * SUB - 1, SUB)
        keep = inside(tile, half)
        values = []
        for layer in range(layers):
            total = acc[half, layer, at, :] + WEIGHT_TV * (div[half, layer, at, :] + flux[half, layer, before, :])
            total = total + DAMPING * source[half, layer, at, :]
            values.append(jnp.where(keep, total, 0.0))
        return at, values

    slope_pass(s, x0, 0, *reach(s, 4 * radius), div, flux, where)
    forward(x0, 5 * radius, residual)
    backward(4 * radius)

    def first_step(tile, carry):
        for half in range(2):
            at, values = slope(x0, half, tile)
            for layer in range(layers):
                g0[half, layer, at, :] = values[layer]
                x1[half, layer, at, :] = x0[half, layer, at, :] - START_STEP * values[layer]
        return carry

    lax.fori_loop(*reach(s, 4 * radius), first_step, 0)

    slope_pass(s, x1, 0, *reach(s, 2 * radius), div, flux, where)
    forward(x1, 3 * radius, residual)
    backward(2 * radius)
    low, high = reach(s, 2 * radius)

    def second_step(tile, carry):
        for half in range(2):
            at, values = slope(x1, half, tile)
            local = pl.ds(pl.multiple_of((tile - low) * SUB, SUB), SUB)
            for layer in range(layers):
                g1_ref[half, layer, local, :] = values[layer]
                x1_ref[half, layer, local, :] = x1[half, layer, at, :]
                x1[half, layer, at, :] = values[layer]
        return carry

    lax.fori_loop(low, high, second_step, 0)
    centre = slice(first_tile * SUB, last_tile * SUB)
    pull_ref[...] = acc[0, :, centre, :]

    forward(x1, radius, plain)
    backward(0)
    again_ref[...] = acc[0, :, centre, :]

    def sums(tile, carry):
        at = pl.ds(pl.multiple_of(tile * SUB, SUB), SUB)
        zero_sq, cross, one_sq = carry
        for layer in range(layers):
            a, b = g0[0, layer, at, :], x1[0, layer, at, :]
            zero_sq, cross, one_sq = zero_sq + a * a, cross + a * (b - a), one_sq + b * b
        return zero_sq, cross, one_sq

    start = jnp.zeros((SUB, breadth), F32)
    totals = lax.fori_loop(first_tile, last_tile, sums, (start, start, start))
    zero_sq, cross, one_sq = [jnp.sum(t, axis=(0, 1), keepdims=True) for t in totals]
    row = jnp.where(lane == 0, zero_sq, jnp.where(lane == 1, cross, one_sq))
    part_ref[...] = jnp.broadcast_to(row, part_ref.shape)


def step_kernel(s, sums_ref, x1_ref, g1_ref, pull_ref, again_ref, x2_ref, g2_ref, part_ref, keep_ref, x2, div, flux):
    where = place()
    layers, height, breadth = s["layers"], s["height"], s["breadth"]
    low, high = reach(s, 2 * s["radius"])
    lane = lax.broadcasted_iota(jnp.int32, (1, breadth), 1)
    total = jnp.sum(sums_ref[...], axis=0, keepdims=True)
    zero_sq, cross, one_sq = [
        jnp.sum(jnp.where(lane == number, total, 0.0), axis=(0, 1), keepdims=True) for number in range(3)
    ]
    step = (START_STEP * START_STEP * zero_sq) / (-START_STEP * cross)
    count = (high - low) * SUB
    for half in range(2):
        for layer in range(layers):
            x2[half, layer, :count, :] = x1_ref[half, layer] - step * g1_ref[half, layer]
    begin = s["first"] - low
    slope_pass(s, x2, low * SUB, begin, begin + height // SUB, div, flux, where)

    def body(tile, carry):
        at = pl.ds(pl.multiple_of(tile * SUB, SUB), SUB)
        before = pl.ds(tile * SUB - 1, SUB)
        out = pl.ds(pl.multiple_of((tile - begin) * SUB, SUB), SUB)
        for layer in range(layers):
            here = x2[0, layer, at, :]
            slope = pull_ref[layer, out, :] - step * again_ref[layer, out, :]
            slope = slope + WEIGHT_TV * (div[0, layer, at, :] + flux[0, layer, before, :]) + DAMPING * here
            x2_ref[layer, out, :] = here
            g2_ref[layer, out, :] = slope
            old = g1_ref[0, layer, at, :]
            carry = carry + old * (slope - old)
        return carry

    total = lax.fori_loop(begin, begin + height // SUB, body, jnp.zeros((SUB, breadth), F32))
    growth = -step * jnp.sum(total, axis=(0, 1), keepdims=True)
    part_ref[...] = jnp.broadcast_to(growth, part_ref.shape)
    keep_ref[...] = jnp.broadcast_to(step * step * one_sq, keep_ref.shape)


def final_kernel(sums_ref, keep_ref, x2_ref, g2_ref, out_ref):
    step = keep_ref[:1, :] / jnp.sum(sums_ref[...], axis=0, keepdims=True)
    for layer in range(x2_ref.shape[0]):
        out_ref[layer] = x2_ref[layer] - step * g2_ref[layer]


def pairings(count):
    def both(start):
        pairs = []
        for i in range(start, count - 1, 2):
            pairs += [(i, i + 1), (i + 1, i)]
        return pairs

    return both(0), both(1)


def call(kernel, outs, scratch=(), inputs=None):
    whole = pl.BlockSpec(memory_space=pltpu.VMEM)
    return pl.pallas_call(
        kernel,
        out_shape=outs,
        in_specs=inputs,
        out_specs=jax.tree.map(lambda _: whole, outs),
        scratch_shapes=list(scratch),
        compiler_params=pltpu.CompilerParams(vmem_limit_bytes=VMEM_BYTES),
    )


def per_device(observed, profiles, tile_index):
    layers, height, breadth = observed.shape
    s = plan(layers, height, breadth, profiles.shape[2])
    halo, rows, taps = s["halo"], s["rows"], s["taps"]
    ring = 2 * breadth
    gy = lax.axis_index("gy")
    n = lax.axis_size("gy") * lax.axis_size("gx")
    vmem, smem = pl.BlockSpec(memory_space=pltpu.VMEM), pl.BlockSpec(memory_space=pltpu.SMEM)
    sds = jax.ShapeDtypeStruct

    even = lax.rem(gy, 2) == 0
    bottom, top = jnp.int32(height - halo), jnp.int32(0)
    to_even = lax.dynamic_slice_in_dim(observed, jnp.where(even, bottom, top), halo, axis=1)
    to_odd = lax.dynamic_slice_in_dim(observed, jnp.where(even, top, bottom), halo, axis=1)
    first_pairs, second_pairs = pairings(lax.axis_size("gy"))
    from_even = lax.ppermute(to_even, "gy", first_pairs)
    from_odd = lax.ppermute(to_odd, "gy", second_pairs)

    taps_all, m_high, m_low = call(
        functools.partial(weights_kernel, s),
        (sds((3, 2, 2, taps, SUB, breadth), F32), sds((3, ring, ring), BF16), sds((3, ring, ring), BF16)),
        inputs=[smem, smem],
    )(tile_index, profiles.transpose(2, 1, 0))

    packed = (layers // s["per_pack"], height + 2 * halo, breadth)
    first, second = call(
        functools.partial(pack_kernel, s), (sds(packed, F32), sds(packed, F32)), inputs=[vmem] * 3
    )(observed, from_even, from_odd)
    first_pairs, second_pairs = pairings(lax.axis_size("gx"))
    got_first = lax.ppermute(first, "gx", first_pairs)
    got_second = lax.ppermute(second, "gx", second_pairs)

    big = pltpu.VMEM((2, layers, rows, breadth), F32)
    low, high = reach(s, 2 * s["radius"])
    wide = (2, layers, (high - low) * SUB, breadth)
    tile = sds((layers, height, breadth), F32)
    x1, g1, pull, again, part = call(
        functools.partial(main_kernel, s),
        (sds(wide, F32), sds(wide, F32), tile, tile, sds((n, breadth), F32)),
        scratch=[big] * 15,
        inputs=[vmem] * 8,
    )(observed, from_even, from_odd, got_first, got_second, taps_all, m_high, m_low)
    sums = lax.all_to_all(part, ("gy", "gx"), 0, 0, tiled=True)
    work = pltpu.VMEM((2, layers, (high - low + 1) * SUB, breadth), F32)
    x2, g2, part, keep = call(
        functools.partial(step_kernel, s),
        (tile, tile, sds((n, breadth), F32), sds((SUB, breadth), F32)),
        scratch=[work] * 3,
        inputs=[vmem] * 5,
    )(sums, x1, g1, pull, again)
    sums = lax.all_to_all(part, ("gy", "gx"), 0, 0, tiled=True)
    return call(final_kernel, tile, inputs=[vmem] * 4)(sums, keep, x2, g2)


def solution(mesh):
    in_specs = (P(None, "gy", "gx"), P(), P())
    out_specs = P(None, "gy", "gx")
    return jax.shard_map(
        per_device, mesh=mesh, in_specs=in_specs, out_specs=out_specs, check_vma=False
    )
```

profile of v0, /device:TPU:0, one launch (start us, length us, event | category | flops | bytes accessed | tf_op | source)
XLA Modules:
  0.0 65.2 jit_solution(15393275166811448599)
XLA Ops:
  0.0 0.0 copy-start
  0.0 1.1 %constant_dynamic-slice_fusion = (f32[16,24,128]{2,1,0:T(8,128)S(1)}, f32[16,24,128]{2,1,0:T(8,128)S(1)}) fusion(f32[16,32,128]{2,1,0:T(8,128)} %tile_ref.3, s32[]{:T(128)S(6)} %select_n.10, s32[]{:T(128)S(6)} %select_n.9), kind=kLoop, calls=%fused_computation | loop fusion | bytes 786440 | tf_op jit(solution)/shard_map/dynamic_slice | solution.py:459
  1.1 0.7 %collective-permute-start.1 = (f32[16,24,128]{2,1,0:T(8,128)S(1)}, f32[16,24,128]{2,1,0:T(8,128)S(1)}, u32[]{:S(2)}, u32[]{:S(2)}) collective-permute-start(f32[16,24,128]{2,1,0:T(8,128)S(1)} %get-tuple-element.33), channel_id=1, source_target_pairs={{8,16},{16,8},{9,17},{17,9},{10,18},{18,10},{11,19},{19,11},{12,20... | collective-permute-start | bytes 589832 | tf_op jit(solution)/shard_map/ppermute | solution.py:462
  1.8 5.9 %collective-permute-start = (f32[16,24,128]{2,1,0:T(8,128)S(1)}, f32[16,24,128]{2,1,0:T(8,128)S(1)}, u32[]{:S(2)}, u32[]{:S(2)}) collective-permute-start(f32[16,24,128]{2,1,0:T(8,128)S(1)} %get-tuple-element.34), channel_id=1, source_target_pairs={{0,8},{8,0},{16,24},{24,16},{1,9},{9,1},{17,25},{25,17},{2,10},{10... | collective-permute-start | bytes 589832 | tf_op jit(solution)/shard_map/ppermute | solution.py:461
  7.7 0.0 collective-permute-done.1.odd_ref
  7.7 4.6 %collective-permute-done.even_ref = f32[16,24,128]{2,1,0:T(8,128)S(1)} collective-permute-done((f32[16,24,128]{2,1,0:T(8,128)S(1)}, f32[16,24,128]{2,1,0:T(8,128)S(1)}, u32[]{:S(2)}, u32[]{:S(2)}) %collective-permute-start) | collective-permute-done | bytes 196640 | tf_op jit(solution)/shard_map/ppermute | solution.py:461
  12.3 0.0 copy-done
  12.3 0.0 copy-start.1
  12.3 0.4 shard_map.37
  12.7 0.0 copy-start.2
  12.7 0.1 collective-permute-start.2
  12.8 0.7 %collective-permute-start.3 = (f32[4,80,128]{2,1,0:T(8,128)S(1)}, f32[4,80,128]{2,1,0:T(8,128)S(1)}, u32[]{:S(2)}, u32[]{:S(2)}) collective-permute-start(f32[4,80,128]{2,1,0:T(8,128)S(1)} %get-tuple-element.20), channel_id=1, source_target_pairs={{1,2},{2,1},{3,4},{4,3},{5,6},{6,5},{9,10},{10,9},{11,12},{12,11},... | collective-permute-start | bytes 491528 | tf_op jit(solution)/shard_map/ppermute | solution.py:476
  13.5 0.0 copy-done.1
  13.5 0.0 copy-done.2
  13.5 2.1 %shard_map.38 = (f32[3,2,2,9,8,128]{5,4,3,2,1,0:T(8,128)S(1)}, bf16[3,256,256]{2,1,0:T(8,128)(2,1)S(1)}, bf16[3,256,256]{2,1,0:T(8,128)(2,1)S(1)}) custom-call(s32[4,8]{1,0:T(4,128)S(1)} %copy-done.2, f32[9,3,64]{2,1,0:T(4,128)S(1)} %bitcast.11), custom_call_target="tpu_custom_call" | custom-call | tf_op jit(solution)/shard_map/pallas_call | solution.py:464
  15.6 0.0 collective-permute-done.2.first_ref
  15.6 0.0 collective-permute-done.3.second_ref
  15.6 22.2 %shard_map.39 = (f32[2,16,48,128]{3,2,1,0:T(8,128)S(1)}, f32[2,16,48,128]{3,2,1,0:T(8,128)S(1)}, f32[16,32,128]{2,1,0:T(8,128)S(1)}, f32[16,32,128]{2,1,0:T(8,128)S(1)}, f32[32,128]{1,0:T(8,128)S(1)}) custom-call(f32[16,32,128]{2,1,0:T(8,128)S(1)} %copy-done, f32[16,24,128]{2,1,0:T(8,128)S(1)} %collective-permute-done.even_ref, ...), custom_call_target="tpu_custom_call" | custom-call | tf_op jit(solution)/shard_map/pallas_call | solution.py:482
  37.9 16.2 %all_to_all.22 = f32[32,1,128]{2,1,0:T(1,128)S(1)} all-to-all(f32[32,1,128]{2,1,0:T(1,128)S(1)} %bitcast.12), channel_id=1, replica_groups=mesh['gy'=4,'gx'=8] {'gy','gx'}, dimensions={0} | all-to-all | bytes 32768 | tf_op jit(solution)/shard_map/all_to_all | solution.py:488
  54.1 1.5 %shard_map.40 = (f32[16,32,128]{2,1,0:T(8,128)S(1)}, f32[16,32,128]{2,1,0:T(8,128)S(1)}, f32[32,128]{1,0:T(8,128)S(1)}, f32[8,128]{1,0:T(8,128)S(1)}) custom-call(f32[32,128]{1,0:T(8,128)S(1)} %bitcast.9, f32[2,16,48,128]{3,2,1,0:T(8,128)S(1)} %get-tuple-element.25.x1_ref, f32[2,16,48,128]{3,2,1,0:T(8,128)S(1)} %get-tuple-element.26.g1_ref, ...), custom_call_target="tpu_custom_call" | custom-call | tf_op jit(solution)/shard_map/pallas_call | solution.py:490
  55.6 8.8 %all_to_all.23 = f32[32,1,128]{2,1,0:T(1,128)S(1)} all-to-all(f32[32,1,128]{2,1,0:T(1,128)S(1)} %bitcast.13), channel_id=1, replica_groups=mesh['gy'=4,'gx'=8] {'gy','gx'}, dimensions={0} | all-to-all | bytes 32768 | tf_op jit(solution)/shard_map/all_to_all | solution.py:496
  64.4 0.7 %shard_map.41 = f32[16,32,128]{2,1,0:T(8,128)} custom-call(f32[32,128]{1,0:T(8,128)S(1)} %bitcast.10, f32[8,128]{1,0:T(8,128)S(1)} %get-tuple-element.30.keep_ref, f32[16,32,128]{2,1,0:T(8,128)S(1)} %get-tuple-element.31.x2_ref, f32[16,32,128]{2,1,0:T(8,128)S(1)} %get-tuple-element.32.g2_ref), custom_call_target="tpu_custom_call" | custom-call | tf_op jit(solution)/shard_map/pallas_call | solution.py:497
Async XLA Ops:
  0.0 12.3 %copy-start = (f32[16,32,128]{2,1,0:T(8,128)S(1)}, f32[16,32,128]{2,1,0:T(8,128)}, u32[]{:S(2)}) copy-start(f32[16,32,128]{2,1,0:T(8,128)} %tile_ref.3) | copy-start | bytes 786436
  1.1 6.6 %collective-permute-start.1 = (f32[16,24,128]{2,1,0:T(8,128)S(1)}, f32[16,24,128]{2,1,0:T(8,128)S(1)}, u32[]{:S(2)}, u32[]{:S(2)}) collective-permute-start(f32[16,24,128]{2,1,0:T(8,128)S(1)} %get-tuple-element.33), channel_id=1, source_target_pairs={{8,16},{16,8},{9,17},{17,9},{10,18},{18,10},{11,19},{19,11},{12,20... | collective-permute-start | bytes 589832 | tf_op jit(solution)/shard_map/ppermute | solution.py:462
  1.8 10.5 %collective-permute-start = (f32[16,24,128]{2,1,0:T(8,128)S(1)}, f32[16,24,128]{2,1,0:T(8,128)S(1)}, u32[]{:S(2)}, u32[]{:S(2)}) collective-permute-start(f32[16,24,128]{2,1,0:T(8,128)S(1)} %get-tuple-element.34), channel_id=1, source_target_pairs={{0,8},{8,0},{16,24},{24,16},{1,9},{9,1},{17,25},{25,17},{2,10},{10... | collective-permute-start | bytes 589832 | tf_op jit(solution)/shard_map/ppermute | solution.py:461
  12.3 1.2 %copy-start.1 = (f32[64,3,9]{0,1,2:T(4,128)S(1)}, f32[64,3,9]{0,1,2:T(4,128)}, u32[]{:S(2)}) copy-start(f32[64,3,9]{0,1,2:T(4,128)} %param.4) | copy-start | bytes 20740
  12.7 0.8 %copy-start.2 = (s32[4,8]{1,0:T(4,128)S(1)}, s32[4,8]{1,0:T(4,128)}, u32[]{:S(2)}) copy-start(s32[4,8]{1,0:T(4,128)} %index_ref.1) | copy-start | bytes 388
  12.7 2.9 %collective-permute-start.2 = (f32[4,80,128]{2,1,0:T(8,128)S(1)}, f32[4,80,128]{2,1,0:T(8,128)S(1)}, u32[]{:S(2)}, u32[]{:S(2)}) collective-permute-start(f32[4,80,128]{2,1,0:T(8,128)S(1)} %get-tuple-element.19), channel_id=1, source_target_pairs={{0,1},{1,0},{2,3},{3,2},{4,5},{5,4},{6,7},{7,6},{8,9},{9,8},{10,11... | collective-permute-start | bytes 491528 | tf_op jit(solution)/shard_map/ppermute | solution.py:475
  12.8 2.8 %collective-permute-start.3 = (f32[4,80,128]{2,1,0:T(8,128)S(1)}, f32[4,80,128]{2,1,0:T(8,128)S(1)}, u32[]{:S(2)}, u32[]{:S(2)}) collective-permute-start(f32[4,80,128]{2,1,0:T(8,128)S(1)} %get-tuple-element.20), channel_id=1, source_target_pairs={{1,2},{2,1},{3,4},{4,3},{5,6},{6,5},{9,10},{10,9},{11,12},{12,11},... | collective-permute-start | bytes 491528 | tf_op jit(solution)/shard_map/ppermute | solution.py:476
where the time goes:
time: 65.4 us; the launch traced here: 65.2 us
  Pallas kernels  27 us (41%)
  blocking collectives  25 us (38%)
  starting transfers between devices  7.32 us (11%)
  waiting for transfers between devices  4.63 us (7%)
  local copies, waits for them, and re-layouts  1.12 us (2%)
    all_to_all x2, blocking collectives, per_device(): sums = lax.all_to_all(part, ('gy', 'gx'), 0, 0, tiled=True)  25 us
    pallas_call x1, Pallas kernels, per_device(): call(functools.partial(main_kernel, s), (sds(wide, F32), sds(wide, F32),...  22.2 us
    ppermute x1, starting transfers between devices, per_device(): from_even = lax.ppermute(to_even, 'gy', first_pairs)  5.9 us
    ppermute x1, waiting for transfers between devices, per_device(): from_even = lax.ppermute(to_even, 'gy', first_pairs)  4.62 us
    pallas_call x1, Pallas kernels, per_device(): call(functools.partial(weights_kernel, s), (sds((3, 2, 2, taps, SUB, brea...  2.09 us
    pallas_call x1, Pallas kernels, per_device(): call(functools.partial(step_kernel, s), (tile, tile, sds((n, breadth), F3...  1.5 us
  transfers between devices with their start and end apart: 4, of which 1 were waited for; matrix products, arithmetic and copies ran while one was open for 0% of the time, Pallas kernels for 3%

commit v1 on v0

v1 whole, which is shorter than its diff:
```python
import functools
import jax
import jax.numpy as jnp
from jax import lax
from jax.experimental import pallas as pl
from jax.experimental.pallas import tpu as pltpu
from jax.sharding import PartitionSpec as P

ITERS = 2
WEIGHT_TV = 0.02
SMOOTHING = 0.1
DAMPING = 0.05
START_STEP = 0.5
SUB = 8
F32 = jnp.float32
BF16 = jnp.bfloat16
VMEM_BYTES = 44 * 1024 * 1024


def plan(layers, height, breadth, taps):
    radius = (taps - 1) // 2
    halo = 6 * radius
    off = -(-halo // SUB) * SUB + SUB
    return dict(
        layers=layers, height=height, breadth=breadth, taps=taps, radius=radius, halo=halo, off=off,
        rows=height + 2 * off, groups=-(-layers * halo // breadth), first=off // SUB, last=(off + height) // SUB,
        tiles=(height + 2 * off) // SUB,
    )


def reach(s, extent):
    low = (s["off"] - extent) // SUB
    high = -(-(s["off"] + s["height"] + extent) // SUB)
    return low, high


def bands(s):
    return ((0, s["first"]), (s["first"], s["last"]), (s["last"], s["tiles"]))


def place():
    return lax.axis_index("gy"), lax.axis_index("gx"), lax.axis_size("gy"), lax.axis_size("gx")


def weights_kernel(s, index_ref, profiles_ref, taps_ref, forward_ref, backward_ref, full):
    gy, gx, ny, nx = place()
    breadth, taps, radius = s["breadth"], s["taps"], s["radius"]
    ring = 2 * breadth
    lane = lax.broadcasted_iota(jnp.int32, (SUB, breadth), 1)
    chunk = 32

    def split(value):
        upper = value.astype(BF16)
        return upper, (value - upper.astype(F32)).astype(BF16)

    for band in range(3):
        row = gy + (band - 1)
        picked = []
        for side in range(3):
            col = gx + (side - 1)
            inside = (row >= 0) & (row < ny) & (col >= 0) & (col < nx)
            number = index_ref[jnp.clip(row, 0, ny - 1), jnp.clip(col, 0, nx - 1)]
            picked.append((inside, number))
        columns = []
        for dim in range(3):
            for tap in range(taps):
                left, centre, right = [
                    jnp.where(inside, profiles_ref[tap, dim, number], 0.0) for inside, number in picked
                ]
                main = jnp.full((SUB, breadth), centre, F32)
                side = jnp.where(lane < breadth // 2, right, left)
                if dim < 2:
                    taps_ref[band, dim, 0, tap] = main
                    taps_ref[band, dim, 1, tap] = side
                else:
                    columns.append(jnp.concatenate([main, side], axis=1)[:1])

        def build(piece, carry, band=band, columns=columns):
            start = pl.multiple_of(piece * chunk, chunk)
            source = lax.broadcasted_iota(jnp.int32, (chunk, ring), 0) + start
            target = lax.broadcasted_iota(jnp.int32, (chunk, ring), 1)
            distance = target - source + radius
            distance = jnp.where(distance < 0, distance + ring, distance)
            distance = jnp.where(distance >= ring, distance - ring, distance)
            total = jnp.zeros((chunk, ring), F32)
            for tap in range(taps):
                total = jnp.where(distance == tap, columns[tap], total)
            full[pl.ds(start, chunk), :] = total
            return carry

        lax.fori_loop(0, ring // chunk, build, 0)
        value = full[...]
        for ref, matrix in ((forward_ref, value), (backward_ref, value.T)):
            upper, lower = split(matrix)
            ref[band, :ring, :] = upper
            ref[band, ring:2 * ring, :] = lower
            ref[band, 2 * ring:, :] = upper


def strip_places(s, layer):
    group, lane = divmod(layer * s["halo"], s["breadth"])
    return group, lane, min(s["halo"], s["breadth"] - lane)


def pack_kernel(s, tile_ref, even_ref, odd_ref, first_ref, second_ref):
    gy, gx, _, _ = place()
    halo, height, breadth = s["halo"], s["height"], s["breadth"]
    row_even, col_even = lax.rem(gy, 2) == 0, lax.rem(gx, 2) == 0
    lane = lax.broadcasted_iota(jnp.int32, (1, breadth), 1)
    for start, count in ((0, halo), (halo, height), (halo + height, halo)):
        first = [jnp.zeros((count, breadth), F32)] * s["groups"]
        second = list(first)
        for layer in range(s["layers"]):
            if start == halo:
                value = tile_ref[layer]
            elif start == 0:
                value = jnp.where(row_even, odd_ref[layer], even_ref[layer])
            else:
                value = jnp.where(row_even, even_ref[layer], odd_ref[layer])
            group, begin, here = strip_places(s, layer)
            from_left, from_right = begin, (begin + halo) % breadth
            to_first = pltpu.roll(value, jnp.where(col_even, from_right, from_left), 1)
            to_second = pltpu.roll(value, jnp.where(col_even, from_left, from_right), 1)
            parts = [(group, (lane >= begin) & (lane < begin + here))]
            if here < halo:
                parts.append((group + 1, lane < halo - here))
            for number, mine in parts:
                first[number] = jnp.where(mine, to_first, first[number])
                second[number] = jnp.where(mine, to_second, second[number])
        for number in range(s["groups"]):
            first_ref[number, start:start + count, :] = first[number]
            second_ref[number, start:start + count, :] = second[number]


def unpack_layer(s, groups, layer, to):
    breadth = s["breadth"]
    lane = lax.broadcasted_iota(jnp.int32, (1, breadth), 1)
    group, begin, here = strip_places(s, layer)
    value = groups[group]
    if here < s["halo"]:
        value = jnp.where(lane >= begin, value, groups[group + 1])
    shift = (to - begin) % breadth
    return pltpu.roll(value, shift, 1) if shift else value


def row_depth(s, load, row_taps, depth_taps, transposed):
    layers, taps, radius = s["layers"], s["taps"], s["radius"]
    mixed = []
    for layer in range(layers):
        total = None
        for tap in range(taps):
            term = row_taps[tap] * load(layer, tap - radius if transposed else radius - tap)
            total = term if total is None else total + term
        mixed.append(total)
    outs = []
    for layer in range(layers):
        total = None
        for tap in range(taps):
            shift = tap - radius if transposed else radius - tap
            if 0 <= layer + shift < layers:
                term = depth_taps[tap] * mixed[layer + shift]
                total = term if total is None else total + term
        outs.append(total)
    return outs


def slope_tile(s, source, shift, tile, divergence, flux_rows, where):
    gy, gx, ny, nx = where
    layers, height, breadth = s["layers"], s["height"], s["breadth"]
    ring = 2 * breadth
    lane = lax.broadcasted_iota(jnp.int32, (SUB, ring), 1)
    col = gx * breadth + jnp.where(lane < breadth + breadth // 2, lane, lane - ring)
    col_mask = jnp.where((col >= 0) & (col < nx * breadth - 1), 1.0, 0.0).astype(F32)
    start = tile * SUB
    row = gy * height + start - s["off"] + shift + lax.broadcasted_iota(jnp.int32, (SUB, ring), 0)
    row_mask = jnp.where((row >= 0) & (row < ny * height - 1), 1.0, 0.0).astype(F32)

    def load(layer, begin):
        return jnp.concatenate([source[half, layer, begin:begin + SUB, :] for half in range(2)], axis=1)

    here = load(0, start)
    flux_before = None
    for layer in range(layers):
        below = load(layer, start + 1)
        step_rows = (below - here) * row_mask
        step_cols = (pltpu.roll(here, ring - 1, 1) - here) * col_mask
        square = step_rows * step_rows + step_cols * step_cols + SMOOTHING * SMOOTHING
        if layer + 1 < layers:
            after = load(layer + 1, start)
            step_depth = after - here
            square = square + step_depth * step_depth
        inverse = lax.rsqrt(square)
        f_rows, f_cols = step_rows * inverse, step_cols * inverse
        total = pltpu.roll(f_cols, 1, 1) - f_cols - f_rows
        if flux_before is not None:
            total = total + flux_before
        if layer + 1 < layers:
            flux_before = step_depth * inverse
            total = total - flux_before
            here = after
        for half in range(2):
            part = slice(half * breadth, (half + 1) * breadth)
            divergence[half, layer, start:start + SUB, :] = total[:, part]
            flux_rows[half, layer, start:start + SUB, :] = f_rows[:, part]


def main_kernel(s, tile_ref, even_ref, odd_ref, first_ref, second_ref, taps_ref, forward_ref, backward_ref,
                x1_ref, g1_ref, pull_ref, again_ref, part_ref,
                x0, x1, x2, g0, y0, y1, y2, r0, r1, r2, q0, q1, q2, acc, div, flux):
    where = place()
    gy, gx, ny, nx = where
    layers, height, breadth, off = s["layers"], s["height"], s["breadth"], s["off"]
    halo, radius, taps = s["halo"], s["radius"], s["taps"]
    begin, end = s["first"], s["last"]
    row_even, col_even = lax.rem(gy, 2) == 0, lax.rem(gx, 2) == 0
    lane = lax.broadcasted_iota(jnp.int32, (1, breadth), 1)
    xs, ys, rs, qs = (x0, x1, x2), (y0, y1, y2), (r0, r1, r2), (q0, q1, q2)
    span = bands(s)

    def rows(tile, stop=None):
        return slice(tile * SUB, (tile + 1 if stop is None else stop) * SUB)

    top = off - halo
    x0[0, :, top:off, :] = jnp.where(row_even, odd_ref[...], even_ref[...])
    x0[0, :, off:off + height, :] = tile_ref[...]
    x0[0, :, off + height:off + height + halo, :] = jnp.where(row_even, even_ref[...], odd_ref[...])
    firsts = [first_ref[g] for g in range(s["groups"])]
    seconds = [second_ref[g] for g in range(s["groups"])]
    rights = [jnp.where(col_even, a, b) for a, b in zip(firsts, seconds)]
    lefts = [jnp.where(col_even, b, a) for a, b in zip(firsts, seconds)]
    for layer in range(layers):
        value = jnp.where(lane < halo, unpack_layer(s, rights, layer, 0), 0.0)
        value = jnp.where(lane >= breadth - halo, unpack_layer(s, lefts, layer, breadth - halo), value)
        x0[1, layer, top:off + height + halo, :] = value
    zero = jnp.zeros((2, layers, SUB, breadth), F32)
    for ref, tiles in ((y0, (0,)), (y2, (s["tiles"] - 1,)), (r0, (begin, begin + 1)),
                       (r1, (begin - 2, begin - 1, end, end + 1)), (r2, (end - 2, end - 1))):
        for tile in tiles:
            ref[:, :, rows(tile), :] = zero

    def chunk(ref, low, high):
        value = jnp.concatenate(
            [ref[half, :, rows(low, high), :].reshape(layers * (high - low) * SUB, breadth) for half in range(2)], axis=1)
        upper = value.astype(BF16)
        lower = (value - upper.astype(F32)).astype(BF16)
        return jnp.concatenate([upper, upper, lower], axis=1)

    def halves(result, low, high):
        return [result[:, h * breadth:(h + 1) * breadth].reshape(layers, (high - low) * SUB, breadth) for h in range(2)]

    def taps_of(band, half):
        return [[taps_ref[band, dim, half, t] for t in range(taps)] for dim in (1, 0)]

    def one_pass(number):
        x = xs[number]
        low, high = reach(s, (5 - 2 * number) * radius)
        in_low, in_high = reach(s, (6 - 2 * number) * radius)
        back_low, back_high = reach(s, (4 - 2 * number) * radius)
        out = [(max(low, a), min(high, b)) for a, b in span]
        back = [(max(back_low, a - 1), min(back_high, b + 1)) for a, b in span]
        done = set()

        def columns(band):
            a, b = max(out[band][0] - 1, in_low), min(out[band][1] + 1, in_high)
            result = jnp.dot(chunk(x, a, b), forward_ref[band], preferred_element_type=F32)
            for half, piece in enumerate(halves(result, a, b)):
                ys[band][half, :, rows(a, b), :] = piece

        def blur_rows(band):
            for tile in range(*out[band]):
                for half in range(2):
                    load = lambda layer, shift: ys[band][half, layer, tile * SUB + shift:(tile + 1) * SUB + shift, :]
                    outs = row_depth(s, load, *taps_of(band, half), False)
                    for layer in range(layers):
                        value = outs[layer] if number == 2 else outs[layer] - x0[half, layer, rows(tile), :]
                        rs[band][half, layer, rows(tile), :] = value

        def back_rows(band):
            for tile in range(*back[band]):
                for half in range(2):
                    load = lambda layer, shift: rs[band][half, layer, tile * SUB + shift:(tile + 1) * SUB + shift, :]
                    outs = row_depth(s, load, *taps_of(band, half), True)
                    for layer in range(layers):
                        qs[band][half, layer, rows(tile), :] = outs[layer]

        def back_columns(band):
            a, b = back[band]
            result = jnp.dot(chunk(qs[band], a, b), backward_ref[band], preferred_element_type=F32)
            for half, piece in enumerate(halves(result, a, b)):
                for tile in range(a, b):
                    part = piece[:, (tile - a) * SUB:(tile - a + 1) * SUB, :]
                    acc[half, :, rows(tile), :] = acc[half, :, rows(tile), :] + part if tile in done else part
            done.update(range(a, b))

        def inside(tile, half):
            row = gy * height + tile * SUB - off + lax.broadcasted_iota(jnp.int32, (SUB, breadth), 0)
            here = lax.broadcasted_iota(jnp.int32, (SUB, breadth), 1)
            if half == 1:
                here = jnp.where(here < breadth // 2, here + breadth, here - breadth)
            col = gx * breadth + here
            return (row >= 0) & (row < ny * height) & (col >= 0) & (col < nx * breadth)

        def update(tile):
            for half in range(2):
                keep = inside(tile, half)
                for layer in range(layers):
                    here = x[half, layer, rows(tile), :]
                    total = acc[half, layer, rows(tile), :] + DAMPING * here
                    before = flux[half, layer, tile * SUB - 1:(tile + 1) * SUB - 1, :]
                    total = total + WEIGHT_TV * (div[half, layer, rows(tile), :] + before)
                    total = jnp.where(keep, total, 0.0)
                    if number == 0:
                        xs[1][half, layer, rows(tile), :] = here - START_STEP * total
                        if half == 0 and begin <= tile < end:
                            g0[layer, rows(tile), :] = total
                    else:
                        xs[2][half, layer, rows(tile), :] = total

        def slopes(a, b):
            if number < 2:
                for tile in range(a, b):
                    slope_tile(s, x, 0, tile, div, flux, where)

        middle = (begin + end) // 2
        columns(0)
        slopes(back_low - 1, middle)
        columns(1)
        blur_rows(0)
        columns(2)
        back_rows(0)
        blur_rows(1)
        back_columns(0)
        back_rows(1)
        back_columns(1)
        blur_rows(2)
        slopes(middle, back_high)
        back_rows(2)
        back_columns(2)
        if number == 1:
            pull_ref[...] = acc[0, :, rows(begin, end), :]
        if number < 2:
            for tile in range(back_low, back_high):
                update(tile)

    for number in range(3):
        one_pass(number)
    again_ref[...] = acc[0, :, rows(begin, end), :]
    low, high = reach(s, 2 * radius)
    x1_ref[...] = x1[:, :, rows(low, high), :]
    g1_ref[...] = x2[:, :, rows(low, high), :]

    zero_sq = cross = one_sq = jnp.zeros((SUB, breadth), F32)
    for tile in range(begin, end):
        for layer in range(layers):
            a, b = g0[layer, rows(tile), :], x2[0, layer, rows(tile), :]
            zero_sq, cross, one_sq = zero_sq + a * a, cross + a * (b - a), one_sq + b * b
    zero_sq, cross, one_sq = [jnp.sum(t, axis=(0, 1), keepdims=True) for t in (zero_sq, cross, one_sq)]
    row = jnp.where(lane == 0, zero_sq, jnp.where(lane == 1, cross, one_sq))
    part_ref[...] = jnp.broadcast_to(row, part_ref.shape)


def step_kernel(s, sums_ref, x1_ref, g1_ref, pull_ref, again_ref, x2_ref, g2_ref, part_ref, keep_ref, x2, div, flux):
    where = place()
    layers, height, breadth = s["layers"], s["height"], s["breadth"]
    low, high = reach(s, 2 * s["radius"])
    lane = lax.broadcasted_iota(jnp.int32, (1, breadth), 1)
    total = jnp.sum(sums_ref[...], axis=0, keepdims=True)
    zero_sq, cross, one_sq = [
        jnp.sum(jnp.where(lane == number, total, 0.0), axis=(0, 1), keepdims=True) for number in range(3)
    ]
    step = (START_STEP * START_STEP * zero_sq) / (-START_STEP * cross)
    count = (high - low) * SUB
    for half in range(2):
        for layer in range(layers):
            x2[half, layer, :count, :] = x1_ref[half, layer] - step * g1_ref[half, layer]
    begin = s["first"] - low
    total = jnp.zeros((SUB, breadth), F32)
    for tile in range(begin - 1, begin + height // SUB):
        slope_tile(s, x2, low * SUB, tile, div, flux, where)
        if tile < begin:
            continue
        at, out = slice(tile * SUB, (tile + 1) * SUB), slice((tile - begin) * SUB, (tile - begin + 1) * SUB)
        for layer in range(layers):
            here = x2[0, layer, at, :]
            slope = pull_ref[layer, out, :] - step * again_ref[layer, out, :] + DAMPING * here
            slope = slope + WEIGHT_TV * (div[0, layer, at, :] + flux[0, layer, tile * SUB - 1:(tile + 1) * SUB - 1, :])
            x2_ref[layer, out, :] = here
            g2_ref[layer, out, :] = slope
            old = g1_ref[0, layer, at, :]
            total = total + old * (slope - old)
    growth = -step * jnp.sum(total, axis=(0, 1), keepdims=True)
    part_ref[...] = jnp.broadcast_to(growth, part_ref.shape)
    keep_ref[...] = jnp.broadcast_to(step * step * one_sq, keep_ref.shape)


def final_kernel(sums_ref, keep_ref, x2_ref, g2_ref, out_ref):
    step = keep_ref[:1, :] / jnp.sum(sums_ref[...], axis=0, keepdims=True)
    for layer in range(x2_ref.shape[0]):
        out_ref[layer] = x2_ref[layer] - step * g2_ref[layer]


def pairings(count):
    def both(start):
        pairs = []
        for i in range(start, count - 1, 2):
            pairs += [(i, i + 1), (i + 1, i)]
        return pairs

    return both(0), both(1)


def call(kernel, outs, scratch=(), inputs=None):
    whole = pl.BlockSpec(memory_space=pltpu.VMEM)
    return pl.pallas_call(
        kernel,
        out_shape=outs,
        in_specs=inputs,
        out_specs=jax.tree.map(lambda _: whole, outs),
        scratch_shapes=list(scratch),
        compiler_params=pltpu.CompilerParams(vmem_limit_bytes=VMEM_BYTES),
    )


def per_device(observed, profiles, tile_index):
    layers, height, breadth = observed.shape
    s = plan(layers, height, breadth, profiles.shape[2])
    halo, rows, taps = s["halo"], s["rows"], s["taps"]
    ring = 2 * breadth
    gy = lax.axis_index("gy")
    n = lax.axis_size("gy") * lax.axis_size("gx")
    vmem, smem = pl.BlockSpec(memory_space=pltpu.VMEM), pl.BlockSpec(memory_space=pltpu.SMEM)
    sds = jax.ShapeDtypeStruct

    even = lax.rem(gy, 2) == 0
    bottom, top = jnp.int32(height - halo), jnp.int32(0)
    to_even = lax.dynamic_slice_in_dim(observed, jnp.where(even, bottom, top), halo, axis=1)
    to_odd = lax.dynamic_slice_in_dim(observed, jnp.where(even, top, bottom), halo, axis=1)
    first_pairs, second_pairs = pairings(lax.axis_size("gy"))
    from_even = lax.ppermute(to_even, "gy", first_pairs)
    from_odd = lax.ppermute(to_odd, "gy", second_pairs)

    taps_all, forward, backward = call(
        functools.partial(weights_kernel, s),
        (sds((3, 2, 2, taps, SUB, breadth), F32), sds((3, 3 * ring, ring), BF16), sds((3, 3 * ring, ring), BF16)),
        scratch=[pltpu.VMEM((ring, ring), F32)],
        inputs=[smem, smem],
    )(tile_index, profiles.transpose(2, 1, 0))

    packed = (s["groups"], height + 2 * halo, breadth)
    first, second = call(
        functools.partial(pack_kernel, s), (sds(packed, F32), sds(packed, F32)), inputs=[vmem] * 3
    )(observed, from_even, from_odd)
    first_pairs, second_pairs = pairings(lax.axis_size("gx"))
    got_first = lax.ppermute(first, "gx", first_pairs)
    got_second = lax.ppermute(second, "gx", second_pairs)

    big = (2, layers, rows, breadth)
    low, high = reach(s, 2 * s["radius"])
    wide = (2, layers, (high - low) * SUB, breadth)
    tile = sds((layers, height, breadth), F32)
    x1, g1, pull, again, part = call(
        functools.partial(main_kernel, s),
        (sds(wide, F32), sds(wide, F32), tile, tile, sds((n, breadth), F32)),
        scratch=[pltpu.VMEM(shape, F32) for shape in [big] * 3 + [big[1:]] + [big] * 12],
        inputs=[vmem] * 8,
    )(observed, from_even, from_odd, got_first, got_second, taps_all, forward, backward)
    sums = lax.all_to_all(part, ("gy", "gx"), 0, 0, tiled=True)
    work = pltpu.VMEM((2, layers, (high - low + 1) * SUB, breadth), F32)
    x2, g2, part, keep = call(
        functools.partial(step_kernel, s),
        (tile, tile, sds((n, breadth), F32), sds((SUB, breadth), F32)),
        scratch=[work] * 3,
        inputs=[vmem] * 5,
    )(sums, x1, g1, pull, again)
    sums = lax.all_to_all(part, ("gy", "gx"), 0, 0, tiled=True)
    return call(final_kernel, tile, inputs=[vmem] * 4)(sums, keep, x2, g2)


def solution(mesh):
    in_specs = (P(None, "gy", "gx"), P(), P())
    out_specs = P(None, "gy", "gx")
    return jax.shard_map(
        per_device, mesh=mesh, in_specs=in_specs, out_specs=out_specs, check_vma=False
    )
```

time: 65.4 us -> 56.2 us (0.86)
  Pallas kernels: 27 us -> 18 us
  blocking collectives: 25 us -> 24 us
  local copies, waits for them, and re-layouts: 1.12 us -> 2.06 us
    pallas_call x1, Pallas kernels: 22.2 us -> 13.6 us  [per_device(): call(functools.partial(main_kernel, s), (sds(wide, F32), sds(wide, F32),...]
    all_to_all x2, blocking collectives: 25 us -> 24 us  [per_device(): sums = lax.all_to_all(part, ('gy', 'gx'), 0, 0, tiled=True)]
    unnamed x6 -> x8, local copies, waits for them, and re-layouts: 0.01 us -> 0.96 us
  transfers between devices with their start and end apart: 4 -> 4, of which waited for: 1 -> 1; matrix products, arithmetic and copies ran while one was open for 0% -> 0% of each run, Pallas kernels for 3% -> 4%
where the time goes in v1:
time: 56.2 us; the launch traced here: 56 us
  blocking collectives  24 us (43%)
  Pallas kernels  18 us (32%)
  starting transfers between devices  7.33 us (13%)
  waiting for transfers between devices  4.63 us (8%)
  local copies, waits for them, and re-layouts  2.06 us (4%)
    all_to_all x2, blocking collectives, per_device(): sums = lax.all_to_all(part, ('gy', 'gx'), 0, 0, tiled=True)  24 us
    pallas_call x1, Pallas kernels, per_device(): call(functools.partial(main_kernel, s), (sds(wide, F32), sds(wide, F32),...  13.6 us
    ppermute x1, starting transfers between devices, per_device(): from_even = lax.ppermute(to_even, 'gy', first_pairs)  5.91 us
    ppermute x1, waiting for transfers between devices, per_device(): from_even = lax.ppermute(to_even, 'gy', first_pairs)  4.62 us
    pallas_call x1, Pallas kernels, per_device(): call(functools.partial(weights_kernel, s), (sds((3, 2, 2, taps, SUB, brea...  2.3 us
  transfers between devices with their start and end apart: 4, of which 1 were waited for; matrix products, arithmetic and copies ran while one was open for 0% of the time, Pallas kernels for 4%

profile of v1, /device:TPU:0, one launch (start us, length us, event | category | flops | bytes accessed | tf_op | source)
XLA Modules:
  0.0 56.0 jit_solution(1854573361759241837)
XLA Ops:
  0.0 0.0 copy-start.1
  0.0 0.0 copy-start.3
  0.0 0.0 copy-start.2
  0.0 1.1 %constant_dynamic-slice_fusion = (f32[16,24,128]{2,1,0:T(8,128)S(1)}, f32[16,24,128]{2,1,0:T(8,128)S(1)}) fusion(f32[16,32,128]{2,1,0:T(8,128)} %tile_ref.3, s32[]{:T(128)S(6)} %select_n.10, s32[]{:T(128)S(6)} %select_n.9), kind=kLoop, calls=%fused_computation | loop fusion | bytes 786440 | tf_op jit(solution)/shard_map/dynamic_slice | solution.py:437
  1.1 0.7 %collective-permute-start.1 = (f32[16,24,128]{2,1,0:T(8,128)S(1)}, f32[16,24,128]{2,1,0:T(8,128)S(1)}, u32[]{:S(2)}, u32[]{:S(2)}) collective-permute-start(f32[16,24,128]{2,1,0:T(8,128)S(1)} %get-tuple-element.33), channel_id=1, source_target_pairs={{8,16},{16,8},{9,17},{17,9},{10,18},{18,10},{11,19},{19,11},{12,20... | collective-permute-start | bytes 589832 | tf_op jit(solution)/shard_map/ppermute | solution.py:440
  1.8 5.9 %collective-permute-start = (f32[16,24,128]{2,1,0:T(8,128)S(1)}, f32[16,24,128]{2,1,0:T(8,128)S(1)}, u32[]{:S(2)}, u32[]{:S(2)}) collective-permute-start(f32[16,24,128]{2,1,0:T(8,128)S(1)} %get-tuple-element.34), channel_id=1, source_target_pairs={{0,8},{8,0},{16,24},{24,16},{1,9},{9,1},{17,25},{25,17},{2,10},{10... | collective-permute-start | bytes 589832 | tf_op jit(solution)/shard_map/ppermute | solution.py:439
  7.7 0.0 collective-permute-done.1.odd_ref
  7.7 4.6 %collective-permute-done.even_ref = f32[16,24,128]{2,1,0:T(8,128)S(1)} collective-permute-done((f32[16,24,128]{2,1,0:T(8,128)S(1)}, f32[16,24,128]{2,1,0:T(8,128)S(1)}, u32[]{:S(2)}, u32[]{:S(2)}) %collective-permute-start) | collective-permute-done | bytes 196640 | tf_op jit(solution)/shard_map/ppermute | solution.py:439
  12.3 0.0 copy-start
  12.3 0.9 %copy-done = f32[16,32,128]{2,1,0:T(8,128)S(1)} copy-done((f32[16,32,128]{2,1,0:T(8,128)S(1)}, f32[16,32,128]{2,1,0:T(8,128)}, u32[]{:S(2)}) %copy-start) | copy-done | bytes 262168
  13.3 0.4 shard_map.37
  13.7 0.1 collective-permute-start.2
  13.8 0.7 %collective-permute-start.3 = (f32[3,80,128]{2,1,0:T(8,128)S(1)}, f32[3,80,128]{2,1,0:T(8,128)S(1)}, u32[]{:S(2)}, u32[]{:S(2)}) collective-permute-start(f32[3,80,128]{2,1,0:T(8,128)S(1)} %get-tuple-element.20), channel_id=1, source_target_pairs={{1,2},{2,1},{3,4},{4,3},{5,6},{6,5},{9,10},{10,9},{11,12},{12,11},... | collective-permute-start | bytes 368648 | tf_op jit(solution)/shard_map/ppermute | solution.py:455
  14.4 0.0 copy-done.3
  14.5 0.0 copy-done.2
  14.5 2.3 %shard_map.38 = (f32[3,2,2,9,8,128]{5,4,3,2,1,0:T(8,128)S(1)}, bf16[3,768,256]{2,1,0:T(8,128)(2,1)S(1)}, bf16[3,768,256]{2,1,0:T(8,128)(2,1)S(1)}) custom-call(s32[4,8]{1,0:T(4,128)S(1)} %copy-done.3, f32[9,3,64]{2,1,0:T(4,128)S(1)} %bitcast.11), custom_call_target="tpu_custom_call" | custom-call | tf_op jit(solution)/shard_map/pallas_call | solution.py:442
  16.8 0.0 collective-permute-done.2.first_ref
  16.8 0.0 collective-permute-done.3.second_ref
  16.8 0.0 copy-done.1
  16.8 13.6 %shard_map.39 = (f32[2,16,48,128]{3,2,1,0:T(8,128)S(1)}, f32[2,16,48,128]{3,2,1,0:T(8,128)S(1)}, f32[16,32,128]{2,1,0:T(8,128)S(1)}, f32[16,32,128]{2,1,0:T(8,128)S(1)}, f32[32,128]{1,0:T(8,128)S(1)}) custom-call(f32[16,32,128]{2,1,0:T(8,128)S(1)} %copy-done.1, f32[16,24,128]{2,1,0:T(8,128)S(1)} %collective-permute-done.even_ref, ...), custom_call_target="tpu_custom_call" | custom-call | tf_op jit(solution)/shard_map/pallas_call | solution.py:461
  30.4 15.1 %all_to_all.22 = f32[32,1,128]{2,1,0:T(1,128)S(1)} all-to-all(f32[32,1,128]{2,1,0:T(1,128)S(1)} %bitcast.12), channel_id=1, replica_groups=mesh['gy'=4,'gx'=8] {'gy','gx'}, dimensions={0} | all-to-all | bytes 32768 | tf_op jit(solution)/shard_map/all_to_all | solution.py:467
  45.5 0.9 %shard_map.40 = (f32[16,32,128]{2,1,0:T(8,128)S(1)}, f32[16,32,128]{2,1,0:T(8,128)S(1)}, f32[32,128]{1,0:T(8,128)S(1)}, f32[8,128]{1,0:T(8,128)S(1)}) custom-call(f32[32,128]{1,0:T(8,128)S(1)} %bitcast.9, f32[2,16,48,128]{3,2,1,0:T(8,128)S(1)} %get-tuple-element.25.x1_ref, f32[2,16,48,128]{3,2,1,0:T(8,128)S(1)} %get-tuple-element.26.g1_ref, ...), custom_call_target="tpu_custom_call" | custom-call | tf_op jit(solution)/shard_map/pallas_call | solution.py:469
  46.4 8.8 %all_to_all.23 = f32[32,1,128]{2,1,0:T(1,128)S(1)} all-to-all(f32[32,1,128]{2,1,0:T(1,128)S(1)} %bitcast.13), channel_id=1, replica_groups=mesh['gy'=4,'gx'=8] {'gy','gx'}, dimensions={0} | all-to-all | bytes 32768 | tf_op jit(solution)/shard_map/all_to_all | solution.py:475
  55.3 0.7 %shard_map.41 = f32[16,32,128]{2,1,0:T(8,128)} custom-call(f32[32,128]{1,0:T(8,128)S(1)} %bitcast.10, f32[8,128]{1,0:T(8,128)S(1)} %get-tuple-element.30.keep_ref, f32[16,32,128]{2,1,0:T(8,128)S(1)} %get-tuple-element.31.x2_ref, f32[16,32,128]{2,1,0:T(8,128)S(1)} %get-tuple-element.32.g2_ref), custom_call_target="tpu_custom_call" | custom-call | tf_op jit(solution)/shard_map/pallas_call | solution.py:476
Async XLA Ops:
  0.0 16.8 %copy-start.1 = (f32[16,32,128]{2,1,0:T(8,128)S(1)}, f32[16,32,128]{2,1,0:T(8,128)}, u32[]{:S(2)}) copy-start(f32[16,32,128]{2,1,0:T(8,128)} %tile_ref.3) | copy-start | bytes 786436
  0.0 14.4 %copy-start.3 = (s32[4,8]{1,0:T(4,128)S(1)}, s32[4,8]{1,0:T(4,128)}, u32[]{:S(2)}) copy-start(s32[4,8]{1,0:T(4,128)} %index_ref.1) | copy-start | bytes 388
  0.0 14.4 %copy-start.2 = (f32[64,3,9]{0,1,2:T(4,128)S(1)}, f32[64,3,9]{0,1,2:T(4,128)}, u32[]{:S(2)}) copy-start(f32[64,3,9]{0,1,2:T(4,128)} %param.4) | copy-start | bytes 20740
  1.1 6.6 %collective-permute-start.1 = (f32[16,24,128]{2,1,0:T(8,128)S(1)}, f32[16,24,128]{2,1,0:T(8,128)S(1)}, u32[]{:S(2)}, u32[]{:S(2)}) collective-permute-start(f32[16,24,128]{2,1,0:T(8,128)S(1)} %get-tuple-element.33), channel_id=1, source_target_pairs={{8,16},{16,8},{9,17},{17,9},{10,18},{18,10},{11,19},{19,11},{12,20... | collective-permute-start | bytes 589832 | tf_op jit(solution)/shard_map/ppermute | solution.py:440
  1.8 10.5 %collective-permute-start = (f32[16,24,128]{2,1,0:T(8,128)S(1)}, f32[16,24,128]{2,1,0:T(8,128)S(1)}, u32[]{:S(2)}, u32[]{:S(2)}) collective-permute-start(f32[16,24,128]{2,1,0:T(8,128)S(1)} %get-tuple-element.34), channel_id=1, source_target_pairs={{0,8},{8,0},{16,24},{24,16},{1,9},{9,1},{17,25},{25,17},{2,10},{10... | collective-permute-start | bytes 589832 | tf_op jit(solution)/shard_map/ppermute | solution.py:439
  12.3 1.0 %copy-start = (f32[16,32,128]{2,1,0:T(8,128)S(1)}, f32[16,32,128]{2,1,0:T(8,128)}, u32[]{:S(2)}) copy-start(f32[16,32,128]{2,1,0:T(8,128)} %tile_ref.3) | copy-start | bytes 786436
  13.7 3.1 %collective-permute-start.2 = (f32[3,80,128]{2,1,0:T(8,128)S(1)}, f32[3,80,128]{2,1,0:T(8,128)S(1)}, u32[]{:S(2)}, u32[]{:S(2)}) collective-permute-start(f32[3,80,128]{2,1,0:T(8,128)S(1)} %get-tuple-element.19), channel_id=1, source_target_pairs={{0,1},{1,0},{2,3},{3,2},{4,5},{5,4},{6,7},{7,6},{8,9},{9,8},{10,11... | collective-permute-start | bytes 368648 | tf_op jit(solution)/shard_map/ppermute | solution.py:454
  13.8 3.0 %collective-permute-start.3 = (f32[3,80,128]{2,1,0:T(8,128)S(1)}, f32[3,80,128]{2,1,0:T(8,128)S(1)}, u32[]{:S(2)}, u32[]{:S(2)}) collective-permute-start(f32[3,80,128]{2,1,0:T(8,128)S(1)} %get-tuple-element.20), channel_id=1, source_target_pairs={{1,2},{2,1},{3,4},{4,3},{5,6},{6,5},{9,10},{10,9},{11,12},{12,11},... | collective-permute-start | bytes 368648 | tf_op jit(solution)/shard_map/ppermute | solution.py:455

commit v2 on v1

--- a/solution.py
+++ b/solution.py
@@ -42,7 +42,7 @@
     return lax.axis_index("gy"), lax.axis_index("gx"), lax.axis_size("gy"), lax.axis_size("gx")
 
 
-def weights_kernel(s, index_ref, profiles_ref, taps_ref, forward_ref, backward_ref, full):
+def weights_kernel(s, index_ref, profiles_ref, after_ref, taps_ref, forward_ref, backward_ref, full):
     gy, gx, ny, nx = place()
     breadth, taps, radius = s["breadth"], s["taps"], s["radius"]
     ring = 2 * breadth
@@ -102,7 +102,11 @@
     return group, lane, min(s["halo"], s["breadth"] - lane)
 
 
-def pack_kernel(s, tile_ref, even_ref, odd_ref, first_ref, second_ref):
+def copy_kernel(tile_ref, out_ref):
+    out_ref[...] = tile_ref[...]
+
+
+def pack_kernel(s, tile_ref, even_ref, odd_ref, first_ref, second_ref, centre_ref):
     gy, gx, _, _ = place()
     halo, height, breadth = s["halo"], s["height"], s["breadth"]
     row_even, col_even = lax.rem(gy, 2) == 0, lax.rem(gx, 2) == 0
@@ -117,6 +121,7 @@
                 value = jnp.where(row_even, odd_ref[layer], even_ref[layer])
             else:
                 value = jnp.where(row_even, even_ref[layer], odd_ref[layer])
+            centre_ref[layer, start:start + count, :] = value
             group, begin, here = strip_places(s, layer)
             from_left, from_right = begin, (begin + halo) % breadth
             to_first = pltpu.roll(value, jnp.where(col_even, from_right, from_left), 1)
@@ -204,7 +209,7 @@
             flux_rows[half, layer, start:start + SUB, :] = f_rows[:, part]
 
 
-def main_kernel(s, tile_ref, even_ref, odd_ref, first_ref, second_ref, taps_ref, forward_ref, backward_ref,
+def main_kernel(s, centre_ref, first_ref, second_ref, taps_ref, forward_ref, backward_ref,
                 x1_ref, g1_ref, pull_ref, again_ref, part_ref,
                 x0, x1, x2, g0, y0, y1, y2, r0, r1, r2, q0, q1, q2, acc, div, flux):
     where = place()
@@ -212,7 +217,7 @@
     layers, height, breadth, off = s["layers"], s["height"], s["breadth"], s["off"]
     halo, radius, taps = s["halo"], s["radius"], s["taps"]
     begin, end = s["first"], s["last"]
-    row_even, col_even = lax.rem(gy, 2) == 0, lax.rem(gx, 2) == 0
+    col_even = lax.rem(gx, 2) == 0
     lane = lax.broadcasted_iota(jnp.int32, (1, breadth), 1)
     xs, ys, rs, qs = (x0, x1, x2), (y0, y1, y2), (r0, r1, r2), (q0, q1, q2)
     span = bands(s)
@@ -221,9 +226,7 @@
         return slice(tile * SUB, (tile + 1 if stop is None else stop) * SUB)
 
     top = off - halo
-    x0[0, :, top:off, :] = jnp.where(row_even, odd_ref[...], even_ref[...])
-    x0[0, :, off:off + height, :] = tile_ref[...]
-    x0[0, :, off + height:off + height + halo, :] = jnp.where(row_even, even_ref[...], odd_ref[...])
+    x0[0, :, top:off + height + halo, :] = centre_ref[...]
     firsts = [first_ref[g] for g in range(s["groups"])]
     seconds = [second_ref[g] for g in range(s["groups"])]
     rights = [jnp.where(col_even, a, b) for a, b in zip(firsts, seconds)]
@@ -439,17 +442,20 @@
     from_even = lax.ppermute(to_even, "gy", first_pairs)
     from_odd = lax.ppermute(to_odd, "gy", second_pairs)
 
+    packed = (s["groups"], height + 2 * halo, breadth)
+    tile_here = call(copy_kernel, sds(observed.shape, F32), inputs=[vmem])(observed)
+    first, second, centre = call(
+        functools.partial(pack_kernel, s),
+        (sds(packed, F32), sds(packed, F32), sds((layers, height + 2 * halo, breadth), F32)),
+        inputs=[vmem] * 3,
+    )(tile_here, from_even, from_odd)
     taps_all, forward, backward = call(
         functools.partial(weights_kernel, s),
         (sds((3, 2, 2, taps, SUB, breadth), F32), sds((3, 3 * ring, ring), BF16), sds((3, 3 * ring, ring), BF16)),
         scratch=[pltpu.VMEM((ring, ring), F32)],
-        inputs=[smem, smem],
-    )(tile_index, profiles.transpose(2, 1, 0))
-
-    packed = (s["groups"], height + 2 * halo, breadth)
-    first, second = call(
-        functools.partial(pack_kernel, s), (sds(packed, F32), sds(packed, F32)), inputs=[vmem] * 3
-    )(observed, from_even, from_odd)
+        inputs=[smem, smem, pl.BlockSpec(memory_space=pl.ANY)],
+    )(tile_index, profiles.transpose(2, 1, 0), second)
+    first, taps_all = lax.optimization_barrier((first, taps_all))
     first_pairs, second_pairs = pairings(lax.axis_size("gx"))
     got_first = lax.ppermute(first, "gx", first_pairs)
     got_second = lax.ppermute(second, "gx", second_pairs)
@@ -462,8 +468,8 @@
         functools.partial(main_kernel, s),
         (sds(wide, F32), sds(wide, F32), tile, tile, sds((n, breadth), F32)),
         scratch=[pltpu.VMEM(shape, F32) for shape in [big] * 3 + [big[1:]] + [big] * 12],
-        inputs=[vmem] * 8,
-    )(observed, from_even, from_odd, got_first, got_second, taps_all, forward, backward)
+        inputs=[vmem] * 6,
+    )(centre, got_first, got_second, taps_all, forward, backward)
     sums = lax.all_to_all(part, ("gy", "gx"), 0, 0, tiled=True)
     work = pltpu.VMEM((2, layers, (high - low + 1) * SUB, breadth), F32)
     x2, g2, part, keep = call(

time: 56.2 us -> 54.6 us (0.972)
  blocking collectives: 24 us -> 19.5 us
  starting transfers between devices: 7.33 us -> 10.2 us
    all_to_all x2, blocking collectives: 24 us -> 19.5 us  [per_device(): sums = lax.all_to_all(part, ('gy', 'gx'), 0, 0, tiled=True)]
    ppermute x1, starting transfers between devices: 0.07 us -> 2.91 us  [per_device(): got_first = lax.ppermute(first, 'gx', first_pairs)]
    ppermute x1, waiting for transfers between devices: 4.62 us -> 3.64 us  [per_device(): from_even = lax.ppermute(to_even, 'gy', first_pairs)]
    ppermute x1, waiting for transfers between devices: 0.01 us -> 0.97 us  [per_device(): got_first = lax.ppermute(first, 'gx', first_pairs)]
  transfers between devices with their start and end apart: 4 -> 4, of which waited for: 1 -> 2; matrix products, arithmetic and copies ran while one was open for 0% -> 0% of each run, Pallas kernels for 4% -> 4%
where the time goes in v2:
time: 54.6 us; the launch traced here: 54.4 us
  blocking collectives  19.5 us (36%)
  Pallas kernels  18 us (33%)
  starting transfers between devices  10.2 us (19%)
  waiting for transfers between devices  4.62 us (8%)
  local copies, waits for them, and re-layouts  2.03 us (4%)
    all_to_all x2, blocking collectives, per_device(): sums = lax.all_to_all(part, ('gy', 'gx'), 0, 0, tiled=True)  19.5 us
    pallas_call x1, Pallas kernels, per_device(): call(functools.partial(main_kernel, s), (sds(wide, F32), sds(wide, F32),...  13.5 us
    ppermute x1, starting transfers between devices, per_device(): from_even = lax.ppermute(to_even, 'gy', first_pairs)  5.9 us
    ppermute x1, waiting for transfers between devices, per_device(): from_even = lax.ppermute(to_even, 'gy', first_pairs)  3.64 us
    ppermute x1, starting transfers between devices, per_device(): got_first = lax.ppermute(first, 'gx', first_pairs)  2.91 us
    pallas_call x1, Pallas kernels, per_device(): call(functools.partial(weights_kernel, s), (sds((3, 2, 2, taps, SUB, brea...  2.3 us
  transfers between devices with their start and end apart: 4, of which 2 were waited for; matrix products, arithmetic and copies ran while one was open for 0% of the time, Pallas kernels for 4%

profile of v2, /device:TPU:0, one launch (start us, length us, event | category | flops | bytes accessed | tf_op | source)
XLA Modules:
  0.0 54.4 jit_solution(10420956178250133751)
XLA Ops:
  0.0 0.0 copy-start.2
  0.0 0.0 copy-start.1
  0.0 1.1 %constant_dynamic-slice_fusion = (f32[16,24,128]{2,1,0:T(8,128)S(1)}, f32[16,24,128]{2,1,0:T(8,128)S(1)}) fusion(f32[16,32,128]{2,1,0:T(8,128)} %tile_ref.1, s32[]{:T(128)S(6)} %select_n.10, s32[]{:T(128)S(6)} %select_n.9), kind=kLoop, calls=%fused_computation | loop fusion | bytes 786440 | tf_op jit(solution)/shard_map/dynamic_slice | solution.py:440
  1.1 0.7 %collective-permute-start.1 = (f32[16,24,128]{2,1,0:T(8,128)S(1)}, f32[16,24,128]{2,1,0:T(8,128)S(1)}, u32[]{:S(2)}, u32[]{:S(2)}) collective-permute-start(f32[16,24,128]{2,1,0:T(8,128)S(1)} %get-tuple-element.39), channel_id=1, source_target_pairs={{8,16},{16,8},{9,17},{17,9},{10,18},{18,10},{11,19},{19,11},{12,20... | collective-permute-start | bytes 589832 | tf_op jit(solution)/shard_map/ppermute | solution.py:443
  1.8 5.9 %collective-permute-start = (f32[16,24,128]{2,1,0:T(8,128)S(1)}, f32[16,24,128]{2,1,0:T(8,128)S(1)}, u32[]{:S(2)}, u32[]{:S(2)}) collective-permute-start(f32[16,24,128]{2,1,0:T(8,128)S(1)} %get-tuple-element.40), channel_id=1, source_target_pairs={{0,8},{8,0},{16,24},{24,16},{1,9},{9,1},{17,25},{25,17},{2,10},{10... | collective-permute-start | bytes 589832 | tf_op jit(solution)/shard_map/ppermute | solution.py:442
  7.7 0.0 copy-start
  7.7 0.9 %copy-done = f32[16,32,128]{2,1,0:T(8,128)S(1)} copy-done((f32[16,32,128]{2,1,0:T(8,128)S(1)}, f32[16,32,128]{2,1,0:T(8,128)}, u32[]{:S(2)}) %copy-start) | copy-done | bytes 262168
  8.6 0.0 collective-permute-done.1.odd_ref
  8.6 3.6 %collective-permute-done.even_ref = f32[16,24,128]{2,1,0:T(8,128)S(1)} collective-permute-done((f32[16,24,128]{2,1,0:T(8,128)S(1)}, f32[16,24,128]{2,1,0:T(8,128)S(1)}, u32[]{:S(2)}, u32[]{:S(2)}) %collective-permute-start) | collective-permute-done | bytes 196640 | tf_op jit(solution)/shard_map/ppermute | solution.py:442
  12.3 0.4 shard_map.38
  12.7 0.7 %collective-permute-start.3 = (f32[3,80,128]{2,1,0:T(8,128)S(1)}, f32[3,80,128]{2,1,0:T(8,128)S(1)}, u32[]{:S(2)}, u32[]{:S(2)}) collective-permute-start(f32[3,80,128]{2,1,0:T(8,128)S(1)} %get-tuple-element.24.after_ref), channel_id=1, source_target_pairs={{1,2},{2,1},{3,4},{4,3},{5,6},{6,5},{9,10},{10,9},{11,12},{12,11},... | collective-permute-start | bytes 368648 | tf_op jit(solution)/shard_map/ppermute | solution.py:461
  13.4 0.0 copy-done.2
  13.4 0.0 copy-done.1
  13.4 2.3 %shard_map.39 = (f32[3,2,2,9,8,128]{5,4,3,2,1,0:T(8,128)S(1)}, bf16[3,768,256]{2,1,0:T(8,128)(2,1)S(1)}, bf16[3,768,256]{2,1,0:T(8,128)(2,1)S(1)}) custom-call(s32[4,8]{1,0:T(4,128)S(1)} %copy-done.2, f32[9,3,64]{2,1,0:T(4,128)S(1)} %bitcast.11, f32[3,80,128]{2,1,0:T(8,128)S(1)} %get-tuple-element.24.after_ref), custom_call_target="tpu_custom_call" | custom-call | tf_op jit(solution)/shard_map/pallas_call | solution.py:452
  15.7 2.9 %collective-permute-start.2 = (f32[3,80,128]{2,1,0:T(8,128)S(1)}, f32[3,80,128]{2,1,0:T(8,128)S(1)}, u32[]{:S(2)}, u32[]{:S(2)}) collective-permute-start(f32[3,80,128]{2,1,0:T(8,128)S(1)} %get-tuple-element.26), channel_id=1, source_target_pairs={{0,1},{1,0},{2,3},{3,2},{4,5},{5,4},{6,7},{7,6},{8,9},{9,8},{10,11... | collective-permute-start | bytes 368648 | tf_op jit(solution)/shard_map/ppermute | solution.py:460
  18.6 0.0 collective-permute-done.3.second_ref
  18.6 1.0 %collective-permute-done.2.first_ref = f32[3,80,128]{2,1,0:T(8,128)S(1)} collective-permute-done((f32[3,80,128]{2,1,0:T(8,128)S(1)}, f32[3,80,128]{2,1,0:T(8,128)S(1)}, u32[]{:S(2)}, u32[]{:S(2)}) %collective-permute-start.2) | collective-permute-done | bytes 122912 | tf_op jit(solution)/shard_map/ppermute | solution.py:460
  19.6 13.5 %shard_map.40 = (f32[2,16,48,128]{3,2,1,0:T(8,128)S(1)}, f32[2,16,48,128]{3,2,1,0:T(8,128)S(1)}, f32[16,32,128]{2,1,0:T(8,128)S(1)}, f32[16,32,128]{2,1,0:T(8,128)S(1)}, f32[32,128]{1,0:T(8,128)S(1)}) custom-call(f32[16,80,128]{2,1,0:T(8,128)S(1)} %get-tuple-element.22.centre_ref, f32[3,80,128]{2,1,0:T(8,128)S(1)} %collective-permute-done.2.first_ref, ...), custom_call_target="tpu_custom_call" | custom-call | tf_op jit(solution)/shard_map/pallas_call | solution.py:467
  33.1 10.7 %all_to_all.22 = f32[32,1,128]{2,1,0:T(1,128)S(1)} all-to-all(f32[32,1,128]{2,1,0:T(1,128)S(1)} %bitcast.12), channel_id=1, replica_groups=mesh['gy'=4,'gx'=8] {'gy','gx'}, dimensions={0} | all-to-all | bytes 32768 | tf_op jit(solution)/shard_map/all_to_all | solution.py:473
  43.8 0.9 %shard_map.41 = (f32[16,32,128]{2,1,0:T(8,128)S(1)}, f32[16,32,128]{2,1,0:T(8,128)S(1)}, f32[32,128]{1,0:T(8,128)S(1)}, f32[8,128]{1,0:T(8,128)S(1)}) custom-call(f32[32,128]{1,0:T(8,128)S(1)} %bitcast.9, f32[2,16,48,128]{3,2,1,0:T(8,128)S(1)} %get-tuple-element.31.x1_ref, f32[2,16,48,128]{3,2,1,0:T(8,128)S(1)} %get-tuple-element.32.g1_ref, ...), custom_call_target="tpu_custom_call" | custom-call | tf_op jit(solution)/shard_map/pallas_call | solution.py:475
  44.8 8.8 %all_to_all.23 = f32[32,1,128]{2,1,0:T(1,128)S(1)} all-to-all(f32[32,1,128]{2,1,0:T(1,128)S(1)} %bitcast.13), channel_id=1, replica_groups=mesh['gy'=4,'gx'=8] {'gy','gx'}, dimensions={0} | all-to-all | bytes 32768 | tf_op jit(solution)/shard_map/all_to_all | solution.py:481
  53.6 0.7 %shard_map.42 = f32[16,32,128]{2,1,0:T(8,128)} custom-call(f32[32,128]{1,0:T(8,128)S(1)} %bitcast.10, f32[8,128]{1,0:T(8,128)S(1)} %get-tuple-element.36.keep_ref, f32[16,32,128]{2,1,0:T(8,128)S(1)} %get-tuple-element.37.x2_ref, f32[16,32,128]{2,1,0:T(8,128)S(1)} %get-tuple-element.38.g2_ref), custom_call_target="tpu_custom_call" | custom-call | tf_op jit(solution)/shard_map/pallas_call | solution.py:482
  (1 shorter events, 0.0 us)
Async XLA Ops:
  0.0 13.4 %copy-start.2 = (s32[4,8]{1,0:T(4,128)S(1)}, s32[4,8]{1,0:T(4,128)}, u32[]{:S(2)}) copy-start(s32[4,8]{1,0:T(4,128)} %index_ref.1) | copy-start | bytes 388
  0.0 13.4 %copy-start.1 = (f32[64,3,9]{0,1,2:T(4,128)S(1)}, f32[64,3,9]{0,1,2:T(4,128)}, u32[]{:S(2)}) copy-start(f32[64,3,9]{0,1,2:T(4,128)} %param.4) | copy-start | bytes 20740
  1.1 7.6 %collective-permute-start.1 = (f32[16,24,128]{2,1,0:T(8,128)S(1)}, f32[16,24,128]{2,1,0:T(8,128)S(1)}, u32[]{:S(2)}, u32[]{:S(2)}) collective-permute-start(f32[16,24,128]{2,1,0:T(8,128)S(1)} %get-tuple-element.39), channel_id=1, source_target_pairs={{8,16},{16,8},{9,17},{17,9},{10,18},{18,10},{11,19},{19,11},{12,20... | collective-permute-start | bytes 589832 | tf_op jit(solution)/shard_map/ppermute | solution.py:443
  1.8 10.5 %collective-permute-start = (f32[16,24,128]{2,1,0:T(8,128)S(1)}, f32[16,24,128]{2,1,0:T(8,128)S(1)}, u32[]{:S(2)}, u32[]{:S(2)}) collective-permute-start(f32[16,24,128]{2,1,0:T(8,128)S(1)} %get-tuple-element.40), channel_id=1, source_target_pairs={{0,8},{8,0},{16,24},{24,16},{1,9},{9,1},{17,25},{25,17},{2,10},{10... | collective-permute-start | bytes 589832 | tf_op jit(solution)/shard_map/ppermute | solution.py:442
  7.7 0.9 %copy-start = (f32[16,32,128]{2,1,0:T(8,128)S(1)}, f32[16,32,128]{2,1,0:T(8,128)}, u32[]{:S(2)}) copy-start(f32[16,32,128]{2,1,0:T(8,128)} %tile_ref.1) | copy-start | bytes 786436
  12.7 5.9 %collective-permute-start.3 = (f32[3,80,128]{2,1,0:T(8,128)S(1)}, f32[3,80,128]{2,1,0:T(8,128)S(1)}, u32[]{:S(2)}, u32[]{:S(2)}) collective-permute-start(f32[3,80,128]{2,1,0:T(8,128)S(1)} %get-tuple-element.24.after_ref), channel_id=1, source_target_pairs={{1,2},{2,1},{3,4},{4,3},{5,6},{6,5},{9,10},{10,9},{11,12},{12,11},... | collective-permute-start | bytes 368648 | tf_op jit(solution)/shard_map/ppermute | solution.py:461
  15.7 3.9 %collective-permute-start.2 = (f32[3,80,128]{2,1,0:T(8,128)S(1)}, f32[3,80,128]{2,1,0:T(8,128)S(1)}, u32[]{:S(2)}, u32[]{:S(2)}) collective-permute-start(f32[3,80,128]{2,1,0:T(8,128)S(1)} %get-tuple-element.26), channel_id=1, source_target_pairs={{0,1},{1,0},{2,3},{3,2},{4,5},{5,4},{6,7},{7,6},{8,9},{9,8},{10,11... | collective-permute-start | bytes 368648 | tf_op jit(solution)/shard_map/ppermute | solution.py:460

commit v3 on v2

v3 whole, which is shorter than its diff:
```python
import functools
import jax
import jax.numpy as jnp
from jax import lax
from jax.experimental import pallas as pl
from jax.experimental.pallas import tpu as pltpu
from jax.sharding import PartitionSpec as P

ITERS = 2
WEIGHT_TV = 0.02
SMOOTHING = 0.1
DAMPING = 0.05
START_STEP = 0.5
SUB = 8
F32 = jnp.float32
BF16 = jnp.bfloat16
VMEM_BYTES = 36 * 1024 * 1024


def plan(layers, height, breadth, taps):
    radius = (taps - 1) // 2
    halo = 6 * radius
    off = -(-halo // SUB) * SUB + SUB
    return dict(
        layers=layers, height=height, breadth=breadth, taps=taps, radius=radius, halo=halo, off=off,
        rows=height + 2 * off, groups=-(-layers * halo // breadth), pairs=layers // 2, planes=layers + layers // 2, quarter=breadth // 4, first=off // SUB, last=(off + height) // SUB,
        tiles=(height + 2 * off) // SUB,
    )


def reach(s, extent):
    low = (s["off"] - extent) // SUB
    high = -(-(s["off"] + s["height"] + extent) // SUB)
    return low, high


def bands(s):
    return ((0, s["first"]), (s["first"], s["last"]), (s["last"], s["tiles"]))


def place():
    return lax.axis_index("gy"), lax.axis_index("gx"), lax.axis_size("gy"), lax.axis_size("gx")


def column_of(s, place, member):
    breadth, quarter = s["breadth"], s["quarter"]
    side = place - breadth
    right, left = (0, 3 * quarter) if member == 0 else (2 * quarter, quarter)
    column = jnp.where((side >= right) & (side < right + quarter), breadth + side - right, 1 << 20)
    column = jnp.where((side >= left) & (side < left + quarter), side - left - quarter, column)
    return jnp.where(place < breadth, place, column)


def weights_kernel(s, index_ref, profiles_ref, taps_ref, columns_ref):
    gy, gx, ny, nx = place()
    breadth, taps = s["breadth"], s["taps"]
    lane = lax.broadcasted_iota(jnp.int32, (SUB, breadth), 1)
    is_right = lax.rem(lane // s["quarter"], 2) == 0
    for band in range(3):
        row = gy + (band - 1)
        picked = []
        for side in range(3):
            col = gx + (side - 1)
            inside = (row >= 0) & (row < ny) & (col >= 0) & (col < nx)
            number = index_ref[jnp.clip(row, 0, ny - 1), jnp.clip(col, 0, nx - 1)]
            picked.append((inside, number))
        for dim in range(3):
            for tap in range(taps):
                left, centre, right = [
                    jnp.where(inside, profiles_ref[tap, dim, number], 0.0) for inside, number in picked
                ]
                own, side = jnp.full((SUB, breadth), centre, F32), jnp.where(is_right, right, left)
                if dim < 2:
                    taps_ref[band, dim, 0, tap] = own
                    taps_ref[band, dim, 1, tap] = side
                else:
                    columns_ref[band, tap] = jnp.concatenate([own, side], axis=1)


def matrices_kernel(s, columns_ref, after_ref, forward_ref, backward_ref, full):
    breadth, taps, radius = s["breadth"], s["taps"], s["radius"]
    ring = 2 * breadth
    chunk = 32
    target = lax.broadcasted_iota(jnp.int32, (1, ring), 1)
    for number in range(6):
        band, member = divmod(number, 2)
        columns = [columns_ref[band, t, :1, :] for t in range(taps)]
        reached = column_of(s, target, member)
        reached = jnp.where(reached < 1 << 19, reached + radius, -(1 << 20))
        for start in range(0, ring, chunk):
            source = lax.broadcasted_iota(jnp.int32, (chunk, 1), 0) + start
            distance = reached - column_of(s, source, member)
            total = jnp.zeros((chunk, ring), F32)
            for tap in range(taps):
                total = jnp.where(distance == tap, columns[tap], total)
            full[start:start + chunk, :] = total
        matrix = full[...]
        for ref, value in ((forward_ref, matrix), (backward_ref, matrix.T)):
            upper = value.astype(BF16)
            ref[number, :ring, :] = upper
            ref[number, ring:2 * ring, :] = (value - upper.astype(F32)).astype(BF16)
            ref[number, 2 * ring:, :] = upper


def strip_places(s, layer):
    group, lane = divmod(layer * s["halo"], s["breadth"])
    return group, lane, min(s["halo"], s["breadth"] - lane)


def copy_kernel(tile_ref, out_ref):
    out_ref[...] = tile_ref[...]


def pack_kernel(s, tile_ref, even_ref, odd_ref, after_ref, first_ref, second_ref, centre_ref):
    gy, gx, _, _ = place()
    halo, height, breadth = s["halo"], s["height"], s["breadth"]
    row_even, col_even = lax.rem(gy, 2) == 0, lax.rem(gx, 2) == 0
    lane = lax.broadcasted_iota(jnp.int32, (1, breadth), 1)
    for start, count in ((0, halo), (halo, height), (halo + height, halo)):
        first = [jnp.zeros((count, breadth), F32)] * s["groups"]
        second = list(first)
        for layer in range(s["layers"]):
            if start == halo:
                value = tile_ref[layer]
            elif start == 0:
                value = jnp.where(row_even, odd_ref[layer], even_ref[layer])
            else:
                value = jnp.where(row_even, even_ref[layer], odd_ref[layer])
            centre_ref[layer, start:start + count, :] = value
            group, begin, here = strip_places(s, layer)
            from_left, from_right = begin, (begin + halo) % breadth
            to_first = pltpu.roll(value, jnp.where(col_even, from_right, from_left), 1)
            to_second = pltpu.roll(value, jnp.where(col_even, from_left, from_right), 1)
            parts = [(group, (lane >= begin) & (lane < begin + here))]
            if here < halo:
                parts.append((group + 1, lane < halo - here))
            for number, mine in parts:
                first[number] = jnp.where(mine, to_first, first[number])
                second[number] = jnp.where(mine, to_second, second[number])
        for number in range(s["groups"]):
            first_ref[number, start:start + count, :] = first[number]
            second_ref[number, start:start + count, :] = second[number]


def unpack_layer(s, groups, layer, to):
    breadth = s["breadth"]
    lane = lax.broadcasted_iota(jnp.int32, (1, breadth), 1)
    group, begin, here = strip_places(s, layer)
    value = groups[group]
    if here < s["halo"]:
        value = jnp.where(lane >= begin, value, groups[group + 1])
    shift = (to - begin) % breadth
    return pltpu.roll(value, shift, 1) if shift else value


def first_lanes(s):
    lane = lax.broadcasted_iota(jnp.int32, (1, s["breadth"]), 1)
    return (lane < s["quarter"]) | (lane >= 3 * s["quarter"])


def swap_layers(s, value):
    return pltpu.roll(value, 2 * s["quarter"], 1)


def weighted(taps, values):
    total = None
    for tap, value in zip(taps, values):
        if value is not None:
            total = tap * value if total is None else total + tap * value
    return total


def row_depth(s, load, side, row_taps, depth_taps, transposed):
    layers, taps, radius, pairs = s["layers"], s["taps"], s["radius"], s["pairs"]
    shifts = [t - radius if transposed else radius - t for t in range(taps)]
    base, count = (layers, pairs) if side else (0, layers)
    mixed = [weighted(row_taps, [load(base + p, shift) for shift in shifts]) for p in range(count)]
    beyond = {}
    if side:
        first = first_lanes(s)
        for step in range(1, radius + 1):
            beyond[-step] = jnp.where(first, 0.0, swap_layers(s, mixed[pairs - step]))
            beyond[pairs - 1 + step] = jnp.where(first, swap_layers(s, mixed[step - 1]), 0.0)
    at = lambda p: mixed[p] if 0 <= p < count else beyond.get(p)
    return [weighted(depth_taps, [at(p + shift) for shift in shifts]) for p in range(count)]


def slope_tile(s, source, shift, tile, divergence, flux_rows, where):
    gy, gx, ny, nx = where
    layers, height, breadth, pairs, quarter = s["layers"], s["height"], s["breadth"], s["pairs"], s["quarter"]
    lane = lax.broadcasted_iota(jnp.int32, (SUB, breadth), 1)
    side_col = jnp.where(lax.rem(lane // quarter, 2) == 0, breadth + lax.rem(lane, quarter), lax.rem(lane, quarter) - quarter)
    masks = []
    for col in (lane, side_col):
        col = gx * breadth + col
        masks.append(jnp.where((col >= 0) & (col < nx * breadth - 1), 1.0, 0.0).astype(F32))
    start = tile * SUB
    row = gy * height + start - s["off"] + shift + lax.broadcasted_iota(jnp.int32, (SUB, breadth), 0)
    row_mask = jnp.where((row >= 0) & (row < ny * height - 1), 1.0, 0.0).astype(F32)
    last, first = breadth - 1, first_lanes(s)
    rows = slice(start, start + SUB)

    def swap(value):
        return swap_layers(s, value)

    before = [None, None, None]
    heres = [source[plane, rows, :] for plane in (0, pairs, layers)]
    for p in range(pairs):
        planes = (p, p + pairs, layers + p)
        afters = [source[plane + 1, rows, :] if p + 1 < pairs else None for plane in planes]
        if p + 1 == pairs:
            afters[0] = source[pairs, rows, :]
            afters[2] = jnp.where(first, swap(source[layers, rows, :]), heres[2])
        rolled = [pltpu.roll(value, breadth - 1, 1) for value in heres]
        nexts = [
            jnp.where(lane == last, rolled[2], rolled[0]),
            jnp.where(lane == last, swap(rolled[2]), rolled[1]),
            jnp.where(lane == last, rolled[0], jnp.where(lane == 2 * quarter - 1, swap(rolled[1]), rolled[2])),
        ]
        f_cols, totals = [], []
        for k, plane in enumerate(planes):
            here = heres[k]
            step_rows = (source[plane, start + 1:start + 1 + SUB, :] - here) * row_mask
            step_cols = (nexts[k] - here) * masks[k // 2]
            square = step_rows * step_rows + step_cols * step_cols + SMOOTHING * SMOOTHING
            if afters[k] is not None:
                step_depth = afters[k] - here
                square = square + step_depth * step_depth
            inverse = lax.rsqrt(square)
            f_rows = step_rows * inverse
            flux_rows[plane, rows, :] = f_rows
            f_cols.append(step_cols * inverse)
            total = -f_cols[k] - f_rows
            if before[k] is not None:
                total = total + before[k]
            before[k] = None
            if afters[k] is not None:
                before[k] = step_depth * inverse
                total = total - before[k]
            totals.append(total)
        rolled = [pltpu.roll(value, 1, 1) for value in f_cols]
        totals[0] = totals[0] + jnp.where(lane == 0, rolled[2], rolled[0])
        totals[1] = totals[1] + jnp.where(lane == 0, swap(rolled[2]), rolled[1])
        totals[2] = totals[2] + jnp.where(lane == 0, rolled[0], jnp.where(lane == 2 * quarter, swap(rolled[1]), rolled[2]))
        for plane, total in zip(planes, totals):
            divergence[plane, rows, :] = total
        heres = afters
    divergence[pairs, rows, :] = divergence[pairs, rows, :] + before[0]
    divergence[layers, rows, :] = divergence[layers, rows, :] + jnp.where(first, 0.0, swap(before[2]))


def main_kernel(s, centre_ref, first_ref, second_ref, taps_ref, forward_ref, backward_ref,
                x1_ref, g1_ref, pull_ref, again_ref, part_ref,
                x0, x1, x2, g0, y0, y1, y2, r0, r1, r2, q0, q1, q2, acc, div, flux):
    where = place()
    gy, gx, ny, nx = where
    layers, height, breadth, off = s["layers"], s["height"], s["breadth"], s["off"]
    halo, radius, taps, pairs, planes, quarter = [s[k] for k in ("halo", "radius", "taps", "pairs", "planes", "quarter")]
    begin, end = s["first"], s["last"]
    col_even = lax.rem(gx, 2) == 0
    lane = lax.broadcasted_iota(jnp.int32, (1, breadth), 1)
    xs, ys, rs, qs = (x0, x1, x2), (y0, y1, y2), (r0, r1, r2), (q0, q1, q2)
    span = bands(s)

    def rows(tile, stop=None):
        return slice(tile * SUB, (tile + 1 if stop is None else stop) * SUB)

    top = off - halo
    x0[:layers, top:off + height + halo, :] = centre_ref[...]
    firsts = [first_ref[g] for g in range(s["groups"])]
    seconds = [second_ref[g] for g in range(s["groups"])]
    rights = [jnp.where(col_even, a, b) for a, b in zip(firsts, seconds)]
    lefts = [jnp.where(col_even, b, a) for a, b in zip(firsts, seconds)]
    for p in range(pairs):
        value = jnp.zeros((height + 2 * halo, breadth), F32)
        for groups, layer, to in ((rights, p, 0), (lefts, p + pairs, 2 * quarter - halo),
                                  (rights, p + pairs, 2 * quarter), (lefts, p, breadth - halo)):
            value = jnp.where((lane >= to) & (lane < to + halo), unpack_layer(s, groups, layer, to), value)
        x0[layers + p, top:off + height + halo, :] = value
    zero = jnp.zeros((planes, SUB, breadth), F32)
    for ref, tiles in ((y0, (0,)), (y2, (s["tiles"] - 1,)), (r0, (begin, begin + 1)),
                       (r1, (begin - 2, begin - 1, end, end + 1)), (r2, (end - 2, end - 1))):
        for tile in tiles:
            ref[:, rows(tile), :] = zero

    def product(ref, low, high, band, matrices):
        count = (high - low) * SUB

        def split(a, b):
            value = ref[a:b, rows(low, high), :].reshape((b - a) * count, breadth)
            upper = value.astype(BF16)
            return upper, (value - upper.astype(F32)).astype(BF16)

        side_high, side_low = split(layers, planes)
        own, side = [], None
        for member in range(2):
            high_part, low_part = split(member * pairs, (member + 1) * pairs)
            parts = [high_part, side_high] * 2 + [low_part, side_low]
            result = jnp.dot(jnp.concatenate(parts, axis=1), matrices[2 * band + member], preferred_element_type=F32)
            own.append(result[:, :breadth].reshape(pairs, count, breadth))
            rest = result[:, breadth:]
            side = rest if side is None else side + rest
        return [(0, own[0]), (pairs, own[1]), (layers, side.reshape(pairs, count, breadth))]

    def taps_of(band, half):
        return [[taps_ref[band, dim, half, t] for t in range(taps)] for dim in (1, 0)]

    def one_pass(number):
        x = xs[number]
        low, high = reach(s, (5 - 2 * number) * radius)
        in_low, in_high = reach(s, (6 - 2 * number) * radius)
        back_low, back_high = reach(s, (4 - 2 * number) * radius)
        out = [(max(low, a), min(high, b)) for a, b in span]
        back = [(max(back_low, a - 1), min(back_high, b + 1)) for a, b in span]
        done = set()

        def columns(band):
            a, b = max(out[band][0] - 1, in_low), min(out[band][1] + 1, in_high)
            for plane, piece in product(x, a, b, band, forward_ref):
                ys[band][plane:plane + pairs, rows(a, b), :] = piece

        def blur_rows(band):
            for tile in range(*out[band]):
                for side in range(2):
                    load = lambda plane, shift: ys[band][plane, tile * SUB + shift:(tile + 1) * SUB + shift, :]
                    for plane, value in enumerate(row_depth(s, load, side, *taps_of(band, side), False), side * layers):
                        if number < 2:
                            value = value - x0[plane, rows(tile), :]
                        rs[band][plane, rows(tile), :] = value

        def back_rows(band):
            for tile in range(*back[band]):
                for side in range(2):
                    load = lambda plane, shift: rs[band][plane, tile * SUB + shift:(tile + 1) * SUB + shift, :]
                    for plane, value in enumerate(row_depth(s, load, side, *taps_of(band, side), True), side * layers):
                        qs[band][plane, rows(tile), :] = value

        def back_columns(band):
            a, b = back[band]
            for plane, piece in product(qs[band], a, b, band, backward_ref):
                for tile in range(a, b):
                    part = piece[:, (tile - a) * SUB:(tile - a + 1) * SUB, :]
                    at = slice(plane, plane + pairs)
                    acc[at, rows(tile), :] = acc[at, rows(tile), :] + part if tile in done else part
            done.update(range(a, b))

        def inside(tile, side):
            row = gy * height + tile * SUB - off + lax.broadcasted_iota(jnp.int32, (SUB, breadth), 0)
            here = lax.broadcasted_iota(jnp.int32, (SUB, breadth), 1)
            if side:
                part = lax.rem(here, quarter)
                here = jnp.where(lax.rem(here // quarter, 2) == 0, breadth + part, part - quarter)
            col = gx * breadth + here
            return (row >= 0) & (row < ny * height) & (col >= 0) & (col < nx * breadth)

        def update(tile):
            keep = [inside(tile, side) for side in range(2)]
            for plane in range(planes):
                here = x[plane, rows(tile), :]
                total = acc[plane, rows(tile), :] + DAMPING * here
                before = flux[plane, tile * SUB - 1:(tile + 1) * SUB - 1, :]
                total = total + WEIGHT_TV * (div[plane, rows(tile), :] + before)
                total = jnp.where(keep[plane // layers], total, 0.0)
                if number == 0:
                    xs[1][plane, rows(tile), :] = here - START_STEP * total
                    if plane < layers and begin <= tile < end:
                        g0[plane, rows(tile), :] = total
                else:
                    xs[2][plane, rows(tile), :] = total

        def slopes(a, b):
            if number < 2:
                for tile in range(a, b):
                    slope_tile(s, x, 0, tile, div, flux, where)

        middle = (begin + end) // 2
        columns(0)
        slopes(back_low - 1, middle)
        columns(1)
        blur_rows(0)
        columns(2)
        back_rows(0)
        blur_rows(1)
        back_columns(0)
        back_rows(1)
        back_columns(1)
        blur_rows(2)
        slopes(middle, back_high)
        back_rows(2)
        back_columns(2)
        if number == 1:
            pull_ref[...] = acc[:layers, rows(begin, end), :]
        if number < 2:
            for tile in range(back_low, back_high):
                update(tile)

    for number in range(3):
        one_pass(number)
    again_ref[...] = acc[:layers, rows(begin, end), :]
    low, high = reach(s, 2 * radius)
    x1_ref[...] = x1[:, rows(low, high), :]
    g1_ref[...] = x2[:, rows(low, high), :]

    zero_sq = cross = one_sq = jnp.zeros((SUB, breadth), F32)
    for tile in range(begin, end):
        for layer in range(layers):
            a, b = g0[layer, rows(tile), :], x2[layer, rows(tile), :]
            zero_sq, cross, one_sq = zero_sq + a * a, cross + a * (b - a), one_sq + b * b
    zero_sq, cross, one_sq = [jnp.sum(t, axis=(0, 1), keepdims=True) for t in (zero_sq, cross, one_sq)]
    row = jnp.where(lane == 0, zero_sq, jnp.where(lane == 1, cross, one_sq))
    part_ref[...] = jnp.broadcast_to(row, part_ref.shape)


def step_kernel(s, sums_ref, x1_ref, g1_ref, pull_ref, again_ref, x2_ref, g2_ref, part_ref, keep_ref, x2, div, flux):
    where = place()
    layers, height, breadth = s["layers"], s["height"], s["breadth"]
    low, high = reach(s, 2 * s["radius"])
    lane = lax.broadcasted_iota(jnp.int32, (1, breadth), 1)
    total = jnp.sum(sums_ref[...], axis=0, keepdims=True)
    zero_sq, cross, one_sq = [
        jnp.sum(jnp.where(lane == number, total, 0.0), axis=(0, 1), keepdims=True) for number in range(3)
    ]
    step = (START_STEP * START_STEP * zero_sq) / (-START_STEP * cross)
    count = (high - low) * SUB
    for plane in range(s["planes"]):
        x2[plane, :count, :] = x1_ref[plane] - step * g1_ref[plane]
    begin = s["first"] - low
    total = jnp.zeros((SUB, breadth), F32)
    for tile in range(begin - 1, begin + height // SUB):
        slope_tile(s, x2, low * SUB, tile, div, flux, where)
        if tile < begin:
            continue
        at, out = slice(tile * SUB, (tile + 1) * SUB), slice((tile - begin) * SUB, (tile - begin + 1) * SUB)
        for layer in range(layers):
            here = x2[layer, at, :]
            slope = pull_ref[layer, out, :] - step * again_ref[layer, out, :] + DAMPING * here
            slope = slope + WEIGHT_TV * (div[layer, at, :] + flux[layer, tile * SUB - 1:(tile + 1) * SUB - 1, :])
            x2_ref[layer, out, :] = here
            g2_ref[layer, out, :] = slope
            old = g1_ref[layer, at, :]
            total = total + old * (slope - old)
    growth = -step * jnp.sum(total, axis=(0, 1), keepdims=True)
    part_ref[...] = jnp.broadcast_to(growth, part_ref.shape)
    keep_ref[...] = jnp.broadcast_to(step * step * one_sq, keep_ref.shape)


def final_kernel(sums_ref, keep_ref, x2_ref, g2_ref, out_ref):
    step = keep_ref[:1, :] / jnp.sum(sums_ref[...], axis=0, keepdims=True)
    for layer in range(x2_ref.shape[0]):
        out_ref[layer] = x2_ref[layer] - step * g2_ref[layer]


def pairings(count):
    def both(start):
        pairs = []
        for i in range(start, count - 1, 2):
            pairs += [(i, i + 1), (i + 1, i)]
        return pairs

    return both(0), both(1)


def call(kernel, outs, scratch=(), inputs=None):
    whole = pl.BlockSpec(memory_space=pltpu.VMEM)
    return pl.pallas_call(
        kernel,
        out_shape=outs,
        in_specs=inputs,
        out_specs=jax.tree.map(lambda _: whole, outs),
        scratch_shapes=list(scratch),
        compiler_params=pltpu.CompilerParams(vmem_limit_bytes=VMEM_BYTES),
    )


def per_device(observed, profiles, tile_index):
    layers, height, breadth = observed.shape
    s = plan(layers, height, breadth, profiles.shape[2])
    halo, rows, taps = s["halo"], s["rows"], s["taps"]
    ring = 2 * breadth
    gy = lax.axis_index("gy")
    n = lax.axis_size("gy") * lax.axis_size("gx")
    vmem, smem = pl.BlockSpec(memory_space=pltpu.VMEM), pl.BlockSpec(memory_space=pltpu.SMEM)
    sds = jax.ShapeDtypeStruct

    even = lax.rem(gy, 2) == 0
    bottom, top = jnp.int32(height - halo), jnp.int32(0)
    to_even = lax.dynamic_slice_in_dim(observed, jnp.where(even, bottom, top), halo, axis=1)
    to_odd = lax.dynamic_slice_in_dim(observed, jnp.where(even, top, bottom), halo, axis=1)
    first_pairs, second_pairs = pairings(lax.axis_size("gy"))
    from_even = lax.ppermute(to_even, "gy", first_pairs)
    from_odd = lax.ppermute(to_odd, "gy", second_pairs)

    packed = (s["groups"], height + 2 * halo, breadth)
    anywhere = pl.BlockSpec(memory_space=pl.ANY)
    taps_all, columns = call(
        functools.partial(weights_kernel, s),
        (sds((3, 2, 2, taps, SUB, breadth), F32), sds((3, taps, SUB, ring), F32)), inputs=[smem, smem],
    )(tile_index, profiles.transpose(2, 1, 0))
    tile_here = call(copy_kernel, sds(observed.shape, F32), inputs=[vmem])(observed)
    first, second, centre = call(
        functools.partial(pack_kernel, s),
        (sds(packed, F32), sds(packed, F32), sds((layers, height + 2 * halo, breadth), F32)),
        inputs=[vmem] * 3 + [anywhere],
    )(tile_here, from_even, from_odd, taps_all)
    matrices = sds((6, 3 * ring, ring), BF16)
    forward, backward = call(
        functools.partial(matrices_kernel, s), (matrices, matrices),
        scratch=[pltpu.VMEM((ring, ring), F32)], inputs=[vmem, anywhere],
    )(columns, second)
    first, backward = lax.optimization_barrier((first, backward))
    first_pairs, second_pairs = pairings(lax.axis_size("gx"))
    got_first = lax.ppermute(first, "gx", first_pairs)
    got_second = lax.ppermute(second, "gx", second_pairs)

    big = (s["planes"], rows, breadth)
    low, high = reach(s, 2 * s["radius"])
    wide = (s["planes"], (high - low) * SUB, breadth)
    tile = sds((layers, height, breadth), F32)
    x1, g1, pull, again, part = call(
        functools.partial(main_kernel, s),
        (sds(wide, F32), sds(wide, F32), tile, tile, sds((n, breadth), F32)),
        scratch=[pltpu.VMEM(shape, F32) for shape in [big] * 3 + [(layers, rows, breadth)] + [big] * 12],
        inputs=[vmem] * 6,
    )(centre, got_first, got_second, taps_all, forward, backward)
    sums = lax.all_to_all(part, ("gy", "gx"), 0, 0, tiled=True)
    work = pltpu.VMEM((s["planes"], (high - low + 1) * SUB, breadth), F32)
    x2, g2, part, keep = call(
        functools.partial(step_kernel, s),
        (tile, tile, sds((n, breadth), F32), sds((SUB, breadth), F32)),
        scratch=[work] * 3,
        inputs=[vmem] * 5,
    )(sums, x1, g1, pull, again)
    sums = lax.all_to_all(part, ("gy", "gx"), 0, 0, tiled=True)
    return call(final_kernel, tile, inputs=[vmem] * 4)(sums, keep, x2, g2)


def solution(mesh):
    in_specs = (P(None, "gy", "gx"), P(), P())
    out_specs = P(None, "gy", "gx")
    return jax.shard_map(
        per_device, mesh=mesh, in_specs=in_specs, out_specs=out_specs, check_vma=False
    )
```

time: 54.6 us -> 51.7 us (0.947)
  Pallas kernels: 18 us -> 14.9 us
  waiting for transfers between devices: 4.62 us -> 2.04 us
  local copies, waits for them, and re-layouts: 2.03 us -> 3.4 us
  blocking collectives: 19.5 us -> 20.8 us
    pallas_call x1, Pallas kernels: 13.5 us -> 10.7 us  [per_device(): call(functools.partial(main_kernel, s), (sds(wide, F32), sds(wide, F32),...]
    ppermute x1, waiting for transfers between devices: 3.64 us -> 1.06 us  [per_device(): from_even = lax.ppermute(to_even, 'gy', first_pairs)]
    unnamed x6, local copies, waits for them, and re-layouts: 0.96 us -> 2.35 us
    all_to_all x2, blocking collectives: 19.5 us -> 20.8 us  [per_device(): sums = lax.all_to_all(part, ('gy', 'gx'), 0, 0, tiled=True)]
    pallas_call x1, Pallas kernels: 2.3 us -> 1.16 us  [per_device(): call(functools.partial(weights_kernel, s), (sds((3, 2, 2, taps, SUB, brea...]
    pallas_call x0 -> x1, Pallas kernels: none -> 1.07 us  [per_device(): call(functools.partial(matrices_kernel, s), (matrices, matrices), scratch...]
where the time goes in v3:
time: 51.7 us; the launch traced here: 51.4 us
  blocking collectives  20.8 us (40%)
  Pallas kernels  14.9 us (29%)
  starting transfers between devices  10.2 us (20%)
  local copies, waits for them, and re-layouts  3.4 us (7%)
  waiting for transfers between devices  2.04 us (4%)
    all_to_all x2, blocking collectives, per_device(): sums = lax.all_to_all(part, ('gy', 'gx'), 0, 0, tiled=True)  20.8 us
    pallas_call x1, Pallas kernels, per_device(): call(functools.partial(main_kernel, s), (sds(wide, F32), sds(wide, F32),...  10.7 us
    ppermute x1, starting transfers between devices, per_device(): from_even = lax.ppermute(to_even, 'gy', first_pairs)  5.9 us
    ppermute x1, starting transfers between devices, per_device(): got_first = lax.ppermute(first, 'gx', first_pairs)  2.91 us
    unnamed x6, local copies, waits for them, and re-layouts  2.35 us
    pallas_call x1, Pallas kernels, per_device(): call(functools.partial(weights_kernel, s), (sds((3, 2, 2, taps, SUB, brea...  1.16 us
    pallas_call x1, Pallas kernels, per_device(): call(functools.partial(matrices_kernel, s), (matrices, matrices), scratch...  1.07 us
    ppermute x1, waiting for transfers between devices, per_device(): from_even = lax.ppermute(to_even, 'gy', first_pairs)  1.06 us
  transfers between devices with their start and end apart: 4, of which 2 were waited for; matrix products, arithmetic and copies ran while one was open for 0% of the time, Pallas kernels for 4%

profile of v3, /device:TPU:0, one launch (start us, length us, event | category | flops | bytes accessed | tf_op | source)
XLA Modules:
  0.0 51.4 jit_solution(14401939835665619117)
XLA Ops:
  0.0 1.1 %constant_dynamic-slice_fusion = (f32[16,24,128]{2,1,0:T(8,128)S(1)}, f32[16,24,128]{2,1,0:T(8,128)S(1)}) fusion(f32[16,32,128]{2,1,0:T(8,128)} %tile_ref.1, s32[]{:T(128)S(6)} %select_n.10, s32[]{:T(128)S(6)} %select_n.9), kind=kLoop, calls=%fused_computation | loop fusion | bytes 786440 | tf_op jit(solution)/shard_map/dynamic_slice | solution.py:488
  1.1 0.7 %collective-permute-start.1 = (f32[16,24,128]{2,1,0:T(8,128)S(1)}, f32[16,24,128]{2,1,0:T(8,128)S(1)}, u32[]{:S(2)}, u32[]{:S(2)}) collective-permute-start(f32[16,24,128]{2,1,0:T(8,128)S(1)} %get-tuple-element.41), channel_id=1, source_target_pairs={{8,16},{16,8},{9,17},{17,9},{10,18},{18,10},{11,19},{19,11},{12,20... | collective-permute-start | bytes 589832 | tf_op jit(solution)/shard_map/ppermute | solution.py:491
  1.7 5.9 %collective-permute-start = (f32[16,24,128]{2,1,0:T(8,128)S(1)}, f32[16,24,128]{2,1,0:T(8,128)S(1)}, u32[]{:S(2)}, u32[]{:S(2)}) collective-permute-start(f32[16,24,128]{2,1,0:T(8,128)S(1)} %get-tuple-element.42), channel_id=1, source_target_pairs={{0,8},{8,0},{16,24},{24,16},{1,9},{9,1},{17,25},{25,17},{2,10},{10... | collective-permute-start | bytes 589832 | tf_op jit(solution)/shard_map/ppermute | solution.py:490
  7.6 0.0 copy-start
  7.6 0.9 %copy-done = f32[16,32,128]{2,1,0:T(8,128)S(1)} copy-done((f32[16,32,128]{2,1,0:T(8,128)S(1)}, f32[16,32,128]{2,1,0:T(8,128)}, u32[]{:S(2)}) %copy-start) | copy-done | bytes 262168
  8.6 0.0 copy-start.1
  8.6 0.7 %copy-done.1 = f32[64,3,9]{0,1,2:T(4,128)S(1)} copy-done((f32[64,3,9]{0,1,2:T(4,128)S(1)}, f32[64,3,9]{0,1,2:T(4,128)}, u32[]{:S(2)}) %copy-start.1) | copy-done | bytes 6936
  9.3 0.0 copy-start.2
  9.3 0.7 %copy-done.2 = s32[4,8]{1,0:T(4,128)S(1)} copy-done((s32[4,8]{1,0:T(4,128)S(1)}, s32[4,8]{1,0:T(4,128)}, u32[]{:S(2)}) %copy-start.2) | copy-done | bytes 152
  10.0 1.2 %shard_map.38 = (f32[3,2,2,9,8,128]{5,4,3,2,1,0:T(8,128)S(1)}, f32[3,9,8,256]{3,2,1,0:T(8,128)S(1)}) custom-call(s32[4,8]{1,0:T(4,128)S(1)} %copy-done.2, f32[9,3,64]{2,1,0:T(4,128)S(1)} %bitcast.11), custom_call_target="tpu_custom_call" | custom-call | tf_op jit(solution)/shard_map/pallas_call | solution.py:495
  11.2 0.0 collective-permute-done.1.odd_ref
  11.2 1.1 %collective-permute-done.even_ref = f32[16,24,128]{2,1,0:T(8,128)S(1)} collective-permute-done((f32[16,24,128]{2,1,0:T(8,128)S(1)}, f32[16,24,128]{2,1,0:T(8,128)S(1)}, u32[]{:S(2)}, u32[]{:S(2)}) %collective-permute-start) | collective-permute-done | bytes 196640 | tf_op jit(solution)/shard_map/ppermute | solution.py:490
  12.3 0.4 shard_map.39
  12.7 0.7 %collective-permute-start.3 = (f32[3,80,128]{2,1,0:T(8,128)S(1)}, f32[3,80,128]{2,1,0:T(8,128)S(1)}, u32[]{:S(2)}, u32[]{:S(2)}) collective-permute-start(f32[3,80,128]{2,1,0:T(8,128)S(1)} %get-tuple-element.27.after_ref), channel_id=1, source_target_pairs={{1,2},{2,1},{3,4},{4,3},{5,6},{6,5},{9,10},{10,9},{11,12},{12,11},... | collective-permute-start | bytes 368648 | tf_op jit(solution)/shard_map/ppermute | solution.py:513
  13.4 1.1 %shard_map.40 = (bf16[6,768,256]{2,1,0:T(8,128)(2,1)S(1)}, bf16[6,768,256]{2,1,0:T(8,128)(2,1)S(1)}) custom-call(f32[3,9,8,256]{3,2,1,0:T(8,128)S(1)} %get-tuple-element.26.columns_ref, f32[3,80,128]{2,1,0:T(8,128)S(1)} %get-tuple-element.27.after_ref), custom_call_target="tpu_custom_call" | custom-call | tf_op jit(solution)/shard_map/pallas_call | solution.py:506
  14.4 2.9 %collective-permute-start.2 = (f32[3,80,128]{2,1,0:T(8,128)S(1)}, f32[3,80,128]{2,1,0:T(8,128)S(1)}, u32[]{:S(2)}, u32[]{:S(2)}) collective-permute-start(f32[3,80,128]{2,1,0:T(8,128)S(1)} %get-tuple-element.29), channel_id=1, source_target_pairs={{0,1},{1,0},{2,3},{3,2},{4,5},{5,4},{6,7},{7,6},{8,9},{9,8},{10,11... | collective-permute-start | bytes 368648 | tf_op jit(solution)/shard_map/ppermute | solution.py:512
  17.3 0.0 collective-permute-done.3.second_ref
  17.3 1.0 %collective-permute-done.2.first_ref = f32[3,80,128]{2,1,0:T(8,128)S(1)} collective-permute-done((f32[3,80,128]{2,1,0:T(8,128)S(1)}, f32[3,80,128]{2,1,0:T(8,128)S(1)}, u32[]{:S(2)}, u32[]{:S(2)}) %collective-permute-start.2) | collective-permute-done | bytes 122912 | tf_op jit(solution)/shard_map/ppermute | solution.py:512
  18.3 10.7 %shard_map.41 = (f32[24,48,128]{2,1,0:T(8,128)S(1)}, f32[24,48,128]{2,1,0:T(8,128)S(1)}, f32[16,32,128]{2,1,0:T(8,128)S(1)}, f32[16,32,128]{2,1,0:T(8,128)S(1)}, f32[32,128]{1,0:T(8,128)S(1)}) custom-call(f32[16,80,128]{2,1,0:T(8,128)S(1)} %get-tuple-element.24.centre_ref, f32[3,80,128]{2,1,0:T(8,128)S(1)} %collective-permute-done.2.first_ref, ...), custom_call_target="tpu_custom_call" | custom-call | tf_op jit(solution)/shard_map/pallas_call | solution.py:519
  29.0 11.9 %all_to_all.22 = f32[32,1,128]{2,1,0:T(1,128)S(1)} all-to-all(f32[32,1,128]{2,1,0:T(1,128)S(1)} %bitcast.12), channel_id=1, replica_groups=mesh['gy'=4,'gx'=8] {'gy','gx'}, dimensions={0} | all-to-all | bytes 32768 | tf_op jit(solution)/shard_map/all_to_all | solution.py:525
  40.9 0.8 %shard_map.42 = (f32[16,32,128]{2,1,0:T(8,128)S(1)}, f32[16,32,128]{2,1,0:T(8,128)S(1)}, f32[32,128]{1,0:T(8,128)S(1)}, f32[8,128]{1,0:T(8,128)S(1)}) custom-call(f32[32,128]{1,0:T(8,128)S(1)} %bitcast.9, f32[24,48,128]{2,1,0:T(8,128)S(1)} %get-tuple-element.33.x1_ref, f32[24,48,128]{2,1,0:T(8,128)S(1)} %get-tuple-element.34.g1_ref, ...), custom_call_target="tpu_custom_call" | custom-call | tf_op jit(solution)/shard_map/pallas_call | solution.py:527
  41.8 8.8 %all_to_all.23 = f32[32,1,128]{2,1,0:T(1,128)S(1)} all-to-all(f32[32,1,128]{2,1,0:T(1,128)S(1)} %bitcast.13), channel_id=1, replica_groups=mesh['gy'=4,'gx'=8] {'gy','gx'}, dimensions={0} | all-to-all | bytes 32768 | tf_op jit(solution)/shard_map/all_to_all | solution.py:533
  50.6 0.7 %shard_map.43 = f32[16,32,128]{2,1,0:T(8,128)} custom-call(f32[32,128]{1,0:T(8,128)S(1)} %bitcast.10, f32[8,128]{1,0:T(8,128)S(1)} %get-tuple-element.38.keep_ref, f32[16,32,128]{2,1,0:T(8,128)S(1)} %get-tuple-element.39.x2_ref, f32[16,32,128]{2,1,0:T(8,128)S(1)} %get-tuple-element.40.g2_ref), custom_call_target="tpu_custom_call" | custom-call | tf_op jit(solution)/shard_map/pallas_call | solution.py:534
  (1 shorter events, 0.0 us)
Async XLA Ops:
  1.1 10.1 %collective-permute-start.1 = (f32[16,24,128]{2,1,0:T(8,128)S(1)}, f32[16,24,128]{2,1,0:T(8,128)S(1)}, u32[]{:S(2)}, u32[]{:S(2)}) collective-permute-start(f32[16,24,128]{2,1,0:T(8,128)S(1)} %get-tuple-element.41), channel_id=1, source_target_pairs={{8,16},{16,8},{9,17},{17,9},{10,18},{18,10},{11,19},{19,11},{12,20... | collective-permute-start | bytes 589832 | tf_op jit(solution)/shard_map/ppermute | solution.py:491
  1.7 10.5 %collective-permute-start = (f32[16,24,128]{2,1,0:T(8,128)S(1)}, f32[16,24,128]{2,1,0:T(8,128)S(1)}, u32[]{:S(2)}, u32[]{:S(2)}) collective-permute-start(f32[16,24,128]{2,1,0:T(8,128)S(1)} %get-tuple-element.42), channel_id=1, source_target_pairs={{0,8},{8,0},{16,24},{24,16},{1,9},{9,1},{17,25},{25,17},{2,10},{10... | collective-permute-start | bytes 589832 | tf_op jit(solution)/shard_map/ppermute | solution.py:490
  7.6 0.9 %copy-start = (f32[16,32,128]{2,1,0:T(8,128)S(1)}, f32[16,32,128]{2,1,0:T(8,128)}, u32[]{:S(2)}) copy-start(f32[16,32,128]{2,1,0:T(8,128)} %tile_ref.1) | copy-start | bytes 786436
  8.6 0.7 %copy-start.1 = (f32[64,3,9]{0,1,2:T(4,128)S(1)}, f32[64,3,9]{0,1,2:T(4,128)}, u32[]{:S(2)}) copy-start(f32[64,3,9]{0,1,2:T(4,128)} %param.4) | copy-start | bytes 20740
  9.3 0.7 %copy-start.2 = (s32[4,8]{1,0:T(4,128)S(1)}, s32[4,8]{1,0:T(4,128)}, u32[]{:S(2)}) copy-start(s32[4,8]{1,0:T(4,128)} %index_ref.1) | copy-start | bytes 388
  12.7 4.7 %collective-permute-start.3 = (f32[3,80,128]{2,1,0:T(8,128)S(1)}, f32[3,80,128]{2,1,0:T(8,128)S(1)}, u32[]{:S(2)}, u32[]{:S(2)}) collective-permute-start(f32[3,80,128]{2,1,0:T(8,128)S(1)} %get-tuple-element.27.after_ref), channel_id=1, source_target_pairs={{1,2},{2,1},{3,4},{4,3},{5,6},{6,5},{9,10},{10,9},{11,12},{12,11},... | collective-permute-start | bytes 368648 | tf_op jit(solution)/shard_map/ppermute | solution.py:513
  14.4 3.9 %collective-permute-start.2 = (f32[3,80,128]{2,1,0:T(8,128)S(1)}, f32[3,80,128]{2,1,0:T(8,128)S(1)}, u32[]{:S(2)}, u32[]{:S(2)}) collective-permute-start(f32[3,80,128]{2,1,0:T(8,128)S(1)} %get-tuple-element.29), channel_id=1, source_target_pairs={{0,1},{1,0},{2,3},{3,2},{4,5},{5,4},{6,7},{7,6},{8,9},{9,8},{10,11... | collective-permute-start | bytes 368648 | tf_op jit(solution)/shard_map/ppermute | solution.py:512

commit v4 on v3

--- a/solution.py
+++ b/solution.py
@@ -77,7 +77,7 @@
                     columns_ref[band, tap] = jnp.concatenate([own, side], axis=1)
 
 
-def matrices_kernel(s, columns_ref, after_ref, forward_ref, backward_ref, full):
+def matrices_kernel(s, columns_ref, taps_ref, after_ref, forward_ref, backward_ref, depth_ref, full):
     breadth, taps, radius = s["breadth"], s["taps"], s["radius"]
     ring = 2 * breadth
     chunk = 32
@@ -100,6 +100,20 @@
             ref[number, :ring, :] = upper
             ref[number, ring:2 * ring, :] = (value - upper.astype(F32)).astype(BF16)
             ref[number, 2 * ring:, :] = upper
+    size = s["layers"] * SUB
+    row = lax.broadcasted_iota(jnp.int32, (size, 1), 0)
+    col = lax.broadcasted_iota(jnp.int32, (1, size), 1)
+    same = lax.rem(row, SUB) == lax.rem(col, SUB)
+    apart = jnp.where(same, row // SUB - col // SUB + radius, -1)
+    for band in range(3):
+        total = jnp.zeros((size, size), F32)
+        for tap in range(taps):
+            total = jnp.where(apart == tap, jnp.broadcast_to(taps_ref[band, 0, 0, tap][:1, :size], (1, size)), total)
+        for number, value in enumerate((total, total.T)):
+            upper = value.astype(BF16)
+            depth_ref[2 * band + number, :, :size] = upper
+            depth_ref[2 * band + number, :, size:2 * size] = upper
+            depth_ref[2 * band + number, :, 2 * size:] = (value - upper.astype(F32)).astype(BF16)
 
 
 def strip_places(s, layer):
@@ -170,22 +184,40 @@
     return total
 
 
-def row_depth(s, load, side, row_taps, depth_taps, transposed):
-    layers, taps, radius, pairs = s["layers"], s["taps"], s["radius"], s["pairs"]
-    shifts = [t - radius if transposed else radius - t for t in range(taps)]
-    base, count = (layers, pairs) if side else (0, layers)
-    mixed = [weighted(row_taps, [load(base + p, shift) for shift in shifts]) for p in range(count)]
+def shifts_of(s, transposed):
+    return [t - s["radius"] if transposed else s["radius"] - t for t in range(s["taps"])]
+
+
+def own_sums(s, loads, row_taps, depth_matrix, transposed):
+    layers, breadth = s["layers"], s["breadth"]
+    mixed = [
+        jnp.concatenate(
+            [weighted(row_taps, [load(p, shift) for shift in shifts_of(s, transposed)]) for p in range(layers)], axis=0)
+        for load in loads
+    ]
+    value = jnp.concatenate(mixed, axis=1)
+    upper = value.astype(BF16)
+    lower = (value - upper.astype(F32)).astype(BF16)
+    result = jnp.dot(depth_matrix, jnp.concatenate([upper, lower, upper], axis=0), preferred_element_type=F32)
+    return [
+        [result[p * SUB:(p + 1) * SUB, k * breadth:(k + 1) * breadth] for p in range(layers)] for k in range(len(loads))
+    ]
+
+
+def side_sums(s, load, row_taps, depth_taps, transposed):
+    layers, radius, pairs = s["layers"], s["radius"], s["pairs"]
+    shifts = shifts_of(s, transposed)
+    mixed = [weighted(row_taps, [load(layers + p, shift) for shift in shifts]) for p in range(pairs)]
     beyond = {}
-    if side:
-        first = first_lanes(s)
-        for step in range(1, radius + 1):
-            beyond[-step] = jnp.where(first, 0.0, swap_layers(s, mixed[pairs - step]))
-            beyond[pairs - 1 + step] = jnp.where(first, swap_layers(s, mixed[step - 1]), 0.0)
-    at = lambda p: mixed[p] if 0 <= p < count else beyond.get(p)
-    return [weighted(depth_taps, [at(p + shift) for shift in shifts]) for p in range(count)]
-
-
-def slope_tile(s, source, shift, tile, divergence, flux_rows, where):
+    first = first_lanes(s)
+    for step in range(1, radius + 1):
+        beyond[-step] = jnp.where(first, 0.0, swap_layers(s, mixed[pairs - step]))
+        beyond[pairs - 1 + step] = jnp.where(first, swap_layers(s, mixed[step - 1]), 0.0)
+    at = lambda p: mixed[p] if 0 <= p < pairs else beyond.get(p)
+    return [weighted(depth_taps, [at(p + shift) for shift in shifts]) for p in range(pairs)]
+
+
+def slope_tile(s, source, shift, tile, divergence, flux_rows, where, rows_only=False):
     gy, gx, ny, nx = where
     layers, height, breadth, pairs, quarter = s["layers"], s["height"], s["breadth"], s["pairs"], s["quarter"]
     lane = lax.broadcasted_iota(jnp.int32, (SUB, breadth), 1)
@@ -197,6 +229,7 @@
     start = tile * SUB
     row = gy * height + start - s["off"] + shift + lax.broadcasted_iota(jnp.int32, (SUB, breadth), 0)
     row_mask = jnp.where((row >= 0) & (row < ny * height - 1), 1.0, 0.0).astype(F32)
+    at_edge = tile * SUB + shift - s["off"] in (-SUB, height - SUB)
     last, first = breadth - 1, first_lanes(s)
     rows = slice(start, start + SUB)
 
@@ -220,7 +253,9 @@
         f_cols, totals = [], []
         for k, plane in enumerate(planes):
             here = heres[k]
-            step_rows = (source[plane, start + 1:start + 1 + SUB, :] - here) * row_mask
+            step_rows = source[plane, start + 1:start + 1 + SUB, :] - here
+            if at_edge:
+                step_rows = step_rows * row_mask
             step_cols = (nexts[k] - here) * masks[k // 2]
             square = step_rows * step_rows + step_cols * step_cols + SMOOTHING * SMOOTHING
             if afters[k] is not None:
@@ -229,6 +264,8 @@
             inverse = lax.rsqrt(square)
             f_rows = step_rows * inverse
             flux_rows[plane, rows, :] = f_rows
+            if rows_only:
+                continue
             f_cols.append(step_cols * inverse)
             total = -f_cols[k] - f_rows
             if before[k] is not None:
@@ -238,18 +275,22 @@
                 before[k] = step_depth * inverse
                 total = total - before[k]
             totals.append(total)
+        heres = afters
+        if rows_only:
+            continue
         rolled = [pltpu.roll(value, 1, 1) for value in f_cols]
         totals[0] = totals[0] + jnp.where(lane == 0, rolled[2], rolled[0])
         totals[1] = totals[1] + jnp.where(lane == 0, swap(rolled[2]), rolled[1])
         totals[2] = totals[2] + jnp.where(lane == 0, rolled[0], jnp.where(lane == 2 * quarter, swap(rolled[1]), rolled[2]))
         for plane, total in zip(planes, totals):
             divergence[plane, rows, :] = total
-        heres = afters
+    if rows_only:
+        return
     divergence[pairs, rows, :] = divergence[pairs, rows, :] + before[0]
     divergence[layers, rows, :] = divergence[layers, rows, :] + jnp.where(first, 0.0, swap(before[2]))
 
 
-def main_kernel(s, centre_ref, first_ref, second_ref, taps_ref, forward_ref, backward_ref,
+def main_kernel(s, centre_ref, first_ref, second_ref, taps_ref, forward_ref, backward_ref, depth_ref,
                 x1_ref, g1_ref, pull_ref, again_ref, part_ref,
                 x0, x1, x2, g0, y0, y1, y2, r0, r1, r2, q0, q1, q2, acc, div, flux):
     where = place()
@@ -283,7 +324,8 @@
         for tile in tiles:
             ref[:, rows(tile), :] = zero
 
-    def product(ref, low, high, band, matrices):
+    def product(ref, low, high, band, matrices, own_only=False):
+        width = breadth if own_only else 2 * breadth
         count = (high - low) * SUB
 
         def split(a, b):
@@ -296,11 +338,13 @@
         for member in range(2):
             high_part, low_part = split(member * pairs, (member + 1) * pairs)
             parts = [high_part, side_high] * 2 + [low_part, side_low]
-            result = jnp.dot(jnp.concatenate(parts, axis=1), matrices[2 * band + member], preferred_element_type=F32)
+            result = jnp.dot(jnp.concatenate(parts, axis=1), matrices[2 * band + member, :, :width], preferred_element_type=F32)
             own.append(result[:, :breadth].reshape(pairs, count, breadth))
-            rest = result[:, breadth:]
-            side = rest if side is None else side + rest
-        return [(0, own[0]), (pairs, own[1]), (layers, side.reshape(pairs, count, breadth))]
+            if not own_only:
+                rest = result[:, breadth:]
+                side = rest if side is None else side + rest
+        pieces = [(0, own[0]), (pairs, own[1])]
+        return pieces if own_only else pieces + [(layers, side.reshape(pairs, count, breadth))]
 
     def taps_of(band, half):
         return [[taps_ref[band, dim, half, t] for t in range(taps)] for dim in (1, 0)]
@@ -319,25 +363,41 @@
             for plane, piece in product(x, a, b, band, forward_ref):
                 ys[band][plane:plane + pairs, rows(a, b), :] = piece
 
+        def sums(band, source, low, high, transposed, emit):
+            own_taps, (row_taps, depth_taps) = taps_of(band, 0)[0], taps_of(band, 1)
+
+            def load_at(tile):
+                def load(plane, shift):
+                    if transposed and ((tile < span[band][0] and shift <= 0) or (tile >= span[band][1] and shift >= 0)):
+                        return None
+                    return source[plane, tile * SUB + shift:(tile + 1) * SUB + shift, :]
+
+                return load
+
+            for at in range(low, high, 2):
+                group = range(at, min(at + 2, high))
+                matrix = depth_ref[2 * band + (1 if transposed else 0)]
+                results = own_sums(s, [load_at(tile) for tile in group], own_taps, matrix, transposed)
+                for tile, result in zip(group, results):
+                    side = side_sums(s, load_at(tile), row_taps, depth_taps, transposed)
+                    for plane, value in enumerate(result + side):
+                        emit(plane, tile, value)
+
         def blur_rows(band):
-            for tile in range(*out[band]):
-                for side in range(2):
-                    load = lambda plane, shift: ys[band][plane, tile * SUB + shift:(tile + 1) * SUB + shift, :]
-                    for plane, value in enumerate(row_depth(s, load, side, *taps_of(band, side), False), side * layers):
-                        if number < 2:
-                            value = value - x0[plane, rows(tile), :]
-                        rs[band][plane, rows(tile), :] = value
+            def emit(plane, tile, value):
+                rs[band][plane, rows(tile), :] = value if number == 2 else value - x0[plane, rows(tile), :]
+
+            sums(band, ys[band], *out[band], False, emit)
 
         def back_rows(band):
-            for tile in range(*back[band]):
-                for side in range(2):
-                    load = lambda plane, shift: rs[band][plane, tile * SUB + shift:(tile + 1) * SUB + shift, :]
-                    for plane, value in enumerate(row_depth(s, load, side, *taps_of(band, side), True), side * layers):
-                        qs[band][plane, rows(tile), :] = value
+            def emit(plane, tile, value):
+                qs[band][plane, rows(tile), :] = value
+
+            sums(band, rs[band], *back[band], True, emit)
 
         def back_columns(band):
             a, b = back[band]
-            for plane, piece in product(qs[band], a, b, band, backward_ref):
+            for plane, piece in product(qs[band], a, b, band, backward_ref, number == 2):
                 for tile in range(a, b):
                     part = piece[:, (tile - a) * SUB:(tile - a + 1) * SUB, :]
                     at = slice(plane, plane + pairs)
@@ -371,7 +431,7 @@
         def slopes(a, b):
             if number < 2:
                 for tile in range(a, b):
-                    slope_tile(s, x, 0, tile, div, flux, where)
+                    slope_tile(s, x, 0, tile, div, flux, where, tile < back_low)
 
         middle = (begin + end) // 2
         columns(0)
@@ -427,7 +487,7 @@
     begin = s["first"] - low
     total = jnp.zeros((SUB, breadth), F32)
     for tile in range(begin - 1, begin + height // SUB):
-        slope_tile(s, x2, low * SUB, tile, div, flux, where)
+        slope_tile(s, x2, low * SUB, tile, div, flux, where, tile < begin)
         if tile < begin:
             continue
         at, out = slice(tile * SUB, (tile + 1) * SUB), slice((tile - begin) * SUB, (tile - begin + 1) * SUB)
@@ -503,10 +563,11 @@
         inputs=[vmem] * 3 + [anywhere],
     )(tile_here, from_even, from_odd, taps_all)
     matrices = sds((6, 3 * ring, ring), BF16)
-    forward, backward = call(
-        functools.partial(matrices_kernel, s), (matrices, matrices),
-        scratch=[pltpu.VMEM((ring, ring), F32)], inputs=[vmem, anywhere],
-    )(columns, second)
+    size = layers * SUB
+    forward, backward, depth = call(
+        functools.partial(matrices_kernel, s), (matrices, matrices, sds((6, size, 3 * size), BF16)),
+        scratch=[pltpu.VMEM((ring, ring), F32)], inputs=[vmem, vmem, anywhere],
+    )(columns, taps_all, second)
     first, backward = lax.optimization_barrier((first, backward))
     first_pairs, second_pairs = pairings(lax.axis_size("gx"))
     got_first = lax.ppermute(first, "gx", first_pairs)
@@ -520,8 +581,8 @@
         functools.partial(main_kernel, s),
         (sds(wide, F32), sds(wide, F32), tile, tile, sds((n, breadth), F32)),
         scratch=[pltpu.VMEM(shape, F32) for shape in [big] * 3 + [(layers, rows, breadth)] + [big] * 12],
-        inputs=[vmem] * 6,
-    )(centre, got_first, got_second, taps_all, forward, backward)
+        inputs=[vmem] * 7,
+    )(centre, got_first, got_second, taps_all, forward, backward, depth)
     sums = lax.all_to_all(part, ("gy", "gx"), 0, 0, tiled=True)
     work = pltpu.VMEM((s["planes"], (high - low + 1) * SUB, breadth), F32)
     x2, g2, part, keep = call(

time: 51.7 us -> 50.8 us (0.983)
  Pallas kernels: 14.9 us -> 14.2 us
    pallas_call x1, Pallas kernels: 10.7 us -> 9.8 us  [per_device(): call(functools.partial(main_kernel, s), (sds(wide, F32), sds(wide, F32),...]
  transfers between devices with their start and end apart: 4 -> 4, of which waited for: 2 -> 2; matrix products, arithmetic and copies ran while one was open for 0% -> 0% of each run, Pallas kernels for 4% -> 5%
where the time goes in v4:
time: 50.8 us; the launch traced here: 50.5 us
  blocking collectives  20.6 us (41%)
  Pallas kernels  14.2 us (28%)
  starting transfers between devices  10.2 us (20%)
  local copies, waits for them, and re-layouts  3.4 us (7%)
  waiting for transfers between devices  2.04 us (4%)
    all_to_all x2, blocking collectives, per_device(): sums = lax.all_to_all(part, ('gy', 'gx'), 0, 0, tiled=True)  20.6 us
    pallas_call x1, Pallas kernels, per_device(): call(functools.partial(main_kernel, s), (sds(wide, F32), sds(wide, F32),...  9.8 us
    ppermute x1, starting transfers between devices, per_device(): from_even = lax.ppermute(to_even, 'gy', first_pairs)  5.9 us
    ppermute x1, starting transfers between devices, per_device(): got_first = lax.ppermute(first, 'gx', first_pairs)  2.91 us
    unnamed x6, local copies, waits for them, and re-layouts  2.35 us
    pallas_call x1, Pallas kernels, per_device(): call(functools.partial(matrices_kernel, s), (matrices, matrices, sds((6,...  1.27 us
    pallas_call x1, Pallas kernels, per_device(): call(functools.partial(weights_kernel, s), (sds((3, 2, 2, taps, SUB, brea...  1.16 us
    ppermute x1, waiting for transfers between devices, per_device(): from_even = lax.ppermute(to_even, 'gy', first_pairs)  1.06 us
  transfers between devices with their start and end apart: 4, of which 2 were waited for; matrix products, arithmetic and copies ran while one was open for 0% of the time, Pallas kernels for 5%

profile of v4, /device:TPU:0, one launch (start us, length us, event | category | flops | bytes accessed | tf_op | source)
XLA Modules:
  0.0 50.5 jit_solution(11104865560716835245)
XLA Ops:
  0.0 1.1 %constant_dynamic-slice_fusion = (f32[16,24,128]{2,1,0:T(8,128)S(1)}, f32[16,24,128]{2,1,0:T(8,128)S(1)}) fusion(f32[16,32,128]{2,1,0:T(8,128)} %tile_ref.1, s32[]{:T(128)S(6)} %select_n.10, s32[]{:T(128)S(6)} %select_n.9), kind=kLoop, calls=%fused_computation | loop fusion | bytes 786440 | tf_op jit(solution)/shard_map/dynamic_slice | solution.py:548
  1.1 0.7 %collective-permute-start.1 = (f32[16,24,128]{2,1,0:T(8,128)S(1)}, f32[16,24,128]{2,1,0:T(8,128)S(1)}, u32[]{:S(2)}, u32[]{:S(2)}) collective-permute-start(f32[16,24,128]{2,1,0:T(8,128)S(1)} %get-tuple-element.43), channel_id=1, source_target_pairs={{8,16},{16,8},{9,17},{17,9},{10,18},{18,10},{11,19},{19,11},{12,20... | collective-permute-start | bytes 589832 | tf_op jit(solution)/shard_map/ppermute | solution.py:551
  1.7 5.9 %collective-permute-start = (f32[16,24,128]{2,1,0:T(8,128)S(1)}, f32[16,24,128]{2,1,0:T(8,128)S(1)}, u32[]{:S(2)}, u32[]{:S(2)}) collective-permute-start(f32[16,24,128]{2,1,0:T(8,128)S(1)} %get-tuple-element.44), channel_id=1, source_target_pairs={{0,8},{8,0},{16,24},{24,16},{1,9},{9,1},{17,25},{25,17},{2,10},{10... | collective-permute-start | bytes 589832 | tf_op jit(solution)/shard_map/ppermute | solution.py:550
  7.6 0.0 copy-start
  7.6 0.9 %copy-done = f32[16,32,128]{2,1,0:T(8,128)S(1)} copy-done((f32[16,32,128]{2,1,0:T(8,128)S(1)}, f32[16,32,128]{2,1,0:T(8,128)}, u32[]{:S(2)}) %copy-start) | copy-done | bytes 262168
  8.6 0.0 copy-start.1
  8.6 0.7 %copy-done.1 = f32[64,3,9]{0,1,2:T(4,128)S(1)} copy-done((f32[64,3,9]{0,1,2:T(4,128)S(1)}, f32[64,3,9]{0,1,2:T(4,128)}, u32[]{:S(2)}) %copy-start.1) | copy-done | bytes 6936
  9.3 0.0 copy-start.2
  9.3 0.7 %copy-done.2 = s32[4,8]{1,0:T(4,128)S(1)} copy-done((s32[4,8]{1,0:T(4,128)S(1)}, s32[4,8]{1,0:T(4,128)}, u32[]{:S(2)}) %copy-start.2) | copy-done | bytes 152
  10.0 1.2 %shard_map.38 = (f32[3,2,2,9,8,128]{5,4,3,2,1,0:T(8,128)S(1)}, f32[3,9,8,256]{3,2,1,0:T(8,128)S(1)}) custom-call(s32[4,8]{1,0:T(4,128)S(1)} %copy-done.2, f32[9,3,64]{2,1,0:T(4,128)S(1)} %bitcast.11), custom_call_target="tpu_custom_call" | custom-call | tf_op jit(solution)/shard_map/pallas_call | solution.py:555
  11.2 0.0 collective-permute-done.1.odd_ref
  11.2 1.1 %collective-permute-done.even_ref = f32[16,24,128]{2,1,0:T(8,128)S(1)} collective-permute-done((f32[16,24,128]{2,1,0:T(8,128)S(1)}, f32[16,24,128]{2,1,0:T(8,128)S(1)}, u32[]{:S(2)}, u32[]{:S(2)}) %collective-permute-start) | collective-permute-done | bytes 196640 | tf_op jit(solution)/shard_map/ppermute | solution.py:550
  12.3 0.4 shard_map.39
  12.7 0.7 %collective-permute-start.3 = (f32[3,80,128]{2,1,0:T(8,128)S(1)}, f32[3,80,128]{2,1,0:T(8,128)S(1)}, u32[]{:S(2)}, u32[]{:S(2)}) collective-permute-start(f32[3,80,128]{2,1,0:T(8,128)S(1)} %get-tuple-element.28.after_ref), channel_id=1, source_target_pairs={{1,2},{2,1},{3,4},{4,3},{5,6},{6,5},{9,10},{10,9},{11,12},{12,11},... | collective-permute-start | bytes 368648 | tf_op jit(solution)/shard_map/ppermute | solution.py:574
  13.4 1.3 %shard_map.40 = (bf16[6,768,256]{2,1,0:T(8,128)(2,1)S(1)}, bf16[6,768,256]{2,1,0:T(8,128)(2,1)S(1)}, bf16[6,128,384]{2,1,0:T(8,128)(2,1)S(1)}) custom-call(f32[3,9,8,256]{3,2,1,0:T(8,128)S(1)} %get-tuple-element.27.columns_ref, f32[3,2,2,9,8,128]{5,4,3,2,1,0:T(8,128)S(1)} %get-tuple-element.24.after_ref.taps_ref, f32[3,80,128]{2,1,0:T(8,128)S(1)} %get-tuple-element.28.after_ref), custom_call_target="tpu_custom_call" | custom-call | tf_op jit(solution)/shard_map/pallas_call | solution.py:567
  14.6 2.9 %collective-permute-start.2 = (f32[3,80,128]{2,1,0:T(8,128)S(1)}, f32[3,80,128]{2,1,0:T(8,128)S(1)}, u32[]{:S(2)}, u32[]{:S(2)}) collective-permute-start(f32[3,80,128]{2,1,0:T(8,128)S(1)} %get-tuple-element.30), channel_id=1, source_target_pairs={{0,1},{1,0},{2,3},{3,2},{4,5},{5,4},{6,7},{7,6},{8,9},{9,8},{10,11... | collective-permute-start | bytes 368648 | tf_op jit(solution)/shard_map/ppermute | solution.py:573
  17.5 0.0 collective-permute-done.3.second_ref
  17.5 1.0 %collective-permute-done.2.first_ref = f32[3,80,128]{2,1,0:T(8,128)S(1)} collective-permute-done((f32[3,80,128]{2,1,0:T(8,128)S(1)}, f32[3,80,128]{2,1,0:T(8,128)S(1)}, u32[]{:S(2)}, u32[]{:S(2)}) %collective-permute-start.2) | collective-permute-done | bytes 122912 | tf_op jit(solution)/shard_map/ppermute | solution.py:573
  18.5 9.8 %shard_map.41 = (f32[24,48,128]{2,1,0:T(8,128)S(1)}, f32[24,48,128]{2,1,0:T(8,128)S(1)}, f32[16,32,128]{2,1,0:T(8,128)S(1)}, f32[16,32,128]{2,1,0:T(8,128)S(1)}, f32[32,128]{1,0:T(8,128)S(1)}) custom-call(f32[16,80,128]{2,1,0:T(8,128)S(1)} %get-tuple-element.25.centre_ref, f32[3,80,128]{2,1,0:T(8,128)S(1)} %collective-permute-done.2.first_ref, ...), custom_call_target="tpu_custom_call" | custom-call | tf_op jit(solution)/shard_map/pallas_call | solution.py:580
  28.3 11.7 %all_to_all.22 = f32[32,1,128]{2,1,0:T(1,128)S(1)} all-to-all(f32[32,1,128]{2,1,0:T(1,128)S(1)} %bitcast.12), channel_id=1, replica_groups=mesh['gy'=4,'gx'=8] {'gy','gx'}, dimensions={0} | all-to-all | bytes 32768 | tf_op jit(solution)/shard_map/all_to_all | solution.py:586
  40.1 0.8 %shard_map.42 = (f32[16,32,128]{2,1,0:T(8,128)S(1)}, f32[16,32,128]{2,1,0:T(8,128)S(1)}, f32[32,128]{1,0:T(8,128)S(1)}, f32[8,128]{1,0:T(8,128)S(1)}) custom-call(f32[32,128]{1,0:T(8,128)S(1)} %bitcast.9, f32[24,48,128]{2,1,0:T(8,128)S(1)} %get-tuple-element.35.x1_ref, f32[24,48,128]{2,1,0:T(8,128)S(1)} %get-tuple-element.36.g1_ref, ...), custom_call_target="tpu_custom_call" | custom-call | tf_op jit(solution)/shard_map/pallas_call | solution.py:588
  40.9 8.8 %all_to_all.23 = f32[32,1,128]{2,1,0:T(1,128)S(1)} all-to-all(f32[32,1,128]{2,1,0:T(1,128)S(1)} %bitcast.13), channel_id=1, replica_groups=mesh['gy'=4,'gx'=8] {'gy','gx'}, dimensions={0} | all-to-all | bytes 32768 | tf_op jit(solution)/shard_map/all_to_all | solution.py:594
  49.7 0.7 %shard_map.43 = f32[16,32,128]{2,1,0:T(8,128)} custom-call(f32[32,128]{1,0:T(8,128)S(1)} %bitcast.10, f32[8,128]{1,0:T(8,128)S(1)} %get-tuple-element.40.keep_ref, f32[16,32,128]{2,1,0:T(8,128)S(1)} %get-tuple-element.41.x2_ref, f32[16,32,128]{2,1,0:T(8,128)S(1)} %get-tuple-element.42.g2_ref), custom_call_target="tpu_custom_call" | custom-call | tf_op jit(solution)/shard_map/pallas_call | solution.py:595
  (1 shorter events, 0.0 us)
Async XLA Ops:
  1.1 10.1 %collective-permute-start.1 = (f32[16,24,128]{2,1,0:T(8,128)S(1)}, f32[16,24,128]{2,1,0:T(8,128)S(1)}, u32[]{:S(2)}, u32[]{:S(2)}) collective-permute-start(f32[16,24,128]{2,1,0:T(8,128)S(1)} %get-tuple-element.43), channel_id=1, source_target_pairs={{8,16},{16,8},{9,17},{17,9},{10,18},{18,10},{11,19},{19,11},{12,20... | collective-permute-start | bytes 589832 | tf_op jit(solution)/shard_map/ppermute | solution.py:551
  1.7 10.5 %collective-permute-start = (f32[16,24,128]{2,1,0:T(8,128)S(1)}, f32[16,24,128]{2,1,0:T(8,128)S(1)}, u32[]{:S(2)}, u32[]{:S(2)}) collective-permute-start(f32[16,24,128]{2,1,0:T(8,128)S(1)} %get-tuple-element.44), channel_id=1, source_target_pairs={{0,8},{8,0},{16,24},{24,16},{1,9},{9,1},{17,25},{25,17},{2,10},{10... | collective-permute-start | bytes 589832 | tf_op jit(solution)/shard_map/ppermute | solution.py:550
  7.6 0.9 %copy-start = (f32[16,32,128]{2,1,0:T(8,128)S(1)}, f32[16,32,128]{2,1,0:T(8,128)}, u32[]{:S(2)}) copy-start(f32[16,32,128]{2,1,0:T(8,128)} %tile_ref.1) | copy-start | bytes 786436
  8.6 0.7 %copy-start.1 = (f32[64,3,9]{0,1,2:T(4,128)S(1)}, f32[64,3,9]{0,1,2:T(4,128)}, u32[]{:S(2)}) copy-start(f32[64,3,9]{0,1,2:T(4,128)} %param.4) | copy-start | bytes 20740
  9.3 0.7 %copy-start.2 = (s32[4,8]{1,0:T(4,128)S(1)}, s32[4,8]{1,0:T(4,128)}, u32[]{:S(2)}) copy-start(s32[4,8]{1,0:T(4,128)} %index_ref.1) | copy-start | bytes 388
  12.7 4.9 %collective-permute-start.3 = (f32[3,80,128]{2,1,0:T(8,128)S(1)}, f32[3,80,128]{2,1,0:T(8,128)S(1)}, u32[]{:S(2)}, u32[]{:S(2)}) collective-permute-start(f32[3,80,128]{2,1,0:T(8,128)S(1)} %get-tuple-element.28.after_ref), channel_id=1, source_target_pairs={{1,2},{2,1},{3,4},{4,3},{5,6},{6,5},{9,10},{10,9},{11,12},{12,11},... | collective-permute-start | bytes 368648 | tf_op jit(solution)/shard_map/ppermute | solution.py:574
  14.6 3.9 %collective-permute-start.2 = (f32[3,80,128]{2,1,0:T(8,128)S(1)}, f32[3,80,128]{2,1,0:T(8,128)S(1)}, u32[]{:S(2)}, u32[]{:S(2)}) collective-permute-start(f32[3,80,128]{2,1,0:T(8,128)S(1)} %get-tuple-element.30), channel_id=1, source_target_pairs={{0,1},{1,0},{2,3},{3,2},{4,5},{5,4},{6,7},{7,6},{8,9},{9,8},{10,11... | collective-permute-start | bytes 368648 | tf_op jit(solution)/shard_map/ppermute | solution.py:573

commit v5 on v4

--- a/solution.py
+++ b/solution.py
@@ -100,20 +100,34 @@
             ref[number, :ring, :] = upper
             ref[number, ring:2 * ring, :] = (value - upper.astype(F32)).astype(BF16)
             ref[number, 2 * ring:, :] = upper
-    size = s["layers"] * SUB
-    row = lax.broadcasted_iota(jnp.int32, (size, 1), 0)
-    col = lax.broadcasted_iota(jnp.int32, (1, size), 1)
-    same = lax.rem(row, SUB) == lax.rem(col, SUB)
-    apart = jnp.where(same, row // SUB - col // SUB + radius, -1)
+    window = SUB + 2 * radius
+    size = s["layers"] * window
+    place_in = lax.broadcasted_iota(jnp.int32, (SUB, size), 1)
+    layer_in, row_in = place_in // window, lax.rem(place_in, window)
+    row_out = lax.broadcasted_iota(jnp.int32, (SUB, size), 0)
+
+    def wide(band, dim, tap):
+        return jnp.broadcast_to(taps_ref[band, dim, 0, tap][:1, :1], (SUB, size))
+
     for band in range(3):
-        total = jnp.zeros((size, size), F32)
-        for tap in range(taps):
-            total = jnp.where(apart == tap, jnp.broadcast_to(taps_ref[band, 0, 0, tap][:1, :size], (1, size)), total)
-        for number, value in enumerate((total, total.T)):
+        for transposed in range(2):
+            number = 2 * band + transposed
+            apart = row_in - row_out if transposed else row_out + 2 * radius - row_in
+            by_row = jnp.zeros((SUB, size), F32)
+            for tap in range(taps):
+                by_row = jnp.where(apart == tap, wide(band, 1, tap), by_row)
+            depth_taps = [wide(band, 0, tap) for tap in range(taps)]
+            for layer in range(s["layers"]):
+                apart = layer_in - layer + radius if transposed else layer - layer_in + radius
+                value = jnp.zeros((SUB, size), F32)
+                for tap in range(taps):
+                    value = jnp.where(apart == tap, depth_taps[tap], value)
+                full[layer * SUB:(layer + 1) * SUB, :size] = value * by_row
+            value = full[:s["layers"] * SUB, :size]
             upper = value.astype(BF16)
-            depth_ref[2 * band + number, :, :size] = upper
-            depth_ref[2 * band + number, :, size:2 * size] = upper
-            depth_ref[2 * band + number, :, 2 * size:] = (value - upper.astype(F32)).astype(BF16)
+            depth_ref[number, :, :size] = upper
+            depth_ref[number, :, size:2 * size] = upper
+            depth_ref[number, :, 2 * size:] = (value - upper.astype(F32)).astype(BF16)
 
 
 def strip_places(s, layer):
@@ -188,19 +202,14 @@
     return [t - s["radius"] if transposed else s["radius"] - t for t in range(s["taps"])]
 
 
-def own_sums(s, loads, row_taps, depth_matrix, transposed):
+def own_sums(s, windows, matrix):
     layers, breadth = s["layers"], s["breadth"]
-    mixed = [
-        jnp.concatenate(
-            [weighted(row_taps, [load(p, shift) for shift in shifts_of(s, transposed)]) for p in range(layers)], axis=0)
-        for load in loads
-    ]
-    value = jnp.concatenate(mixed, axis=1)
+    value = jnp.concatenate([w.reshape(layers * w.shape[1], breadth) for w in windows], axis=1)
     upper = value.astype(BF16)
     lower = (value - upper.astype(F32)).astype(BF16)
-    result = jnp.dot(depth_matrix, jnp.concatenate([upper, lower, upper], axis=0), preferred_element_type=F32)
+    result = jnp.dot(matrix, jnp.concatenate([upper, lower, upper], axis=0), preferred_element_type=F32)
     return [
-        [result[p * SUB:(p + 1) * SUB, k * breadth:(k + 1) * breadth] for p in range(layers)] for k in range(len(loads))
+        [result[p * SUB:(p + 1) * SUB, k * breadth:(k + 1) * breadth] for p in range(layers)] for k in range(len(windows))
     ]
 
 
@@ -364,7 +373,7 @@
                 ys[band][plane:plane + pairs, rows(a, b), :] = piece
 
         def sums(band, source, low, high, transposed, emit):
-            own_taps, (row_taps, depth_taps) = taps_of(band, 0)[0], taps_of(band, 1)
+            row_taps, depth_taps = taps_of(band, 1)
 
             def load_at(tile):
                 def load(plane, shift):
@@ -377,7 +386,8 @@
             for at in range(low, high, 2):
                 group = range(at, min(at + 2, high))
                 matrix = depth_ref[2 * band + (1 if transposed else 0)]
-                results = own_sums(s, [load_at(tile) for tile in group], own_taps, matrix, transposed)
+                windows = [source[:layers, tile * SUB - radius:(tile + 1) * SUB + radius, :] for tile in group]
+                results = own_sums(s, windows, matrix)
                 for tile, result in zip(group, results):
                     side = side_sums(s, load_at(tile), row_taps, depth_taps, transposed)
                     for plane, value in enumerate(result + side):
@@ -563,9 +573,9 @@
         inputs=[vmem] * 3 + [anywhere],
     )(tile_here, from_even, from_odd, taps_all)
     matrices = sds((6, 3 * ring, ring), BF16)
-    size = layers * SUB
+    size = layers * (SUB + 2 * s["radius"])
     forward, backward, depth = call(
-        functools.partial(matrices_kernel, s), (matrices, matrices, sds((6, size, 3 * size), BF16)),
+        functools.partial(matrices_kernel, s), (matrices, matrices, sds((6, layers * SUB, 3 * size), BF16)),
         scratch=[pltpu.VMEM((ring, ring), F32)], inputs=[vmem, vmem, anywhere],
     )(columns, taps_all, second)
     first, backward = lax.optimization_barrier((first, backward))

time: 50.8 us -> 49.8 us (0.980)
    pallas_call x1, Pallas kernels: 9.8 us -> 8.84 us  [per_device(): call(functools.partial(main_kernel, s), (sds(wide, F32), sds(wide, F32),...]
  transfers between devices with their start and end apart: 4 -> 4, of which waited for: 2 -> 2; matrix products, arithmetic and copies ran while one was open for 0% -> 0% of each run, Pallas kernels for 5% -> 6%
where the time goes in v5:
time: 49.8 us; the launch traced here: 49.5 us
  blocking collectives  20.1 us (40%)
  Pallas kernels  13.7 us (28%)
  starting transfers between devices  10.2 us (20%)
  local copies, waits for them, and re-layouts  3.4 us (7%)
  waiting for transfers between devices  2.04 us (4%)
    all_to_all x2, blocking collectives, per_device(): sums = lax.all_to_all(part, ('gy', 'gx'), 0, 0, tiled=True)  20.1 us
    pallas_call x1, Pallas kernels, per_device(): call(functools.partial(main_kernel, s), (sds(wide, F32), sds(wide, F32),...  8.84 us
    ppermute x1, starting transfers between devices, per_device(): from_even = lax.ppermute(to_even, 'gy', first_pairs)  5.9 us
    ppermute x1, starting transfers between devices, per_device(): got_first = lax.ppermute(first, 'gx', first_pairs)  2.91 us
    unnamed x6, local copies, waits for them, and re-layouts  2.35 us
    pallas_call x1, Pallas kernels, per_device(): call(functools.partial(matrices_kernel, s), (matrices, matrices, sds((6,...  1.69 us
    pallas_call x1, Pallas kernels, per_device(): call(functools.partial(weights_kernel, s), (sds((3, 2, 2, taps, SUB, brea...  1.16 us
    ppermute x1, waiting for transfers between devices, per_device(): from_even = lax.ppermute(to_even, 'gy', first_pairs)  1.06 us
  transfers between devices with their start and end apart: 4, of which 2 were waited for; matrix products, arithmetic and copies ran while one was open for 0% of the time, Pallas kernels for 6%

profile of v5, /device:TPU:0, one launch (start us, length us, event | category | flops | bytes accessed | tf_op | source)
XLA Modules:
  0.0 49.5 jit_solution(7380680396528936184)
XLA Ops:
  0.0 1.1 %constant_dynamic-slice_fusion = (f32[16,24,128]{2,1,0:T(8,128)S(1)}, f32[16,24,128]{2,1,0:T(8,128)S(1)}) fusion(f32[16,32,128]{2,1,0:T(8,128)} %tile_ref.1, s32[]{:T(128)S(6)} %select_n.10, s32[]{:T(128)S(6)} %select_n.9), kind=kLoop, calls=%fused_computation | loop fusion | bytes 786440 | tf_op jit(solution)/shard_map/dynamic_slice | solution.py:558
  1.1 0.7 %collective-permute-start.1 = (f32[16,24,128]{2,1,0:T(8,128)S(1)}, f32[16,24,128]{2,1,0:T(8,128)S(1)}, u32[]{:S(2)}, u32[]{:S(2)}) collective-permute-start(f32[16,24,128]{2,1,0:T(8,128)S(1)} %get-tuple-element.43), channel_id=1, source_target_pairs={{8,16},{16,8},{9,17},{17,9},{10,18},{18,10},{11,19},{19,11},{12,20... | collective-permute-start | bytes 589832 | tf_op jit(solution)/shard_map/ppermute | solution.py:561
  1.7 5.9 %collective-permute-start = (f32[16,24,128]{2,1,0:T(8,128)S(1)}, f32[16,24,128]{2,1,0:T(8,128)S(1)}, u32[]{:S(2)}, u32[]{:S(2)}) collective-permute-start(f32[16,24,128]{2,1,0:T(8,128)S(1)} %get-tuple-element.44), channel_id=1, source_target_pairs={{0,8},{8,0},{16,24},{24,16},{1,9},{9,1},{17,25},{25,17},{2,10},{10... | collective-permute-start | bytes 589832 | tf_op jit(solution)/shard_map/ppermute | solution.py:560
  7.6 0.0 copy-start
  7.6 0.9 %copy-done = f32[16,32,128]{2,1,0:T(8,128)S(1)} copy-done((f32[16,32,128]{2,1,0:T(8,128)S(1)}, f32[16,32,128]{2,1,0:T(8,128)}, u32[]{:S(2)}) %copy-start) | copy-done | bytes 262168
  8.6 0.0 copy-start.1
  8.6 0.7 %copy-done.1 = f32[64,3,9]{0,1,2:T(4,128)S(1)} copy-done((f32[64,3,9]{0,1,2:T(4,128)S(1)}, f32[64,3,9]{0,1,2:T(4,128)}, u32[]{:S(2)}) %copy-start.1) | copy-done | bytes 6936
  9.3 0.0 copy-start.2
  9.3 0.7 %copy-done.2 = s32[4,8]{1,0:T(4,128)S(1)} copy-done((s32[4,8]{1,0:T(4,128)S(1)}, s32[4,8]{1,0:T(4,128)}, u32[]{:S(2)}) %copy-start.2) | copy-done | bytes 152
  10.0 1.2 %shard_map.38 = (f32[3,2,2,9,8,128]{5,4,3,2,1,0:T(8,128)S(1)}, f32[3,9,8,256]{3,2,1,0:T(8,128)S(1)}) custom-call(s32[4,8]{1,0:T(4,128)S(1)} %copy-done.2, f32[9,3,64]{2,1,0:T(4,128)S(1)} %bitcast.11), custom_call_target="tpu_custom_call" | custom-call | tf_op jit(solution)/shard_map/pallas_call | solution.py:565
  11.2 0.0 collective-permute-done.1.odd_ref
  11.2 1.1 %collective-permute-done.even_ref = f32[16,24,128]{2,1,0:T(8,128)S(1)} collective-permute-done((f32[16,24,128]{2,1,0:T(8,128)S(1)}, f32[16,24,128]{2,1,0:T(8,128)S(1)}, u32[]{:S(2)}, u32[]{:S(2)}) %collective-permute-start) | collective-permute-done | bytes 196640 | tf_op jit(solution)/shard_map/ppermute | solution.py:560
  12.3 0.4 shard_map.39
  12.7 0.7 %collective-permute-start.3 = (f32[3,80,128]{2,1,0:T(8,128)S(1)}, f32[3,80,128]{2,1,0:T(8,128)S(1)}, u32[]{:S(2)}, u32[]{:S(2)}) collective-permute-start(f32[3,80,128]{2,1,0:T(8,128)S(1)} %get-tuple-element.28.after_ref), channel_id=1, source_target_pairs={{1,2},{2,1},{3,4},{4,3},{5,6},{6,5},{9,10},{10,9},{11,12},{12,11},... | collective-permute-start | bytes 368648 | tf_op jit(solution)/shard_map/ppermute | solution.py:584
  13.4 1.7 %shard_map.40 = (bf16[6,768,256]{2,1,0:T(8,128)(2,1)S(1)}, bf16[6,768,256]{2,1,0:T(8,128)(2,1)S(1)}, bf16[6,128,768]{2,1,0:T(8,128)(2,1)S(1)}) custom-call(f32[3,9,8,256]{3,2,1,0:T(8,128)S(1)} %get-tuple-element.27.columns_ref, f32[3,2,2,9,8,128]{5,4,3,2,1,0:T(8,128)S(1)} %get-tuple-element.24.after_ref.taps_ref, f32[3,80,128]{2,1,0:T(8,128)S(1)} %get-tuple-element.28.after_ref), custom_call_target="tpu_custom_call" | custom-call | tf_op jit(solution)/shard_map/pallas_call | solution.py:577
  15.1 2.9 %collective-permute-start.2 = (f32[3,80,128]{2,1,0:T(8,128)S(1)}, f32[3,80,128]{2,1,0:T(8,128)S(1)}, u32[]{:S(2)}, u32[]{:S(2)}) collective-permute-start(f32[3,80,128]{2,1,0:T(8,128)S(1)} %get-tuple-element.30), channel_id=1, source_target_pairs={{0,1},{1,0},{2,3},{3,2},{4,5},{5,4},{6,7},{7,6},{8,9},{9,8},{10,11... | collective-permute-start | bytes 368648 | tf_op jit(solution)/shard_map/ppermute | solution.py:583
  18.0 0.0 collective-permute-done.3.second_ref
  18.0 1.0 %collective-permute-done.2.first_ref = f32[3,80,128]{2,1,0:T(8,128)S(1)} collective-permute-done((f32[3,80,128]{2,1,0:T(8,128)S(1)}, f32[3,80,128]{2,1,0:T(8,128)S(1)}, u32[]{:S(2)}, u32[]{:S(2)}) %collective-permute-start.2) | collective-permute-done | bytes 122912 | tf_op jit(solution)/shard_map/ppermute | solution.py:583
  18.9 8.8 %shard_map.41 = (f32[24,48,128]{2,1,0:T(8,128)S(1)}, f32[24,48,128]{2,1,0:T(8,128)S(1)}, f32[16,32,128]{2,1,0:T(8,128)S(1)}, f32[16,32,128]{2,1,0:T(8,128)S(1)}, f32[32,128]{1,0:T(8,128)S(1)}) custom-call(f32[16,80,128]{2,1,0:T(8,128)S(1)} %get-tuple-element.25.centre_ref, f32[3,80,128]{2,1,0:T(8,128)S(1)} %collective-permute-done.2.first_ref, ...), custom_call_target="tpu_custom_call" | custom-call | tf_op jit(solution)/shard_map/pallas_call | solution.py:590
  27.8 11.3 %all_to_all.22 = f32[32,1,128]{2,1,0:T(1,128)S(1)} all-to-all(f32[32,1,128]{2,1,0:T(1,128)S(1)} %bitcast.12), channel_id=1, replica_groups=mesh['gy'=4,'gx'=8] {'gy','gx'}, dimensions={0} | all-to-all | bytes 32768 | tf_op jit(solution)/shard_map/all_to_all | solution.py:596
  39.1 0.8 %shard_map.42 = (f32[16,32,128]{2,1,0:T(8,128)S(1)}, f32[16,32,128]{2,1,0:T(8,128)S(1)}, f32[32,128]{1,0:T(8,128)S(1)}, f32[8,128]{1,0:T(8,128)S(1)}) custom-call(f32[32,128]{1,0:T(8,128)S(1)} %bitcast.9, f32[24,48,128]{2,1,0:T(8,128)S(1)} %get-tuple-element.35.x1_ref, f32[24,48,128]{2,1,0:T(8,128)S(1)} %get-tuple-element.36.g1_ref, ...), custom_call_target="tpu_custom_call" | custom-call | tf_op jit(solution)/shard_map/pallas_call | solution.py:598
  39.9 8.8 %all_to_all.23 = f32[32,1,128]{2,1,0:T(1,128)S(1)} all-to-all(f32[32,1,128]{2,1,0:T(1,128)S(1)} %bitcast.13), channel_id=1, replica_groups=mesh['gy'=4,'gx'=8] {'gy','gx'}, dimensions={0} | all-to-all | bytes 32768 | tf_op jit(solution)/shard_map/all_to_all | solution.py:604
  48.8 0.7 %shard_map.43 = f32[16,32,128]{2,1,0:T(8,128)} custom-call(f32[32,128]{1,0:T(8,128)S(1)} %bitcast.10, f32[8,128]{1,0:T(8,128)S(1)} %get-tuple-element.40.keep_ref, f32[16,32,128]{2,1,0:T(8,128)S(1)} %get-tuple-element.41.x2_ref, f32[16,32,128]{2,1,0:T(8,128)S(1)} %get-tuple-element.42.g2_ref), custom_call_target="tpu_custom_call" | custom-call | tf_op jit(solution)/shard_map/pallas_call | solution.py:605
  (1 shorter events, 0.0 us)
Async XLA Ops:
  1.1 10.1 %collective-permute-start.1 = (f32[16,24,128]{2,1,0:T(8,128)S(1)}, f32[16,24,128]{2,1,0:T(8,128)S(1)}, u32[]{:S(2)}, u32[]{:S(2)}) collective-permute-start(f32[16,24,128]{2,1,0:T(8,128)S(1)} %get-tuple-element.43), channel_id=1, source_target_pairs={{8,16},{16,8},{9,17},{17,9},{10,18},{18,10},{11,19},{19,11},{12,20... | collective-permute-start | bytes 589832 | tf_op jit(solution)/shard_map/ppermute | solution.py:561
  1.7 10.5 %collective-permute-start = (f32[16,24,128]{2,1,0:T(8,128)S(1)}, f32[16,24,128]{2,1,0:T(8,128)S(1)}, u32[]{:S(2)}, u32[]{:S(2)}) collective-permute-start(f32[16,24,128]{2,1,0:T(8,128)S(1)} %get-tuple-element.44), channel_id=1, source_target_pairs={{0,8},{8,0},{16,24},{24,16},{1,9},{9,1},{17,25},{25,17},{2,10},{10... | collective-permute-start | bytes 589832 | tf_op jit(solution)/shard_map/ppermute | solution.py:560
  7.6 0.9 %copy-start = (f32[16,32,128]{2,1,0:T(8,128)S(1)}, f32[16,32,128]{2,1,0:T(8,128)}, u32[]{:S(2)}) copy-start(f32[16,32,128]{2,1,0:T(8,128)} %tile_ref.1) | copy-start | bytes 786436
  8.6 0.7 %copy-start.1 = (f32[64,3,9]{0,1,2:T(4,128)S(1)}, f32[64,3,9]{0,1,2:T(4,128)}, u32[]{:S(2)}) copy-start(f32[64,3,9]{0,1,2:T(4,128)} %param.4) | copy-start | bytes 20740
  9.3 0.7 %copy-start.2 = (s32[4,8]{1,0:T(4,128)S(1)}, s32[4,8]{1,0:T(4,128)}, u32[]{:S(2)}) copy-start(s32[4,8]{1,0:T(4,128)} %index_ref.1) | copy-start | bytes 388
  12.7 5.3 %collective-permute-start.3 = (f32[3,80,128]{2,1,0:T(8,128)S(1)}, f32[3,80,128]{2,1,0:T(8,128)S(1)}, u32[]{:S(2)}, u32[]{:S(2)}) collective-permute-start(f32[3,80,128]{2,1,0:T(8,128)S(1)} %get-tuple-element.28.after_ref), channel_id=1, source_target_pairs={{1,2},{2,1},{3,4},{4,3},{5,6},{6,5},{9,10},{10,9},{11,12},{12,11},... | collective-permute-start | bytes 368648 | tf_op jit(solution)/shard_map/ppermute | solution.py:584
  15.1 3.9 %collective-permute-start.2 = (f32[3,80,128]{2,1,0:T(8,128)S(1)}, f32[3,80,128]{2,1,0:T(8,128)S(1)}, u32[]{:S(2)}, u32[]{:S(2)}) collective-permute-start(f32[3,80,128]{2,1,0:T(8,128)S(1)} %get-tuple-element.30), channel_id=1, source_target_pairs={{0,1},{1,0},{2,3},{3,2},{4,5},{5,4},{6,7},{7,6},{8,9},{9,8},{10,11... | collective-permute-start | bytes 368648 | tf_op jit(solution)/shard_map/ppermute | solution.py:583

commit v6 on v5

--- a/solution.py
+++ b/solution.py
@@ -77,7 +77,11 @@
                     columns_ref[band, tap] = jnp.concatenate([own, side], axis=1)
 
 
-def matrices_kernel(s, columns_ref, taps_ref, after_ref, forward_ref, backward_ref, depth_ref, full):
+def matrices_kernel(s, columns_ref, taps_ref, after_ref, centre_ref, forward_ref, backward_ref, depth_ref, first_ref, full):
+    _, gx, _, _ = place()
+    for start in range(0, centre_ref.shape[1], 2 * SUB):
+        values = [centre_ref[layer, start:start + 2 * SUB, :] for layer in range(s["layers"])]
+        pack_strips(s, values, lax.rem(gx, 2) == 0, first_ref, start)
     breadth, taps, radius = s["breadth"], s["taps"], s["radius"]
     ring = 2 * breadth
     chunk = 32
@@ -139,14 +143,27 @@
     out_ref[...] = tile_ref[...]
 
 
-def pack_kernel(s, tile_ref, even_ref, odd_ref, after_ref, first_ref, second_ref, centre_ref):
+def pack_strips(s, values, right, out_ref, start):
+    halo, breadth = s["halo"], s["breadth"]
+    lane = lax.broadcasted_iota(jnp.int32, (1, breadth), 1)
+    count = values[0].shape[0]
+    total = [jnp.zeros((count, breadth), F32)] * s["groups"]
+    for layer, value in enumerate(values):
+        group, begin, here = strip_places(s, layer)
+        moved = pltpu.roll(value, jnp.where(right, (begin + halo) % breadth, begin), 1)
+        total[group] = jnp.where((lane >= begin) & (lane < begin + here), moved, total[group])
+        if here < halo:
+            total[group + 1] = jnp.where(lane < halo - here, moved, total[group + 1])
+    for number in range(s["groups"]):
+        out_ref[number, start:start + count, :] = total[number]
+
+
+def pack_kernel(s, tile_ref, even_ref, odd_ref, after_ref, second_ref, centre_ref):
     gy, gx, _, _ = place()
-    halo, height, breadth = s["halo"], s["height"], s["breadth"]
-    row_even, col_even = lax.rem(gy, 2) == 0, lax.rem(gx, 2) == 0
-    lane = lax.broadcasted_iota(jnp.int32, (1, breadth), 1)
+    halo, height = s["halo"], s["height"]
+    row_even = lax.rem(gy, 2) == 0
     for start, count in ((0, halo), (halo, height), (halo + height, halo)):
-        first = [jnp.zeros((count, breadth), F32)] * s["groups"]
-        second = list(first)
+        values = []
         for layer in range(s["layers"]):
             if start == halo:
                 value = tile_ref[layer]
@@ -155,19 +172,8 @@
             else:
                 value = jnp.where(row_even, even_ref[layer], odd_ref[layer])
             centre_ref[layer, start:start + count, :] = value
-            group, begin, here = strip_places(s, layer)
-            from_left, from_right = begin, (begin + halo) % breadth
-            to_first = pltpu.roll(value, jnp.where(col_even, from_right, from_left), 1)
-            to_second = pltpu.roll(value, jnp.where(col_even, from_left, from_right), 1)
-            parts = [(group, (lane >= begin) & (lane < begin + here))]
-            if here < halo:
-                parts.append((group + 1, lane < halo - here))
-            for number, mine in parts:
-                first[number] = jnp.where(mine, to_first, first[number])
-                second[number] = jnp.where(mine, to_second, second[number])
-        for number in range(s["groups"]):
-            first_ref[number, start:start + count, :] = first[number]
-            second_ref[number, start:start + count, :] = second[number]
+            values.append(value)
+        pack_strips(s, values, lax.rem(gx, 2) == 1, second_ref, start)
 
 
 def unpack_layer(s, groups, layer, to):
@@ -567,18 +573,17 @@
         (sds((3, 2, 2, taps, SUB, breadth), F32), sds((3, taps, SUB, ring), F32)), inputs=[smem, smem],
     )(tile_index, profiles.transpose(2, 1, 0))
     tile_here = call(copy_kernel, sds(observed.shape, F32), inputs=[vmem])(observed)
-    first, second, centre = call(
+    second, centre = call(
         functools.partial(pack_kernel, s),
-        (sds(packed, F32), sds(packed, F32), sds((layers, height + 2 * halo, breadth), F32)),
+        (sds(packed, F32), sds((layers, height + 2 * halo, breadth), F32)),
         inputs=[vmem] * 3 + [anywhere],
     )(tile_here, from_even, from_odd, taps_all)
     matrices = sds((6, 3 * ring, ring), BF16)
     size = layers * (SUB + 2 * s["radius"])
-    forward, backward, depth = call(
-        functools.partial(matrices_kernel, s), (matrices, matrices, sds((6, layers * SUB, 3 * size), BF16)),
-        scratch=[pltpu.VMEM((ring, ring), F32)], inputs=[vmem, vmem, anywhere],
-    )(columns, taps_all, second)
-    first, backward = lax.optimization_barrier((first, backward))
+    forward, backward, depth, first = call(
+        functools.partial(matrices_kernel, s), (matrices, matrices, sds((6, layers * SUB, 3 * size), BF16), sds(packed, F32)),
+        scratch=[pltpu.VMEM((ring, ring), F32)], inputs=[vmem, vmem, anywhere, vmem],
+    )(columns, taps_all, second, centre)
     first_pairs, second_pairs = pairings(lax.axis_size("gx"))
     got_first = lax.ppermute(first, "gx", first_pairs)
     got_second = lax.ppermute(second, "gx", second_pairs)

time: 49.8 us -> 49.6 us (level)
  no operation moved by 1% of the time
where the time goes in v6:
time: 49.6 us; the launch traced here: 49.3 us
  blocking collectives  20 us (40%)
  Pallas kernels  13.7 us (28%)
  starting transfers between devices  10.2 us (21%)
  local copies, waits for them, and re-layouts  3.4 us (7%)
  waiting for transfers between devices  2.04 us (4%)
    all_to_all x2, blocking collectives, per_device(): sums = lax.all_to_all(part, ('gy', 'gx'), 0, 0, tiled=True)  20 us
    pallas_call x1, Pallas kernels, per_device(): call(functools.partial(main_kernel, s), (sds(wide, F32), sds(wide, F32),...  8.84 us
    ppermute x1, starting transfers between devices, per_device(): from_even = lax.ppermute(to_even, 'gy', first_pairs)  5.9 us
    ppermute x1, starting transfers between devices, per_device(): got_first = lax.ppermute(first, 'gx', first_pairs)  2.91 us
    unnamed x6, local copies, waits for them, and re-layouts  2.35 us
    pallas_call x1, Pallas kernels, per_device(): call(functools.partial(matrices_kernel, s), (matrices, matrices, sds((6,...  1.84 us
    pallas_call x1, Pallas kernels, per_device(): call(functools.partial(weights_kernel, s), (sds((3, 2, 2, taps, SUB, brea...  1.16 us
    ppermute x1, waiting for transfers between devices, per_device(): from_even = lax.ppermute(to_even, 'gy', first_pairs)  1.06 us
  transfers between devices with their start and end apart: 4, of which 2 were waited for; matrix products, arithmetic and copies ran while one was open for 0% of the time, Pallas kernels for 6%

profile of v6, /device:TPU:0, one launch (start us, length us, event | category | flops | bytes accessed | tf_op | source)
XLA Modules:
  0.0 49.3 jit_solution(3454716066124580819)
XLA Ops:
  0.0 1.1 %constant_dynamic-slice_fusion = (f32[16,24,128]{2,1,0:T(8,128)S(1)}, f32[16,24,128]{2,1,0:T(8,128)S(1)}) fusion(f32[16,32,128]{2,1,0:T(8,128)} %tile_ref.1, s32[]{:T(128)S(6)} %select_n.10, s32[]{:T(128)S(6)} %select_n.9), kind=kLoop, calls=%fused_computation | loop fusion | bytes 786440 | tf_op jit(solution)/shard_map/dynamic_slice | solution.py:564
  1.1 0.7 %collective-permute-start.1 = (f32[16,24,128]{2,1,0:T(8,128)S(1)}, f32[16,24,128]{2,1,0:T(8,128)S(1)}, u32[]{:S(2)}, u32[]{:S(2)}) collective-permute-start(f32[16,24,128]{2,1,0:T(8,128)S(1)} %get-tuple-element.39), channel_id=1, source_target_pairs={{8,16},{16,8},{9,17},{17,9},{10,18},{18,10},{11,19},{19,11},{12,20... | collective-permute-start | bytes 589832 | tf_op jit(solution)/shard_map/ppermute | solution.py:567
  1.7 5.9 %collective-permute-start = (f32[16,24,128]{2,1,0:T(8,128)S(1)}, f32[16,24,128]{2,1,0:T(8,128)S(1)}, u32[]{:S(2)}, u32[]{:S(2)}) collective-permute-start(f32[16,24,128]{2,1,0:T(8,128)S(1)} %get-tuple-element.40), channel_id=1, source_target_pairs={{0,8},{8,0},{16,24},{24,16},{1,9},{9,1},{17,25},{25,17},{2,10},{10... | collective-permute-start | bytes 589832 | tf_op jit(solution)/shard_map/ppermute | solution.py:566
  7.6 0.0 copy-start
  7.6 0.9 %copy-done = f32[16,32,128]{2,1,0:T(8,128)S(1)} copy-done((f32[16,32,128]{2,1,0:T(8,128)S(1)}, f32[16,32,128]{2,1,0:T(8,128)}, u32[]{:S(2)}) %copy-start) | copy-done | bytes 262168
  8.6 0.0 copy-start.1
  8.6 0.7 %copy-done.1 = f32[64,3,9]{0,1,2:T(4,128)S(1)} copy-done((f32[64,3,9]{0,1,2:T(4,128)S(1)}, f32[64,3,9]{0,1,2:T(4,128)}, u32[]{:S(2)}) %copy-start.1) | copy-done | bytes 6936
  9.3 0.0 copy-start.2
  9.3 0.7 %copy-done.2 = s32[4,8]{1,0:T(4,128)S(1)} copy-done((s32[4,8]{1,0:T(4,128)S(1)}, s32[4,8]{1,0:T(4,128)}, u32[]{:S(2)}) %copy-start.2) | copy-done | bytes 152
  10.0 1.2 %shard_map.38 = (f32[3,2,2,9,8,128]{5,4,3,2,1,0:T(8,128)S(1)}, f32[3,9,8,256]{3,2,1,0:T(8,128)S(1)}) custom-call(s32[4,8]{1,0:T(4,128)S(1)} %copy-done.2, f32[9,3,64]{2,1,0:T(4,128)S(1)} %bitcast.11), custom_call_target="tpu_custom_call" | custom-call | tf_op jit(solution)/shard_map/pallas_call | solution.py:571
  11.2 0.0 collective-permute-done.1.odd_ref
  11.2 1.1 %collective-permute-done.even_ref = f32[16,24,128]{2,1,0:T(8,128)S(1)} collective-permute-done((f32[16,24,128]{2,1,0:T(8,128)S(1)}, f32[16,24,128]{2,1,0:T(8,128)S(1)}, u32[]{:S(2)}, u32[]{:S(2)}) %collective-permute-start) | collective-permute-done | bytes 196640 | tf_op jit(solution)/shard_map/ppermute | solution.py:566
  12.3 0.2 shard_map.39
  12.5 0.7 %collective-permute-start.3 = (f32[3,80,128]{2,1,0:T(8,128)S(1)}, f32[3,80,128]{2,1,0:T(8,128)S(1)}, u32[]{:S(2)}, u32[]{:S(2)}) collective-permute-start(f32[3,80,128]{2,1,0:T(8,128)S(1)} %get-tuple-element.25.after_ref), channel_id=1, source_target_pairs={{1,2},{2,1},{3,4},{4,3},{5,6},{6,5},{9,10},{10,9},{11,12},{12,11},... | collective-permute-start | bytes 368648 | tf_op jit(solution)/shard_map/ppermute | solution.py:589
  13.2 1.8 %shard_map.40 = (bf16[6,768,256]{2,1,0:T(8,128)(2,1)S(1)}, bf16[6,768,256]{2,1,0:T(8,128)(2,1)S(1)}, bf16[6,128,768]{2,1,0:T(8,128)(2,1)S(1)}, f32[3,80,128]{2,1,0:T(8,128)S(1)}) custom-call(f32[3,9,8,256]{3,2,1,0:T(8,128)S(1)} %get-tuple-element.24.columns_ref, f32[3,2,2,9,8,128]{5,4,3,2,1,0:T(8,128)S(1)} %get-tuple-element.22.after_ref.taps_ref, ...), custom_call_target="tpu_custom_call" | custom-call | tf_op jit(solution)/shard_map/pallas_call | solution.py:583
  15.0 2.9 %collective-permute-start.2 = (f32[3,80,128]{2,1,0:T(8,128)S(1)}, f32[3,80,128]{2,1,0:T(8,128)S(1)}, u32[]{:S(2)}, u32[]{:S(2)}) collective-permute-start(f32[3,80,128]{2,1,0:T(8,128)S(1)} %get-tuple-element.26), channel_id=1, source_target_pairs={{0,1},{1,0},{2,3},{3,2},{4,5},{5,4},{6,7},{7,6},{8,9},{9,8},{10,11... | collective-permute-start | bytes 368648 | tf_op jit(solution)/shard_map/ppermute | solution.py:588
  17.9 0.0 collective-permute-done.3.second_ref
  18.0 1.0 %collective-permute-done.2.first_ref = f32[3,80,128]{2,1,0:T(8,128)S(1)} collective-permute-done((f32[3,80,128]{2,1,0:T(8,128)S(1)}, f32[3,80,128]{2,1,0:T(8,128)S(1)}, u32[]{:S(2)}, u32[]{:S(2)}) %collective-permute-start.2) | collective-permute-done | bytes 122912 | tf_op jit(solution)/shard_map/ppermute | solution.py:588
  18.9 8.8 %shard_map.41 = (f32[24,48,128]{2,1,0:T(8,128)S(1)}, f32[24,48,128]{2,1,0:T(8,128)S(1)}, f32[16,32,128]{2,1,0:T(8,128)S(1)}, f32[16,32,128]{2,1,0:T(8,128)S(1)}, f32[32,128]{1,0:T(8,128)S(1)}) custom-call(f32[16,80,128]{2,1,0:T(8,128)S(1)} %get-tuple-element.23.centre_ref, f32[3,80,128]{2,1,0:T(8,128)S(1)} %collective-permute-done.2.first_ref, ...), custom_call_target="tpu_custom_call" | custom-call | tf_op jit(solution)/shard_map/pallas_call | solution.py:595
  27.8 11.2 %all_to_all.22 = f32[32,1,128]{2,1,0:T(1,128)S(1)} all-to-all(f32[32,1,128]{2,1,0:T(1,128)S(1)} %bitcast.12), channel_id=1, replica_groups=mesh['gy'=4,'gx'=8] {'gy','gx'}, dimensions={0} | all-to-all | bytes 32768 | tf_op jit(solution)/shard_map/all_to_all | solution.py:601
  38.9 0.8 %shard_map.42 = (f32[16,32,128]{2,1,0:T(8,128)S(1)}, f32[16,32,128]{2,1,0:T(8,128)S(1)}, f32[32,128]{1,0:T(8,128)S(1)}, f32[8,128]{1,0:T(8,128)S(1)}) custom-call(f32[32,128]{1,0:T(8,128)S(1)} %bitcast.9, f32[24,48,128]{2,1,0:T(8,128)S(1)} %get-tuple-element.31.x1_ref, f32[24,48,128]{2,1,0:T(8,128)S(1)} %get-tuple-element.32.g1_ref, ...), custom_call_target="tpu_custom_call" | custom-call | tf_op jit(solution)/shard_map/pallas_call | solution.py:603
  39.8 8.8 %all_to_all.23 = f32[32,1,128]{2,1,0:T(1,128)S(1)} all-to-all(f32[32,1,128]{2,1,0:T(1,128)S(1)} %bitcast.13), channel_id=1, replica_groups=mesh['gy'=4,'gx'=8] {'gy','gx'}, dimensions={0} | all-to-all | bytes 32768 | tf_op jit(solution)/shard_map/all_to_all | solution.py:609
  48.6 0.7 %shard_map.43 = f32[16,32,128]{2,1,0:T(8,128)} custom-call(f32[32,128]{1,0:T(8,128)S(1)} %bitcast.10, f32[8,128]{1,0:T(8,128)S(1)} %get-tuple-element.36.keep_ref, f32[16,32,128]{2,1,0:T(8,128)S(1)} %get-tuple-element.37.x2_ref, f32[16,32,128]{2,1,0:T(8,128)S(1)} %get-tuple-element.38.g2_ref), custom_call_target="tpu_custom_call" | custom-call | tf_op jit(solution)/shard_map/pallas_call | solution.py:610
  (1 shorter events, 0.0 us)
Async XLA Ops:
  1.1 10.1 %collective-permute-start.1 = (f32[16,24,128]{2,1,0:T(8,128)S(1)}, f32[16,24,128]{2,1,0:T(8,128)S(1)}, u32[]{:S(2)}, u32[]{:S(2)}) collective-permute-start(f32[16,24,128]{2,1,0:T(8,128)S(1)} %get-tuple-element.39), channel_id=1, source_target_pairs={{8,16},{16,8},{9,17},{17,9},{10,18},{18,10},{11,19},{19,11},{12,20... | collective-permute-start | bytes 589832 | tf_op jit(solution)/shard_map/ppermute | solution.py:567
  1.7 10.5 %collective-permute-start = (f32[16,24,128]{2,1,0:T(8,128)S(1)}, f32[16,24,128]{2,1,0:T(8,128)S(1)}, u32[]{:S(2)}, u32[]{:S(2)}) collective-permute-start(f32[16,24,128]{2,1,0:T(8,128)S(1)} %get-tuple-element.40), channel_id=1, source_target_pairs={{0,8},{8,0},{16,24},{24,16},{1,9},{9,1},{17,25},{25,17},{2,10},{10... | collective-permute-start | bytes 589832 | tf_op jit(solution)/shard_map/ppermute | solution.py:566
  7.6 0.9 %copy-start = (f32[16,32,128]{2,1,0:T(8,128)S(1)}, f32[16,32,128]{2,1,0:T(8,128)}, u32[]{:S(2)}) copy-start(f32[16,32,128]{2,1,0:T(8,128)} %tile_ref.1) | copy-start | bytes 786436
  8.6 0.7 %copy-start.1 = (f32[64,3,9]{0,1,2:T(4,128)S(1)}, f32[64,3,9]{0,1,2:T(4,128)}, u32[]{:S(2)}) copy-start(f32[64,3,9]{0,1,2:T(4,128)} %param.4) | copy-start | bytes 20740
  9.3 0.7 %copy-start.2 = (s32[4,8]{1,0:T(4,128)S(1)}, s32[4,8]{1,0:T(4,128)}, u32[]{:S(2)}) copy-start(s32[4,8]{1,0:T(4,128)} %index_ref.1) | copy-start | bytes 388
  12.5 5.4 %collective-permute-start.3 = (f32[3,80,128]{2,1,0:T(8,128)S(1)}, f32[3,80,128]{2,1,0:T(8,128)S(1)}, u32[]{:S(2)}, u32[]{:S(2)}) collective-permute-start(f32[3,80,128]{2,1,0:T(8,128)S(1)} %get-tuple-element.25.after_ref), channel_id=1, source_target_pairs={{1,2},{2,1},{3,4},{4,3},{5,6},{6,5},{9,10},{10,9},{11,12},{12,11},... | collective-permute-start | bytes 368648 | tf_op jit(solution)/shard_map/ppermute | solution.py:589
  15.0 3.9 %collective-permute-start.2 = (f32[3,80,128]{2,1,0:T(8,128)S(1)}, f32[3,80,128]{2,1,0:T(8,128)S(1)}, u32[]{:S(2)}, u32[]{:S(2)}) collective-permute-start(f32[3,80,128]{2,1,0:T(8,128)S(1)} %get-tuple-element.26), channel_id=1, source_target_pairs={{0,1},{1,0},{2,3},{3,2},{4,5},{5,4},{6,7},{7,6},{8,9},{9,8},{10,11... | collective-permute-start | bytes 368648 | tf_op jit(solution)/shard_map/ppermute | solution.py:588

commit v7 on v6

--- a/solution.py
+++ b/solution.py
@@ -232,7 +232,7 @@
     return [weighted(depth_taps, [at(p + shift) for shift in shifts]) for p in range(pairs)]
 
 
-def slope_tile(s, source, shift, tile, divergence, flux_rows, where, rows_only=False):
+def slope_tile(s, source, shift, tile, divergence, flux_rows, where, rows_only=False, own_only=False):
     gy, gx, ny, nx = where
     layers, height, breadth, pairs, quarter = s["layers"], s["height"], s["breadth"], s["pairs"], s["quarter"]
     lane = lax.broadcasted_iota(jnp.int32, (SUB, breadth), 1)
@@ -277,6 +277,9 @@
                 step_depth = afters[k] - here
                 square = square + step_depth * step_depth
             inverse = lax.rsqrt(square)
+            if own_only and k == 2:
+                f_cols.append(step_cols * inverse)
+                continue
             f_rows = step_rows * inverse
             flux_rows[plane, rows, :] = f_rows
             if rows_only:
@@ -296,12 +299,15 @@
         rolled = [pltpu.roll(value, 1, 1) for value in f_cols]
         totals[0] = totals[0] + jnp.where(lane == 0, rolled[2], rolled[0])
         totals[1] = totals[1] + jnp.where(lane == 0, swap(rolled[2]), rolled[1])
-        totals[2] = totals[2] + jnp.where(lane == 0, rolled[0], jnp.where(lane == 2 * quarter, swap(rolled[1]), rolled[2]))
+        if not own_only:
+            totals[2] = totals[2] + jnp.where(lane == 0, rolled[0], jnp.where(lane == 2 * quarter, swap(rolled[1]), rolled[2]))
         for plane, total in zip(planes, totals):
             divergence[plane, rows, :] = total
     if rows_only:
         return
     divergence[pairs, rows, :] = divergence[pairs, rows, :] + before[0]
+    if own_only:
+        return
     divergence[layers, rows, :] = divergence[layers, rows, :] + jnp.where(first, 0.0, swap(before[2]))
 
 
@@ -503,7 +509,7 @@
     begin = s["first"] - low
     total = jnp.zeros((SUB, breadth), F32)
     for tile in range(begin - 1, begin + height // SUB):
-        slope_tile(s, x2, low * SUB, tile, div, flux, where, tile < begin)
+        slope_tile(s, x2, low * SUB, tile, div, flux, where, tile < begin, True)
         if tile < begin:
             continue
         at, out = slice(tile * SUB, (tile + 1) * SUB), slice((tile - begin) * SUB, (tile - begin + 1) * SUB)

time: 49.6 us -> 49.6 us (level)
  no operation moved by 1% of the time
where the time goes in v7:
time: 49.6 us; the launch traced here: 49.3 us
  blocking collectives  20 us (40%)
  Pallas kernels  13.7 us (28%)
  starting transfers between devices  10.2 us (21%)
  local copies, waits for them, and re-layouts  3.4 us (7%)
  waiting for transfers between devices  2.04 us (4%)
    all_to_all x2, blocking collectives, per_device(): sums = lax.all_to_all(part, ('gy', 'gx'), 0, 0, tiled=True)  20 us
    pallas_call x1, Pallas kernels, per_device(): call(functools.partial(main_kernel, s), (sds(wide, F32), sds(wide, F32),...  8.84 us
    ppermute x1, starting transfers between devices, per_device(): from_even = lax.ppermute(to_even, 'gy', first_pairs)  5.9 us
    ppermute x1, starting transfers between devices, per_device(): got_first = lax.ppermute(first, 'gx', first_pairs)  2.91 us
    unnamed x6, local copies, waits for them, and re-layouts  2.35 us
    pallas_call x1, Pallas kernels, per_device(): call(functools.partial(matrices_kernel, s), (matrices, matrices, sds((6,...  1.84 us
    pallas_call x1, Pallas kernels, per_device(): call(functools.partial(weights_kernel, s), (sds((3, 2, 2, taps, SUB, brea...  1.16 us
    ppermute x1, waiting for transfers between devices, per_device(): from_even = lax.ppermute(to_even, 'gy', first_pairs)  1.06 us
  transfers between devices with their start and end apart: 4, of which 2 were waited for; matrix products, arithmetic and copies ran while one was open for 0% of the time, Pallas kernels for 6%

profile of v7, /device:TPU:0, one launch (start us, length us, event | category | flops | bytes accessed | tf_op | source)
XLA Modules:
  0.0 49.3 jit_solution(7128872991211539512)
XLA Ops:
  0.0 1.1 %constant_dynamic-slice_fusion = (f32[16,24,128]{2,1,0:T(8,128)S(1)}, f32[16,24,128]{2,1,0:T(8,128)S(1)}) fusion(f32[16,32,128]{2,1,0:T(8,128)} %tile_ref.1, s32[]{:T(128)S(6)} %select_n.10, s32[]{:T(128)S(6)} %select_n.9), kind=kLoop, calls=%fused_computation | loop fusion | bytes 786440 | tf_op jit(solution)/shard_map/dynamic_slice | solution.py:570
  1.1 0.7 %collective-permute-start.1 = (f32[16,24,128]{2,1,0:T(8,128)S(1)}, f32[16,24,128]{2,1,0:T(8,128)S(1)}, u32[]{:S(2)}, u32[]{:S(2)}) collective-permute-start(f32[16,24,128]{2,1,0:T(8,128)S(1)} %get-tuple-element.39), channel_id=1, source_target_pairs={{8,16},{16,8},{9,17},{17,9},{10,18},{18,10},{11,19},{19,11},{12,20... | collective-permute-start | bytes 589832 | tf_op jit(solution)/shard_map/ppermute | solution.py:573
  1.7 5.9 %collective-permute-start = (f32[16,24,128]{2,1,0:T(8,128)S(1)}, f32[16,24,128]{2,1,0:T(8,128)S(1)}, u32[]{:S(2)}, u32[]{:S(2)}) collective-permute-start(f32[16,24,128]{2,1,0:T(8,128)S(1)} %get-tuple-element.40), channel_id=1, source_target_pairs={{0,8},{8,0},{16,24},{24,16},{1,9},{9,1},{17,25},{25,17},{2,10},{10... | collective-permute-start | bytes 589832 | tf_op jit(solution)/shard_map/ppermute | solution.py:572
  7.6 0.0 copy-start
  7.6 0.9 %copy-done = f32[16,32,128]{2,1,0:T(8,128)S(1)} copy-done((f32[16,32,128]{2,1,0:T(8,128)S(1)}, f32[16,32,128]{2,1,0:T(8,128)}, u32[]{:S(2)}) %copy-start) | copy-done | bytes 262168
  8.6 0.0 copy-start.1
  8.6 0.7 %copy-done.1 = f32[64,3,9]{0,1,2:T(4,128)S(1)} copy-done((f32[64,3,9]{0,1,2:T(4,128)S(1)}, f32[64,3,9]{0,1,2:T(4,128)}, u32[]{:S(2)}) %copy-start.1) | copy-done | bytes 6936
  9.3 0.0 copy-start.2
  9.3 0.7 %copy-done.2 = s32[4,8]{1,0:T(4,128)S(1)} copy-done((s32[4,8]{1,0:T(4,128)S(1)}, s32[4,8]{1,0:T(4,128)}, u32[]{:S(2)}) %copy-start.2) | copy-done | bytes 152
  10.0 1.2 %shard_map.38 = (f32[3,2,2,9,8,128]{5,4,3,2,1,0:T(8,128)S(1)}, f32[3,9,8,256]{3,2,1,0:T(8,128)S(1)}) custom-call(s32[4,8]{1,0:T(4,128)S(1)} %copy-done.2, f32[9,3,64]{2,1,0:T(4,128)S(1)} %bitcast.11), custom_call_target="tpu_custom_call" | custom-call | tf_op jit(solution)/shard_map/pallas_call | solution.py:577
  11.2 0.0 collective-permute-done.1.odd_ref
  11.2 1.1 %collective-permute-done.even_ref = f32[16,24,128]{2,1,0:T(8,128)S(1)} collective-permute-done((f32[16,24,128]{2,1,0:T(8,128)S(1)}, f32[16,24,128]{2,1,0:T(8,128)S(1)}, u32[]{:S(2)}, u32[]{:S(2)}) %collective-permute-start) | collective-permute-done | bytes 196640 | tf_op jit(solution)/shard_map/ppermute | solution.py:572
  12.3 0.2 shard_map.39
  12.5 0.7 %collective-permute-start.3 = (f32[3,80,128]{2,1,0:T(8,128)S(1)}, f32[3,80,128]{2,1,0:T(8,128)S(1)}, u32[]{:S(2)}, u32[]{:S(2)}) collective-permute-start(f32[3,80,128]{2,1,0:T(8,128)S(1)} %get-tuple-element.25.after_ref), channel_id=1, source_target_pairs={{1,2},{2,1},{3,4},{4,3},{5,6},{6,5},{9,10},{10,9},{11,12},{12,11},... | collective-permute-start | bytes 368648 | tf_op jit(solution)/shard_map/ppermute | solution.py:595
  13.2 1.8 %shard_map.40 = (bf16[6,768,256]{2,1,0:T(8,128)(2,1)S(1)}, bf16[6,768,256]{2,1,0:T(8,128)(2,1)S(1)}, bf16[6,128,768]{2,1,0:T(8,128)(2,1)S(1)}, f32[3,80,128]{2,1,0:T(8,128)S(1)}) custom-call(f32[3,9,8,256]{3,2,1,0:T(8,128)S(1)} %get-tuple-element.24.columns_ref, f32[3,2,2,9,8,128]{5,4,3,2,1,0:T(8,128)S(1)} %get-tuple-element.22.after_ref.taps_ref, ...), custom_call_target="tpu_custom_call" | custom-call | tf_op jit(solution)/shard_map/pallas_call | solution.py:589
  15.0 2.9 %collective-permute-start.2 = (f32[3,80,128]{2,1,0:T(8,128)S(1)}, f32[3,80,128]{2,1,0:T(8,128)S(1)}, u32[]{:S(2)}, u32[]{:S(2)}) collective-permute-start(f32[3,80,128]{2,1,0:T(8,128)S(1)} %get-tuple-element.26), channel_id=1, source_target_pairs={{0,1},{1,0},{2,3},{3,2},{4,5},{5,4},{6,7},{7,6},{8,9},{9,8},{10,11... | collective-permute-start | bytes 368648 | tf_op jit(solution)/shard_map/ppermute | solution.py:594
  17.9 0.0 collective-permute-done.3.second_ref
  18.0 1.0 %collective-permute-done.2.first_ref = f32[3,80,128]{2,1,0:T(8,128)S(1)} collective-permute-done((f32[3,80,128]{2,1,0:T(8,128)S(1)}, f32[3,80,128]{2,1,0:T(8,128)S(1)}, u32[]{:S(2)}, u32[]{:S(2)}) %collective-permute-start.2) | collective-permute-done | bytes 122912 | tf_op jit(solution)/shard_map/ppermute | solution.py:594
  18.9 8.8 %shard_map.41 = (f32[24,48,128]{2,1,0:T(8,128)S(1)}, f32[24,48,128]{2,1,0:T(8,128)S(1)}, f32[16,32,128]{2,1,0:T(8,128)S(1)}, f32[16,32,128]{2,1,0:T(8,128)S(1)}, f32[32,128]{1,0:T(8,128)S(1)}) custom-call(f32[16,80,128]{2,1,0:T(8,128)S(1)} %get-tuple-element.23.centre_ref, f32[3,80,128]{2,1,0:T(8,128)S(1)} %collective-permute-done.2.first_ref, ...), custom_call_target="tpu_custom_call" | custom-call | tf_op jit(solution)/shard_map/pallas_call | solution.py:601
  27.8 11.2 %all_to_all.22 = f32[32,1,128]{2,1,0:T(1,128)S(1)} all-to-all(f32[32,1,128]{2,1,0:T(1,128)S(1)} %bitcast.12), channel_id=1, replica_groups=mesh['gy'=4,'gx'=8] {'gy','gx'}, dimensions={0} | all-to-all | bytes 32768 | tf_op jit(solution)/shard_map/all_to_all | solution.py:607
  38.9 0.8 %shard_map.42 = (f32[16,32,128]{2,1,0:T(8,128)S(1)}, f32[16,32,128]{2,1,0:T(8,128)S(1)}, f32[32,128]{1,0:T(8,128)S(1)}, f32[8,128]{1,0:T(8,128)S(1)}) custom-call(f32[32,128]{1,0:T(8,128)S(1)} %bitcast.9, f32[24,48,128]{2,1,0:T(8,128)S(1)} %get-tuple-element.31.x1_ref, f32[24,48,128]{2,1,0:T(8,128)S(1)} %get-tuple-element.32.g1_ref, ...), custom_call_target="tpu_custom_call" | custom-call | tf_op jit(solution)/shard_map/pallas_call | solution.py:609
  39.7 8.8 %all_to_all.23 = f32[32,1,128]{2,1,0:T(1,128)S(1)} all-to-all(f32[32,1,128]{2,1,0:T(1,128)S(1)} %bitcast.13), channel_id=1, replica_groups=mesh['gy'=4,'gx'=8] {'gy','gx'}, dimensions={0} | all-to-all | bytes 32768 | tf_op jit(solution)/shard_map/all_to_all | solution.py:615
  48.6 0.7 %shard_map.43 = f32[16,32,128]{2,1,0:T(8,128)} custom-call(f32[32,128]{1,0:T(8,128)S(1)} %bitcast.10, f32[8,128]{1,0:T(8,128)S(1)} %get-tuple-element.36.keep_ref, f32[16,32,128]{2,1,0:T(8,128)S(1)} %get-tuple-element.37.x2_ref, f32[16,32,128]{2,1,0:T(8,128)S(1)} %get-tuple-element.38.g2_ref), custom_call_target="tpu_custom_call" | custom-call | tf_op jit(solution)/shard_map/pallas_call | solution.py:616
  (1 shorter events, 0.0 us)
Async XLA Ops:
  1.1 10.1 %collective-permute-start.1 = (f32[16,24,128]{2,1,0:T(8,128)S(1)}, f32[16,24,128]{2,1,0:T(8,128)S(1)}, u32[]{:S(2)}, u32[]{:S(2)}) collective-permute-start(f32[16,24,128]{2,1,0:T(8,128)S(1)} %get-tuple-element.39), channel_id=1, source_target_pairs={{8,16},{16,8},{9,17},{17,9},{10,18},{18,10},{11,19},{19,11},{12,20... | collective-permute-start | bytes 589832 | tf_op jit(solution)/shard_map/ppermute | solution.py:573
  1.7 10.5 %collective-permute-start = (f32[16,24,128]{2,1,0:T(8,128)S(1)}, f32[16,24,128]{2,1,0:T(8,128)S(1)}, u32[]{:S(2)}, u32[]{:S(2)}) collective-permute-start(f32[16,24,128]{2,1,0:T(8,128)S(1)} %get-tuple-element.40), channel_id=1, source_target_pairs={{0,8},{8,0},{16,24},{24,16},{1,9},{9,1},{17,25},{25,17},{2,10},{10... | collective-permute-start | bytes 589832 | tf_op jit(solution)/shard_map/ppermute | solution.py:572
  7.6 0.9 %copy-start = (f32[16,32,128]{2,1,0:T(8,128)S(1)}, f32[16,32,128]{2,1,0:T(8,128)}, u32[]{:S(2)}) copy-start(f32[16,32,128]{2,1,0:T(8,128)} %tile_ref.1) | copy-start | bytes 786436
  8.6 0.7 %copy-start.1 = (f32[64,3,9]{0,1,2:T(4,128)S(1)}, f32[64,3,9]{0,1,2:T(4,128)}, u32[]{:S(2)}) copy-start(f32[64,3,9]{0,1,2:T(4,128)} %param.4) | copy-start | bytes 20740
  9.3 0.7 %copy-start.2 = (s32[4,8]{1,0:T(4,128)S(1)}, s32[4,8]{1,0:T(4,128)}, u32[]{:S(2)}) copy-start(s32[4,8]{1,0:T(4,128)} %index_ref.1) | copy-start | bytes 388
  12.5 5.4 %collective-permute-start.3 = (f32[3,80,128]{2,1,0:T(8,128)S(1)}, f32[3,80,128]{2,1,0:T(8,128)S(1)}, u32[]{:S(2)}, u32[]{:S(2)}) collective-permute-start(f32[3,80,128]{2,1,0:T(8,128)S(1)} %get-tuple-element.25.after_ref), channel_id=1, source_target_pairs={{1,2},{2,1},{3,4},{4,3},{5,6},{6,5},{9,10},{10,9},{11,12},{12,11},... | collective-permute-start | bytes 368648 | tf_op jit(solution)/shard_map/ppermute | solution.py:595
  15.0 3.9 %collective-permute-start.2 = (f32[3,80,128]{2,1,0:T(8,128)S(1)}, f32[3,80,128]{2,1,0:T(8,128)S(1)}, u32[]{:S(2)}, u32[]{:S(2)}) collective-permute-start(f32[3,80,128]{2,1,0:T(8,128)S(1)} %get-tuple-element.26), channel_id=1, source_target_pairs={{0,1},{1,0},{2,3},{3,2},{4,5},{5,4},{6,7},{7,6},{8,9},{9,8},{10,11... | collective-permute-start | bytes 368648 | tf_op jit(solution)/shard_map/ppermute | solution.py:594
